TPU v7x, 32 devices: a whole 2x2x4 slice. The times are simulated.
32 devices in a mesh: atom: 4 (over x, core), ka: 8 (over z, y).
Axes of the slice: x: 2, y: 2, z: 4, core: 2. Of those that a mesh axis runs over, the one named last changes fastest.
Arguments:
- positions: float32 [3, 65536], P(None, 'atom'), may hold values from 0 to 1
- features: bfloat16 [64, 65536], P(None, 'atom'), may hold values from -6 to 6
- species: int32 [65536], P('atom'), may hold values from 0 to 7
- miller: int32 [3, 4096], P(None, 'ka'), may hold values from -8 to 8
- species_table: float32 [64, 8], replicated, may hold values from -6 to 6
- filter_weight: float32 [64, 16], replicated, may hold values from -6 to 6
- norm_gain: float32 [64], replicated, may hold values from 0.25 to 1.75
- up_weight: bfloat16 [256, 64], replicated, may hold values from -0.75 to 0.75
- down_weight: bfloat16 [64, 256], replicated, may hold values from -0.375 to 0.375
Outputs:
- updated: bfloat16 [64, 65536], P(None, ('atom', 'ka'))
All inputs are finite; a program needn't handle non-finite values.
Results may differ from a plain program's by a relative error of at most 0.006.
Values may be sent and summed in bfloat16 or wider, within the bound.
No kernel may reach another device: no remote copies, remote signals or barrier semaphores. Data moves between devices by JAX's collectives and lax.ppermute only.
A program may use at most 64 MiB of HBM per device.

v0:
```python
import functools
import math

import jax
import jax.numpy as jnp
import numpy as np
from jax import lax
from jax.experimental import pallas as pl
from jax.experimental.pallas import tpu as pltpu
from jax.sharding import PartitionSpec as P

K = 4096
NRBF = 16
NSPEC = 8
MAXM = 8
GROUP = 8
ROWS = 304
LANES = 128
PAYLOAD = 400
k_cutoff = 14.0
f32 = jnp.float32
bf16 = jnp.bfloat16


def fit(function, terms, odd):
    nodes = np.cos((np.arange(64) + 0.5) * np.pi / 64) * 0.5
    nodes = np.abs(nodes)
    target = function(2.0 * np.pi * nodes)
    if odd:
        target = target / nodes
    series = np.polynomial.chebyshev.Chebyshev.fit(nodes * nodes, target, terms - 1, domain=[0, 0.25])
    return [float(v) for v in series.convert(kind=np.polynomial.Polynomial).coef]


SIN = fit(np.sin, 7, True)
COS = fit(np.cos, 7, False)


def horner(coefs, x):
    total = coefs[-1] * x + coefs[-2]
    for value in coefs[-3::-1]:
        total = total * x + value
    return total


def harmonics(x, multiples):
    turns = x * multiples
    turns = turns - jnp.floor(turns + 0.5)
    square = turns * turns
    return horner(COS, square), turns * horner(SIN, square)


def iota(shape, axis):
    return lax.broadcasted_iota(jnp.int32, shape, axis)


def factor_kernel(ka_split, sub, pos, feat, species, table, basis_out, z_out, acc_out, local_out, a_scr):
    step = pl.program_id(0)
    me = lax.axis_index("ka")
    group = me // ka_split
    width = pos.shape[1]
    first = pl.multiple_of((group // 2) * 16, 16)
    odd = (group % 2) == 1
    own_table = table[pl.ds(pl.multiple_of(group * GROUP, GROUP), GROUP), :]
    multiples = (iota((8, sub), 0) + 1).astype(f32)
    tail = (iota((16, sub), 0) == 0).astype(f32).astype(bf16)

    @pl.when(step == 0)
    def _():
        acc_out[...] = jnp.zeros_like(acc_out)

    @pl.when(step == me)
    def _():
        local_out[...] = feat[...]

    for start in range(0, width, sub):
        part = pl.ds(start, sub)
        c0, s0 = harmonics(pos[0:1, part], multiples)
        c1, s1 = harmonics(pos[1:2, part], multiples)
        c2, s2 = harmonics(pos[2:3, part], multiples)
        z_out[0:8, part] = c2
        z_out[8:16, part] = s2
        block = 0
        for left, right in ((c0, c1), (s0, s1), (s0, c1), (c0, s1)):
            for m in range(0, MAXM, 2):
                both = jnp.concatenate([left[m : m + 1] * right, left[m + 1 : m + 2] * right], 0)
                basis_out[block : block + 16, part] = both.astype(bf16)
                block += 16
        basis_out[256:272, part] = jnp.concatenate([c0, s0], 0).astype(bf16)
        basis_out[272:288, part] = jnp.concatenate([c1, s1], 0).astype(bf16)
        basis_out[288:304, part] = tail
        kinds = species[0:1, part]
        embedded = jnp.zeros((GROUP, sub), f32)
        for s in range(NSPEC):
            embedded = jnp.where(kinds == s, own_table[:, s : s + 1], embedded)
        wide = feat[pl.ds(first, 16), part].astype(f32)
        own = jnp.where(odd, wide[8:16], wide[0:8])
        source = (own + embedded).astype(bf16).astype(f32)
        for row, wave in ((0, c2), (64, s2)):
            for m in range(0, MAXM, 2):
                both = jnp.concatenate([source * wave[m : m + 1], source * wave[m + 1 : m + 2]], 0)
                a_scr[row + 8 * m : row + 8 * m + 16, part] = both.astype(bf16)
        a_scr[128:144, part] = jnp.concatenate([source, jnp.zeros_like(source)], 0).astype(bf16)
    acc_out[...] += lax.dot_general(
        basis_out[...], a_scr[...], (((1,), (1,)), ((), ())), preferred_element_type=f32
    )


def pack_kernel(acc, *refs):
    millers, out = refs[:-1], refs[-1]
    out[0:ROWS, :] = acc[:, 0:LANES].astype(bf16)
    tail = jnp.concatenate([acc[:, 128:144], jnp.zeros((ROWS, 112), f32)], 1)
    tail = jnp.concatenate([tail, jnp.zeros((384 - ROWS, LANES), f32)], 0)
    flat = tail.T
    zero = jnp.zeros((GROUP, LANES), f32)
    pieces = [flat[0:8, 0:128], flat[0:8, 128:256], flat[0:8, 256:384], zero]
    out[304:336, :] = jnp.concatenate(pieces, 0).astype(bf16)
    counts = jnp.zeros((32, 256), f32)
    for ref in millers:
        m0, m1, m2 = ref[0:1, :], ref[1:2, :], ref[2:3, :]
        sign = jnp.where(17 * m0 + m1 < 0, -1, 1)
        m0, m1, m2 = m0 * sign, m1 * sign, m2 * sign
        inner = jnp.where(
            m1 > 0, 8 * m0 + m1 - 9, jnp.where(m1 < 0, 55 + 8 * m0 - m1, 127 + m0)
        )
        row = jnp.where(m0 > 0, inner, jnp.where(m1 > 0, 135 + m1, 144))
        column = jnp.where(row == 144, jnp.abs(m2), m2) + MAXM
        size = row.shape[1]
        row_hot = (iota((256, size), 0) == row).astype(f32).astype(bf16)
        column_hot = (iota((32, size), 0) == column).astype(f32).astype(bf16)
        counts = counts + lax.dot_general(
            column_hot, row_hot, (((1,), (1,)), ((), ())), preferred_element_type=f32
        )
    out[336:368, :] = counts[:, 0:128].astype(bf16)
    out[368:400, :] = counts[:, 128:256].astype(bf16)


def radial_sum(square, weight_of):
    magnitude = jnp.sqrt(square)
    total = None
    for b in range(NRBF):
        offset = (magnitude - b * (k_cutoff / (NRBF - 1))) * (NRBF / k_cutoff)
        term = weight_of(b) * jnp.exp(-(offset * offset))
        total = term if total is None else total + term
    return total


def filter_rows(payload, weights, group, scaling, gt_scr):
    total = payload[0].astype(f32)
    for a in range(1, payload.shape[0]):
        total = total + payload[a].astype(f32)
    counts = jnp.concatenate([total[336:368], total[368:400]], 1)
    lane = iota((32, LANES), 1)
    index = iota((32, LANES), 0) - MAXM
    height = (lane % 64) // 8 + 1
    plus = jnp.where(jnp.abs(index) == height, 1.0, 0.0)
    minus = jnp.where(index == height, 1.0, jnp.where(index == -height, -1.0, 0.0))
    minus = jnp.where(lane < 64, -minus, minus)
    spread = jnp.concatenate([plus, minus], 1).astype(f32)
    wide = lax.dot_general(
        counts.T, spread, (((1,), (0,)), ((), ())),
        precision=lax.Precision.HIGHEST, preferred_element_type=f32,
    )
    pick = (iota((64, LANES), 0) == group * GROUP + iota((64, LANES), 1) % 8).astype(f32)
    across = lax.dot_general(
        weights[...].T, pick, (((1,), (0,)), ((), ())),
        precision=lax.Precision.HIGHEST, preferred_element_type=f32,
    )
    lane = iota((88, LANES), 1)
    row = iota((88, LANES), 0)
    third = (lane % 64) // 8 + 1
    first = row // 8 + 1
    second = row % 8 + 1
    planar = jnp.where(
        row < 64,
        first * first + second * second,
        jnp.where(row < 80, second * second, 0),
    )
    radial = radial_sum((planar + third * third).astype(f32), lambda b: across[b : b + 1, :]) * scaling
    radial = jnp.concatenate([radial[0:64], radial], 0)
    w_sum = wide[0:152, 0:128] * radial
    w_dif = wide[0:152, 128:256] * radial
    cc, ss, sc, cs = total[0:64], total[64:128], total[128:192], total[192:256]
    zero = jnp.zeros((8, LANES), f32)
    v_cos = jnp.concatenate([cc - ss, cc + ss, total[256:264], total[272:280], total[288:296]], 0)
    v_sin = jnp.concatenate([sc + cs, sc - cs, total[264:272], total[280:288], zero], 0)
    g_cos = w_sum * v_cos + w_dif * pltpu.roll(v_sin, 64, 1)
    g_sin = w_sum * v_sin - w_dif * pltpu.roll(v_cos, 64, 1)
    cp, cm, sp, sm = g_cos[0:64], g_cos[64:128], g_sin[0:64], g_sin[64:128]
    rows = [cp + cm, cm - cp, sp + sm, sp - sm, g_cos[128:136], g_sin[128:136]]
    rows += [g_cos[136:144], g_sin[136:144], g_cos[144:152], jnp.zeros((88, LANES), f32)]
    full = jnp.concatenate(rows, 0)
    gt_scr[0:128, :] = full.T.astype(bf16)

    lane = iota((8, LANES), 1)
    cell = lane % 64
    cell = (cell // 8 + 1) * (cell // 8 + 1) + (cell % 8 + 1) * (cell % 8 + 1)
    edge = jnp.where(lane < 32, (lane % 8 + 1) * (lane % 8 + 1), 0)
    own = weights[pl.ds(pl.multiple_of(group * GROUP, GROUP), GROUP), :]
    flat = radial_sum(
        jnp.concatenate([cell, edge], 1).astype(f32), lambda b: own[:, b : b + 1]
    ) * scaling
    count0 = jnp.broadcast_to(counts[8:9, 0:128], (8, LANES))
    count1 = jnp.broadcast_to(counts[8:9, 128:256], (8, LANES))
    side = jnp.where(
        lane < 8, count1,
        jnp.where(lane < 24, pltpu.roll(count1, 8, 1), jnp.where(lane < 33, pltpu.roll(count1, 16, 1), 0.0)),
    )
    sigma = jnp.where(lane < 64, 1.0, -1.0).astype(f32)
    even, uneven, rest = total[304:312], total[312:320], total[320:328]

    def mix(value):
        return pltpu.roll(value, 64, 1) + value * sigma

    even = mix(mix(even) * flat[:, 0:128] * pltpu.roll(count0, 64, 1))
    uneven = mix(mix(uneven) * flat[:, 0:128] * count0)
    rest = rest * flat[:, 128:256] * side
    low = jnp.concatenate([even, uneven, rest], 1)
    gt_scr[128:144, :] = jnp.concatenate([low, jnp.zeros_like(low)], 0).astype(bf16)


def back_kernel(ka_split, scaling, sub, payload, weights, basis, z, out, gt_scr):
    @pl.when(pl.program_id(0) == 0)
    def _():
        filter_rows(payload, weights, lax.axis_index("ka") // ka_split, scaling, gt_scr)

    table = gt_scr[:, 0:ROWS]
    for start in range(0, basis.shape[1], sub):
        part = pl.ds(start, sub)
        product = jnp.dot(table, basis[:, part], preferred_element_type=f32)
        message = product[128:136]
        for m in range(16):
            message = message + z[m : m + 1, part] * product[8 * m : 8 * m + 8]
        out[0, :, part] = message.astype(bf16)


def update_kernel(sub, message, feat, gain, up, down, out):
    width = feat.shape[1]
    eye = iota((64, 64), 0) == iota((64, 64), 1)
    column = jnp.sum(jnp.where(eye, jnp.broadcast_to(gain[...], (64, 64)), 0.0), axis=1, keepdims=True)
    for start in range(0, width, sub):
        part = pl.ds(start, sub)
        value = message[:, :, part].astype(f32).reshape(64, sub)
        mean_sq = jnp.mean(value * value, axis=0, keepdims=True)
        normed = (value * lax.rsqrt(mean_sq + 1e-06) * column).astype(bf16)
        pre = jnp.dot(up[...], normed, preferred_element_type=f32)
        hidden = (pre * (1.0 / (1.0 + jnp.exp(-pre)))).astype(bf16)
        update = jnp.dot(down[...], hidden, preferred_element_type=f32)
        out[:, part] = (feat[:, part].astype(f32) + update).astype(bf16)


def body(
    positions,
    features,
    species,
    miller,
    species_table,
    filter_weight,
    norm_gain,
    up_weight,
    down_weight,
):
    atoms_here = features.shape[1]
    channels = features.shape[0]
    n_atom = lax.axis_size("atom")
    n_ka = lax.axis_size("ka")
    ka_split = n_ka // (channels // GROUP)
    local_count = atoms_here // n_ka
    scaling = 1.0 / math.sqrt(atoms_here * n_atom * K)
    params = pltpu.CompilerParams(vmem_limit_bytes=48 * 1024 * 1024)

    blocks = n_ka // n_atom
    millers = []
    for j in range(blocks):
        pairs = []
        for a in range(n_atom):
            for b in range(n_ka):
                pairs.append((a * n_ka + (b ^ (blocks * a + j)), a * n_ka + b))
        millers.append(lax.ppermute(miller, ("atom", "ka"), pairs))

    whole = pl.BlockSpec(memory_space=pltpu.VMEM)
    basis, z, acc, local_features = pl.pallas_call(
        functools.partial(factor_kernel, ka_split, 512),
        grid=(n_ka,),
        in_specs=[
            pl.BlockSpec((3, local_count), lambda i: (0, i)),
            pl.BlockSpec((channels, local_count), lambda i: (0, i)),
            pl.BlockSpec((1, local_count), lambda i: (0, i)),
            whole,
        ],
        out_specs=[
            pl.BlockSpec((ROWS, local_count), lambda i: (0, i)),
            pl.BlockSpec((16, local_count), lambda i: (0, i)),
            pl.BlockSpec((ROWS, 144), lambda i: (0, 0)),
            pl.BlockSpec((channels, local_count), lambda i: (0, 0)),
        ],
        out_shape=[
            jax.ShapeDtypeStruct((ROWS, atoms_here), bf16),
            jax.ShapeDtypeStruct((16, atoms_here), f32),
            jax.ShapeDtypeStruct((ROWS, 144), f32),
            jax.ShapeDtypeStruct((channels, local_count), bf16),
        ],
        scratch_shapes=[pltpu.VMEM((144, local_count), bf16)],
        compiler_params=params,
        cost_estimate=pl.CostEstimate(flops=5 * 10**9, bytes_accessed=14 * 10**6, transcendentals=0),
        name="factors",
    )(positions, features, species.reshape(1, atoms_here), species_table)

    payload = pl.pallas_call(
        pack_kernel,
        in_specs=[whole] * (1 + blocks),
        out_specs=whole,
        out_shape=jax.ShapeDtypeStruct((PAYLOAD, LANES), bf16),
        compiler_params=params,
        name="pack",
    )(acc, *millers)
    gathered = lax.all_gather(payload, "atom")

    message = pl.pallas_call(
        functools.partial(back_kernel, ka_split, scaling, 512),
        grid=(n_ka,),
        in_specs=[
            whole,
            whole,
            pl.BlockSpec((ROWS, local_count), lambda i: (0, i)),
            pl.BlockSpec((16, local_count), lambda i: (0, i)),
        ],
        out_specs=pl.BlockSpec((1, GROUP, local_count), lambda i: (i, 0, 0)),
        out_shape=jax.ShapeDtypeStruct((n_ka, GROUP, local_count), bf16),
        scratch_shapes=[pltpu.VMEM((144, 384), bf16)],
        compiler_params=params,
        cost_estimate=pl.CostEstimate(flops=5 * 10**9, bytes_accessed=11 * 10**6, transcendentals=0),
        name="back",
    )(gathered, filter_weight, basis, z)

    groups = None
    if ka_split > 1:
        message = message.reshape(n_ka // ka_split, ka_split, GROUP, local_count)
        message = lax.dynamic_index_in_dim(message, lax.axis_index("ka") % ka_split, 1, False)
        groups = [[g * ka_split + s for g in range(n_ka // ka_split)] for s in range(ka_split)]
    message = lax.all_to_all(message, "ka", 0, 0, axis_index_groups=groups, tiled=True)

    return pl.pallas_call(
        functools.partial(update_kernel, 512),
        in_specs=[whole] * 5,
        out_specs=whole,
        out_shape=jax.ShapeDtypeStruct((channels, local_count), bf16),
        compiler_params=params,
        name="update",
    )(message, local_features, norm_gain.reshape(1, channels), up_weight, down_weight)


def solution(mesh):
    in_specs = (P(None, "atom"), P(None, "atom"), P("atom"), P(None, "ka"), P(), P(), P(), P(), P())
    out_specs = P(None, ("atom", "ka"))
    return jax.shard_map(body, mesh=mesh, in_specs=in_specs, out_specs=out_specs, check_vma=False)
```

profile of v0, /device:TPU:0, one launch (start us, length us, event | category | flops | bytes accessed | tf_op | source)
XLA Modules:
  0.0 52.4 jit_solution(9797182869018525199)
XLA Ops:
  0.0 1.5 %collective-permute-start = (s32[3,512]{1,0:T(4,128)}, s32[3,512]{1,0:T(4,128)S(1)}, u32[]{:S(2)}, u32[]{:S(2)}) collective-permute-start(s32[3,512]{1,0:T(4,128)} %param.12), channel_id=1, source_target_pairs={{0,0},{1,1},{2,2},{3,3},{4,4},{5,5},{6,6},{7,7},{10,8},{11,9},{8,1... | collective-permute-start | bytes 18440 | tf_op jit(solution)/shard_map/ppermute | solution.py:279
  1.5 3.0 %collective-permute-start.1 = (s32[3,512]{1,0:T(4,128)}, s32[3,512]{1,0:T(4,128)S(1)}, u32[]{:S(2)}, u32[]{:S(2)}) collective-permute-start(s32[3,512]{1,0:T(4,128)} %param.12), channel_id=1, source_target_pairs={{1,0},{0,1},{3,2},{2,3},{5,4},{4,5},{7,6},{6,7},{11,8},{10,9},{9,1... | collective-permute-start | bytes 18440 | tf_op jit(solution)/shard_map/ppermute | solution.py:279
  4.4 0.8 %copy.10.table = f32[64,8]{1,0:T(8,128)S(1)} copy(f32[64,8]{0,1:T(8,128)} %param.13) | data formatting | bytes 4096 | tf_op args[4]
  5.2 1.6 %copy-done.2 = bf16[64,16384]{1,0:T(8,128)(2,1)S(1)} copy-done((bf16[64,16384]{1,0:T(8,128)(2,1)S(1)}, bf16[64,16384]{1,0:T(8,128)(2,1)}, u32[]{:S(2)}) %copy-start.2) | copy-done | bytes 2097176
  6.8 0.9 %copy-done.3 = f32[3,16384]{1,0:T(4,128)S(1)} copy-done((f32[3,16384]{1,0:T(4,128)S(1)}, f32[3,16384]{1,0:T(4,128)}, u32[]{:S(2)}) %copy-start.3) | copy-done | bytes 196632
  7.8 0.8 %copy-done.4 = s32[16384]{0:T(1024)S(1)} copy-done((s32[16384]{0:T(1024)S(1)}, s32[16384]{0:T(1024)}, u32[]{:S(2)}) %copy-start.4) | copy-done | bytes 65560
  8.6 8.0 %factors.1 = (bf16[304,16384]{1,0:T(8,128)(2,1)}, f32[16,16384]{1,0:T(8,128)S(1)}, f32[304,144]{1,0:T(8,128)S(1)}, bf16[64,2048]{1,0:T(8,128)(2,1)S(1)}) custom-call(f32[3,16384]{1,0:T(4,128)S(1)} %copy-done.3, bf16[64,16384]{1,0:T(8,128)(2,1)S(1)} %copy-done.2, s32[1,16384]{1,0:T(1,128)S(1)} %bitcast.5, f32[64,8]{1,0:T(8,128)S(1)} %copy.10.table), custom_call_target="tpu_custom_call" | custom-call | flops 5000000000 | bytes 14000000 | tf_op jit(solution)/shard_map/factors/pallas_call | solution.py:282
  16.6 0.0 copy-done.6
  16.6 0.1 copy.11.weights
  16.7 0.0 collective-permute-done.refs_0_
  16.7 0.0 collective-permute-done.1.refs_1_
  16.7 0.0 copy-start.5
  16.7 0.0 copy-start
  16.8 0.0 copy-start.1
  16.8 0.3 pack.1
  17.1 9.5 %all-gather = bf16[1600,128]{1,0:T(8,128)(2,1)S(1)} all-gather(bf16[400,128]{1,0:T(8,128)(2,1)S(1)} %pack.1), channel_id=2, replica_groups=mesh['atom'=4,'ka'=8] {'atom'}, dimensions={0}, use_global_device_ids=true | all-gather | bytes 512000 | tf_op jit(solution)/shard_map/all_gather | solution.py:317
  26.6 9.4 %back.1 = bf16[8,8,2048]{2,1,0:T(8,128)(2,1)} custom-call(bf16[4,400,128]{2,1,0:T(8,128)(2,1)S(1)} %bitcast.3, f32[64,16]{1,0:T(8,128)S(1)} %copy.11.weights, bf16[304,16384]{1,0:T(8,128)(2,1)} %get-tuple-element.10.basis, f32[16,16384]{1,0:T(8,128)S(1)} %get-tuple-element.11.z), custom_call_target="tpu_custom_call" | custom-call | flops 5000000000 | bytes 11000000 | tf_op jit(solution)/shard_map/back/pallas_call | solution.py:319
  36.0 4.9 %all-to-all-start = ((bf16[8,8,2048]{2,1,0:T(8,128)(2,1)}), bf16[8,8,2048]{2,1,0:T(8,128)(2,1)S(1)}, u32[]{:S(2)}, u32[]{:S(2)}) async-start(bf16[8,8,2048]{2,1,0:T(8,128)(2,1)} %back.1), calls=%async_computation | async-start | bytes 524288 | tf_op jit(solution)/shard_map/all_to_all | solution.py:341
  40.9 0.0 copy-done.5
  40.9 0.1 copy.12.up
  41.0 9.3 %all-to-all-done.message = bf16[8,8,2048]{2,1,0:T(8,128)(2,1)S(1)} async-done(((bf16[8,8,2048]{2,1,0:T(8,128)(2,1)}), bf16[8,8,2048]{2,1,0:T(8,128)(2,1)S(1)}, u32[]{:S(2)}, u32[]{:S(2)}) %all-to-all-start) | async-done | bytes 262176 | tf_op jit(solution)/shard_map/all_to_all | solution.py:341
  50.3 0.0 copy-done
  50.3 0.0 copy-done.1
  50.3 2.1 %update.1 = bf16[64,2048]{1,0:T(8,128)(2,1)} custom-call(bf16[8,8,2048]{2,1,0:T(8,128)(2,1)S(1)} %all-to-all-done.message, bf16[64,2048]{1,0:T(8,128)(2,1)S(1)} %get-tuple-element.12.feat, f32[1,64]{1,0:T(1,128)S(1)} %bitcast.4, bf16[256,64]{1,0:T(8,128)(2,1)S(1)} %copy.12.up, bf16[64,256]{1,0:T(8,128)(2,1)S(1)} %copy-done), custom_call_target="tpu_custom_call" | custom-call | tf_op jit(solution)/shard_map/update/pallas_call | solution.py:343
  (4 shorter events, 0.0 us)
Async XLA Ops:
  0.0 16.6 %copy-start.6 = (f32[64,16]{0,1:T(8,128)S(1)}, f32[64,16]{0,1:T(8,128)}, u32[]{:S(2)}) copy-start(f32[64,16]{0,1:T(8,128)} %param.14) | copy-start | bytes 12292
  0.0 16.7 %collective-permute-start = (s32[3,512]{1,0:T(4,128)}, s32[3,512]{1,0:T(4,128)S(1)}, u32[]{:S(2)}, u32[]{:S(2)}) collective-permute-start(s32[3,512]{1,0:T(4,128)} %param.12), channel_id=1, source_target_pairs={{0,0},{1,1},{2,2},{3,3},{4,4},{5,5},{6,6},{7,7},{10,8},{11,9},{8,1... | collective-permute-start | bytes 18440 | tf_op jit(solution)/shard_map/ppermute | solution.py:279
  1.5 15.3 %collective-permute-start.1 = (s32[3,512]{1,0:T(4,128)}, s32[3,512]{1,0:T(4,128)S(1)}, u32[]{:S(2)}, u32[]{:S(2)}) collective-permute-start(s32[3,512]{1,0:T(4,128)} %param.12), channel_id=1, source_target_pairs={{1,0},{0,1},{3,2},{2,3},{5,4},{4,5},{7,6},{6,7},{11,8},{10,9},{9,1... | collective-permute-start | bytes 18440 | tf_op jit(solution)/shard_map/ppermute | solution.py:279
  5.2 1.6 %copy-start.2 = (bf16[64,16384]{1,0:T(8,128)(2,1)S(1)}, bf16[64,16384]{1,0:T(8,128)(2,1)}, u32[]{:S(2)}) copy-start(bf16[64,16384]{1,0:T(8,128)(2,1)} %feat.1) | copy-start | bytes 6291460
  6.8 0.9 %copy-start.3 = (f32[3,16384]{1,0:T(4,128)S(1)}, f32[3,16384]{1,0:T(4,128)}, u32[]{:S(2)}) copy-start(f32[3,16384]{1,0:T(4,128)} %pos.1) | copy-start | bytes 589828
  7.8 0.8 %copy-start.4 = (s32[16384]{0:T(1024)S(1)}, s32[16384]{0:T(1024)}, u32[]{:S(2)}) copy-start(s32[16384]{0:T(1024)} %param.11) | copy-start | bytes 196612
  16.7 24.2 %copy-start.5 = (bf16[256,64]{0,1:T(8,128)(2,1)S(1)}, bf16[256,64]{0,1:T(8,128)(2,1)}, u32[]{:S(2)}) copy-start(bf16[256,64]{0,1:T(8,128)(2,1)} %param.16) | copy-start | bytes 98308
  16.7 33.6 %copy-start = (bf16[64,256]{1,0:T(8,128)(2,1)S(1)}, bf16[64,256]{1,0:T(8,128)(2,1)}, u32[]{:S(2)}) copy-start(bf16[64,256]{1,0:T(8,128)(2,1)} %down.1) | copy-start | bytes 98308
  16.8 33.6 %copy-start.1 = (f32[64]{0:T(128)S(1)}, f32[64]{0:T(128)}, u32[]{:S(2)}) copy-start(f32[64]{0:T(128)} %param.15) | copy-start | bytes 772
  36.0 14.3 %all-to-all-start = ((bf16[8,8,2048]{2,1,0:T(8,128)(2,1)}), bf16[8,8,2048]{2,1,0:T(8,128)(2,1)S(1)}, u32[]{:S(2)}, u32[]{:S(2)}) async-start(bf16[8,8,2048]{2,1,0:T(8,128)(2,1)} %back.1), calls=%async_computation | async-start | bytes 524288 | tf_op jit(solution)/shard_map/all_to_all | solution.py:341
where the time goes:
time: 53.1 us; the launch traced here: 52.4 us
  Pallas kernels  19.8 us (37%)
  blocking collectives  9.54 us (18%)
  starting transfers between devices  9.34 us (18%)
  waiting for transfers between devices  9.32 us (18%)
  local copies, waits for them, and re-layouts  4.37 us (8%)
    all_gather x1, blocking collectives, body(): gathered = lax.all_gather(payload, 'atom')  9.54 us
    pallas_call x1, Pallas kernels, body(): pl.pallas_call(functools.partial(back_kernel, ka_split, scaling, 512), gr...  9.37 us
    all_to_all x1, waiting for transfers between devices, body(): lax.all_to_all(message, 'ka', 0, 0, axis_index_groups=groups, tiled=True)  9.31 us
    pallas_call x1, Pallas kernels, body(): pl.pallas_call(functools.partial(factor_kernel, ka_split, 512), grid=(n_k...  8.04 us
    all_to_all x1, starting transfers between devices, body(): lax.all_to_all(message, 'ka', 0, 0, axis_index_groups=groups, tiled=True)  4.9 us
    ppermute x2, starting transfers between devices, body(): millers.append(lax.ppermute(miller, ('atom', 'ka'), pairs))  4.44 us
    unnamed x17, local copies, waits for them, and re-layouts  4.37 us
    pallas_call x1, Pallas kernels, body(): pl.pallas_call(functools.partial(update_kernel, 512), in_specs=[whole] *...  2.08 us
  transfers between devices with their start and end apart: 3, of which 1 were waited for; matrix products, arithmetic and copies ran while one was open for 2% of the time, Pallas kernels for 15%

commit v1 on v0

v1 whole, which is shorter than its diff:
```python
import functools
import math

import jax
import jax.numpy as jnp
import numpy as np
from jax import lax
from jax.experimental import pallas as pl
from jax.experimental.pallas import tpu as pltpu
from jax.sharding import PartitionSpec as P

K = 4096
NRBF = 16
NSPEC = 8
MAXM = 8
GROUP = 8
ROWS = 304
CHUNK = 1024
WIDE = 2048
LANES = 128
PAYLOAD = 400
k_cutoff = 14.0
f32 = jnp.float32
bf16 = jnp.bfloat16


def fit(function, terms, odd):
    nodes = np.cos((np.arange(64) + 0.5) * np.pi / 64) * 0.5
    nodes = np.abs(nodes)
    target = function(2.0 * np.pi * nodes)
    if odd:
        target = target / nodes
    series = np.polynomial.chebyshev.Chebyshev.fit(nodes * nodes, target, terms - 1, domain=[0, 0.25])
    return [float(v) for v in series.convert(kind=np.polynomial.Polynomial).coef]


SIN = fit(np.sin, 7, True)
COS = fit(np.cos, 7, False)


def horner(coefs, x):
    total = coefs[-1] * x + coefs[-2]
    for value in coefs[-3::-1]:
        total = total * x + value
    return total


def first_harmonic(x):
    turns = x - jnp.floor(x + 0.5)
    square = turns * turns
    return horner(COS, square), turns * horner(SIN, square)


def iota(shape, axis):
    return lax.broadcasted_iota(jnp.int32, shape, axis)


def waves_to(scr, x):
    cosine, sine = first_harmonic(x)
    twice = cosine + cosine
    lower_c, lower_s = jnp.ones_like(cosine), jnp.zeros_like(sine)
    upper_c, upper_s = cosine, sine
    for m in range(MAXM):
        scr[8 * m : 8 * m + 8, :] = upper_c
        scr[64 + 8 * m : 72 + 8 * m, :] = upper_s
        lower_c, upper_c = upper_c, twice * upper_c - lower_c
        lower_s, upper_s = upper_s, twice * upper_s - lower_s


def spread(scr, row):
    return jnp.broadcast_to(scr[row : row + 1, :], (8, LANES))


def factor_chunk(pos, feat, species, table, odd, start, full, terms, z_out, w0, w1, w2):
    for axis, scr in enumerate((w0, w1, w2)):
        rows = [pos[axis : axis + 1, pl.ds(start + LANES * k, LANES)] for k in range(8)]
        waves_to(scr, jnp.concatenate(rows, 0))
    for k in range(8):
        part = pl.ds(start + LANES * k, LANES)
        c1 = w1[pl.ds(k, 8, stride=8), :]
        s1 = w1[pl.ds(64 + k, 8, stride=8), :]
        for m in range(16):
            left = spread(w0, 8 * m + k)
            full[16 * m : 16 * m + 16, part] = jnp.concatenate([left * c1, left * s1], 0).astype(bf16)
        c0 = w0[pl.ds(k, 8, stride=8), :]
        s0 = w0[pl.ds(64 + k, 8, stride=8), :]
        full[256:272, part] = jnp.concatenate([c0, s0], 0).astype(bf16)
        full[272:288, part] = jnp.concatenate([c1, s1], 0).astype(bf16)
        z_out[0:8, part] = w2[pl.ds(k, 8, stride=8), :]
        z_out[8:16, part] = w2[pl.ds(64 + k, 8, stride=8), :]
        kinds = jnp.broadcast_to(species[0:1, part], (8, LANES))
        embedded = table[0]
        for s in range(1, NSPEC):
            embedded = jnp.where(kinds == s, table[s], embedded)
        wide = feat[:, part].astype(f32)
        own = jnp.where(odd, wide[8:16], wide[0:8])
        source = (own + embedded).astype(bf16).astype(f32)
        for m in range(0, 16, 2):
            pair = [source * spread(w2, 8 * m + k), source * spread(w2, 8 * m + 8 + k)]
            terms[8 * m : 8 * m + 16, part] = jnp.concatenate(pair, 0).astype(bf16)
        terms[128:144, part] = jnp.concatenate([source, jnp.zeros_like(source)], 0).astype(bf16)


def choose(group, count):
    return (iota((count, 64), 1) == group * GROUP + iota((count, 64), 0) % GROUP).astype(f32)


def exact_dot(left, right, left_dim, right_dim):
    return lax.dot_general(
        left, right, (((left_dim,), (right_dim,)), ((), ())),
        precision=lax.Precision.HIGHEST, preferred_element_type=f32,
    )


def factor_kernel(ka_split, pos_hbm, feat_hbm, species_hbm, table, basis, z_out, acc, local_out,
                  pos, feat, species, full, terms, w0, w1, w2, sems, out_sems):
    me = lax.axis_index("ka")
    group = me // ka_split
    atoms, width = feat.shape[1], local_out.shape[1]
    first = pl.multiple_of((group // 2) * 16, 16)
    copies = [
        pltpu.make_async_copy(pos_hbm, pos, sems.at[0]),
        pltpu.make_async_copy(species_hbm, species, sems.at[1]),
        pltpu.make_async_copy(feat_hbm.at[pl.ds(first, 16), :], feat, sems.at[2]),
        pltpu.make_async_copy(
            feat_hbm.at[:, pl.ds(pl.multiple_of(me * width, width), width)], local_out, sems.at[3]
        ),
    ]
    for copy in copies:
        copy.start()
    full[288:304, :] = (iota((16, atoms), 0) == 0).astype(f32).astype(bf16)
    odd = (group % 2) == 1
    own = exact_dot(choose(group, GROUP), table[...], 1, 1)
    columns = [jnp.broadcast_to(own[:, s : s + 1], (8, LANES)) for s in range(NSPEC)]
    for copy in copies:
        copy.wait()

    def store(j):
        part = pl.ds(pl.multiple_of(j * CHUNK, CHUNK), CHUNK)
        return pltpu.make_async_copy(full.at[:, part], basis.at[:, part], out_sems.at[j])

    def step(j, carry):
        start = pl.multiple_of(j * CHUNK, CHUNK)
        factor_chunk(pos, feat, species, columns, odd, start, full, terms, z_out, w0, w1, w2)
        store(j).start()
        return carry

    steps = atoms // CHUNK
    lax.fori_loop(0, steps, step, 0)
    acc[...] = lax.dot_general(
        full[...], terms[...], (((1,), (1,)), ((), ())), preferred_element_type=f32
    )
    for j in range(steps):
        store(j).wait()


def pack_kernel(acc, *refs):
    millers, out = refs[:-1], refs[-1]
    out[0:ROWS, :] = acc[:, 0:LANES].astype(bf16)
    tail = jnp.concatenate([acc[:, 128:144], jnp.zeros((ROWS, 112), f32)], 1)
    tail = jnp.concatenate([tail, jnp.zeros((384 - ROWS, LANES), f32)], 0)
    flat = tail.T
    zero = jnp.zeros((GROUP, LANES), f32)
    pieces = [flat[0:8, 0:128], flat[0:8, 128:256], flat[0:8, 256:384], zero]
    out[304:336, :] = jnp.concatenate(pieces, 0).astype(bf16)
    counts = jnp.zeros((32, 256), f32)
    for ref in millers:
        m0, m1, m2 = ref[0:1, :], ref[1:2, :], ref[2:3, :]
        sign = jnp.where(17 * m0 + m1 < 0, -1, 1)
        m0, m1, m2 = m0 * sign, m1 * sign, m2 * sign
        inner = jnp.where(
            m1 > 0, 16 * m0 + m1 - 17, jnp.where(m1 < 0, 16 * m0 - m1 - 9, 127 + m0)
        )
        row = jnp.where(m0 > 0, inner, jnp.where(m1 > 0, 143 + m1, 160))
        column = jnp.where(row == 160, jnp.abs(m2), m2) + MAXM
        size = row.shape[1]
        row_hot = (iota((256, size), 0) == row).astype(f32).astype(bf16)
        column_hot = (iota((32, size), 0) == column).astype(f32).astype(bf16)
        counts = counts + lax.dot_general(
            column_hot, row_hot, (((1,), (1,)), ((), ())), preferred_element_type=f32
        )
    out[336:368, :] = counts[:, 0:128].astype(bf16)
    out[368:400, :] = counts[:, 128:256].astype(bf16)


def radial_sum(square, weight_of):
    magnitude = jnp.sqrt(square)
    total = None
    for b in range(NRBF):
        offset = (magnitude - b * (k_cutoff / (NRBF - 1))) * (NRBF / k_cutoff)
        term = weight_of(b) * jnp.exp(-(offset * offset))
        total = term if total is None else total + term
    return total


def filter_rows(payload, weights, group, scaling, gt_scr):
    total = payload[0].astype(f32)
    for a in range(1, payload.shape[0]):
        total = total + payload[a].astype(f32)
    counts = jnp.concatenate([total[336:368], total[368:400]], 1)
    lane = iota((32, LANES), 1)
    index = iota((32, LANES), 0) - MAXM
    height = (lane % 64) // 8 + 1
    plus = jnp.where(jnp.abs(index) == height, 1.0, 0.0)
    minus = jnp.where(index == height, 1.0, jnp.where(index == -height, -1.0, 0.0))
    minus = jnp.where(lane < 64, -minus, minus)
    spread = jnp.concatenate([plus, minus], 1).astype(f32)
    wide = exact_dot(counts.T, spread, 1, 0)
    across = exact_dot(weights[...], choose(group, LANES), 1, 1)
    lane = iota((88, LANES), 1)
    row = iota((88, LANES), 0)
    third = (lane % 64) // 8 + 1
    first = row // 8 + 1
    second = row % 8 + 1
    planar = jnp.where(
        row < 64,
        first * first + second * second,
        jnp.where(row < 80, second * second, 0),
    )
    radial = radial_sum((planar + third * third).astype(f32), lambda b: across[b : b + 1, :]) * scaling
    radial = jnp.concatenate([radial[0:64], radial], 0)

    def by_rows(value):
        both = value[0:128].reshape(8, 2, 8, LANES)
        edges = [value[128:136], value[144:152], value[160:168]]
        return jnp.concatenate([both[:, 0].reshape(64, LANES), both[:, 1].reshape(64, LANES)] + edges, 0)

    w_sum = by_rows(wide[:, 0:128]) * radial
    w_dif = by_rows(wide[:, 128:256]) * radial
    upper = total[0:128].reshape(8, 2, 8, LANES)
    lower = total[128:256].reshape(8, 2, 8, LANES)
    cc, cs = upper[:, 0].reshape(64, LANES), upper[:, 1].reshape(64, LANES)
    sc, ss = lower[:, 0].reshape(64, LANES), lower[:, 1].reshape(64, LANES)
    zero = jnp.zeros((8, LANES), f32)
    v_cos = jnp.concatenate([cc - ss, cc + ss, total[256:264], total[272:280], total[288:296]], 0)
    v_sin = jnp.concatenate([sc + cs, sc - cs, total[264:272], total[280:288], zero], 0)
    g_cos = w_sum * v_cos + w_dif * pltpu.roll(v_sin, 64, 1)
    g_sin = w_sum * v_sin - w_dif * pltpu.roll(v_cos, 64, 1)
    cp, cm, sp, sm = g_cos[0:64], g_cos[64:128], g_sin[0:64], g_sin[64:128]

    def pair_up(left, right):
        both = [left.reshape(8, 1, 8, LANES), right.reshape(8, 1, 8, LANES)]
        return jnp.concatenate(both, 1).reshape(128, LANES)

    rows = [pair_up(cp + cm, sp - sm), pair_up(sp + sm, cm - cp), g_cos[128:136], g_sin[128:136]]
    rows += [g_cos[136:144], g_sin[136:144], g_cos[144:152], jnp.zeros((88, LANES), f32)]
    full = jnp.concatenate(rows, 0)
    gt_scr[0:128, :] = full.T.astype(bf16)

    lane = iota((8, LANES), 1)
    cell = (lane // 16 + 1) * (lane // 16 + 1) + (lane % 8 + 1) * (lane % 8 + 1)
    edge = jnp.where(lane < 32, (lane % 8 + 1) * (lane % 8 + 1), 0)
    own = exact_dot(choose(group, GROUP), weights[...], 1, 1)
    flat = radial_sum(
        jnp.concatenate([cell, edge], 1).astype(f32), lambda b: own[:, b : b + 1]
    ) * scaling
    count0 = jnp.broadcast_to(counts[8:9, 0:128], (8, LANES))
    count1 = jnp.broadcast_to(counts[8:9, 128:256], (8, LANES))
    left = (lane // 8) % 2 == 0
    sigma = jnp.where(left, 1.0, -1.0).astype(f32)

    def swap(value):
        return jnp.where(left, pltpu.roll(value, LANES - 8, 1), pltpu.roll(value, 8, 1))

    other = swap(count0)
    x, y, rest = total[304:312], swap(total[312:320]), total[320:328]
    plus = (x - sigma * y) * flat[:, 0:128] * jnp.where(left, count0, other)
    less = (y + sigma * x) * flat[:, 0:128] * jnp.where(left, other, count0)
    rest = rest * flat[:, 128:256] * (count1 + pltpu.roll(count1, 8, 1))
    low = jnp.concatenate([plus + sigma * less, swap(less - sigma * plus), rest], 1)
    gt_scr[128:144, :] = jnp.concatenate([low, jnp.zeros_like(low)], 0).astype(bf16)


def back_kernel(ka_split, scaling, sub, payload, weights, basis_hbm, z, out, gt_scr, basis, sems):
    width = out.shape[2]
    steps = basis.shape[1] // WIDE
    fetches = []
    for j in range(steps):
        part = pl.ds(j * WIDE, WIDE)
        fetches.append(pltpu.make_async_copy(basis_hbm.at[:, part], basis.at[:, part], sems.at[j]))
    for fetch in fetches:
        fetch.start()
    filter_rows(payload, weights, lax.axis_index("ka") // ka_split, scaling, gt_scr)
    for j in range(steps):
        fetches[j].wait()
        product = jnp.dot(
            gt_scr[:, 0:ROWS], basis[:, j * WIDE : (j + 1) * WIDE], preferred_element_type=f32
        )
        for start in range(0, WIDE, sub):
            place = j * WIDE + start
            message = product[128:136, start : start + sub]
            for m in range(16):
                part = product[8 * m : 8 * m + 8, start : start + sub]
                message = message + z[m : m + 1, place : place + sub] * part
            offset = place % width
            out[place // width, :, offset : offset + sub] = message.astype(bf16)


def update_kernel(sub, message, feat, gain, up, down, out):
    width = feat.shape[1]
    eye = iota((64, 64), 0) == iota((64, 64), 1)
    column = jnp.sum(jnp.where(eye, jnp.broadcast_to(gain[...], (64, 64)), 0.0), axis=1, keepdims=True)
    for start in range(0, width, sub):
        part = pl.ds(start, sub)
        value = message[:, :, part].astype(f32).reshape(64, sub)
        mean_sq = jnp.mean(value * value, axis=0, keepdims=True)
        normed = (value * lax.rsqrt(mean_sq + 1e-06) * column).astype(bf16)
        pre = lax.dot_general(up[...], normed, (((0,), (0,)), ((), ())), preferred_element_type=f32)
        half = 0.5 * pre
        hidden = (half + half * jnp.tanh(half)).astype(bf16)
        update = jnp.dot(down[...], hidden, preferred_element_type=f32)
        out[:, part] = (feat[:, part].astype(f32) + update).astype(bf16)


def body(
    positions,
    features,
    species,
    miller,
    species_table,
    filter_weight,
    norm_gain,
    up_weight,
    down_weight,
):
    atoms_here = features.shape[1]
    channels = features.shape[0]
    n_atom = lax.axis_size("atom")
    n_ka = lax.axis_size("ka")
    ka_split = n_ka // (channels // GROUP)
    local_count = atoms_here // n_ka
    scaling = 1.0 / math.sqrt(atoms_here * n_atom * K)
    params = pltpu.CompilerParams(vmem_limit_bytes=24 * 1024 * 1024)

    blocks = n_ka // n_atom
    millers = []
    for j in range(blocks):
        pairs = []
        for a in range(n_atom):
            for b in range(n_ka):
                pairs.append((a * n_ka + (b ^ (blocks * a + j)), a * n_ka + b))
        millers.append(lax.ppermute(miller, ("atom", "ka"), pairs))

    whole = pl.BlockSpec(memory_space=pltpu.VMEM)
    hbm = pl.BlockSpec(memory_space=pltpu.HBM)
    basis, z, acc, local_features = pl.pallas_call(
        functools.partial(factor_kernel, ka_split),
        in_specs=[hbm, hbm, hbm, whole],
        out_specs=[hbm, whole, whole, whole],
        out_shape=[
            pltpu.HBM((ROWS, atoms_here), bf16),
            jax.ShapeDtypeStruct((16, atoms_here), f32),
            jax.ShapeDtypeStruct((ROWS, 144), f32),
            jax.ShapeDtypeStruct((channels, local_count), bf16),
        ],
        scratch_shapes=[
            pltpu.VMEM((3, atoms_here), f32),
            pltpu.VMEM((16, atoms_here), bf16),
            pltpu.VMEM((1, atoms_here), jnp.int32),
            pltpu.VMEM((ROWS, atoms_here), bf16),
            pltpu.VMEM((144, atoms_here), bf16),
            pltpu.VMEM((LANES, LANES), f32),
            pltpu.VMEM((LANES, LANES), f32),
            pltpu.VMEM((LANES, LANES), f32),
            pltpu.SemaphoreType.DMA((4,)),
            pltpu.SemaphoreType.DMA((atoms_here // CHUNK,)),
        ],
        compiler_params=params,
        cost_estimate=pl.CostEstimate(flops=5 * 10**9, bytes_accessed=14 * 10**6, transcendentals=0),
        name="factors",
    )(
        pltpu.with_memory_space_constraint(positions, pltpu.HBM),
        pltpu.with_memory_space_constraint(features, pltpu.HBM),
        pltpu.with_memory_space_constraint(species.reshape(1, atoms_here), pltpu.HBM),
        species_table.T,
    )

    payload = pl.pallas_call(
        pack_kernel,
        in_specs=[whole] * (1 + blocks),
        out_specs=whole,
        out_shape=jax.ShapeDtypeStruct((PAYLOAD, LANES), bf16),
        compiler_params=params,
        name="pack",
    )(acc, *millers)
    gathered = lax.all_gather(payload, "atom")

    message = pl.pallas_call(
        functools.partial(back_kernel, ka_split, scaling, min(512, local_count)),
        in_specs=[whole, whole, hbm, whole],
        out_specs=whole,
        out_shape=jax.ShapeDtypeStruct((n_ka, GROUP, local_count), bf16),
        scratch_shapes=[
            pltpu.VMEM((144, 384), bf16),
            pltpu.VMEM(basis.shape, bf16),
            pltpu.SemaphoreType.DMA((atoms_here // WIDE,)),
        ],
        compiler_params=params,
        cost_estimate=pl.CostEstimate(flops=5 * 10**9, bytes_accessed=11 * 10**6, transcendentals=0),
        name="back",
    )(gathered, filter_weight.T, pltpu.with_memory_space_constraint(basis, pltpu.HBM), z)

    groups = None
    if ka_split > 1:
        message = message.reshape(n_ka // ka_split, ka_split, GROUP, local_count)
        message = lax.dynamic_index_in_dim(message, lax.axis_index("ka") % ka_split, 1, False)
        groups = [[g * ka_split + s for g in range(n_ka // ka_split)] for s in range(ka_split)]
    message = lax.all_to_all(message, "ka", 0, 0, axis_index_groups=groups, tiled=True)

    return pl.pallas_call(
        functools.partial(update_kernel, 512),
        in_specs=[whole] * 5,
        out_specs=whole,
        out_shape=jax.ShapeDtypeStruct((channels, local_count), bf16),
        compiler_params=params,
        name="update",
    )(message, local_features, norm_gain.reshape(1, channels), up_weight.T, down_weight)


def solution(mesh):
    in_specs = (P(None, "atom"), P(None, "atom"), P("atom"), P(None, "ka"), P(), P(), P(), P(), P())
    out_specs = P(None, ("atom", "ka"))
    return jax.shard_map(body, mesh=mesh, in_specs=in_specs, out_specs=out_specs, check_vma=False)
```

time: 53.1 us -> 46 us (0.87)
  blocking collectives: 9.54 us -> 23.5 us
  waiting for transfers between devices: 9.32 us -> 0.01 us
  starting transfers between devices: 9.34 us -> 4.31 us
  local copies, waits for them, and re-layouts: 4.37 us -> 0.71 us
  Pallas kernels: 19.8 us -> 17.1 us
    all_to_all x0 -> x1, blocking collectives: none -> 14.1 us  [body(): lax.all_to_all(message, 'ka', 0, 0, axis_index_groups=groups, tiled=True)]
    all_to_all x1 -> x0, waiting for transfers between devices: 9.31 us -> none  [body(): lax.all_to_all(message, 'ka', 0, 0, axis_index_groups=groups, tiled=True)]
    all_to_all x1 -> x0, starting transfers between devices: 4.9 us -> none  [body(): lax.all_to_all(message, 'ka', 0, 0, axis_index_groups=groups, tiled=True)]
    unnamed x17 -> x10, local copies, waits for them, and re-layouts: 4.37 us -> 0.71 us
    pallas_call x2, Pallas kernels: 17.4 us -> 14.9 us  [the longest x1 8.68 us: body(): pl.pallas_call(functools.partial(factor_kernel, ka_split), in_specs=[hbm,...]
  transfers between devices with their start and end apart: 3 -> 2, of which waited for: 1 -> 0; matrix products, arithmetic and copies ran while one was open for 2% -> 0% of each run, Pallas kernels for 15% -> 19%
where the time goes in v1:
time: 46 us; the launch traced here: 45.7 us
  blocking collectives  23.5 us (51%)
  Pallas kernels  17.1 us (37%)
  starting transfers between devices  4.31 us (9%)
  local copies, waits for them, and re-layouts  0.71 us (2%)
    all_to_all x1, blocking collectives, body(): lax.all_to_all(message, 'ka', 0, 0, axis_index_groups=groups, tiled=True)  14.1 us
    all_gather x1, blocking collectives, body(): gathered = lax.all_gather(payload, 'atom')  9.47 us
    pallas_call x1, Pallas kernels, body(): pl.pallas_call(functools.partial(factor_kernel, ka_split), in_specs=[hbm,...  8.68 us
    pallas_call x1, Pallas kernels, body(): pl.pallas_call(functools.partial(back_kernel, ka_split, scaling, min(512,...  6.2 us
    ppermute x2, starting transfers between devices, body(): millers.append(lax.ppermute(miller, ('atom', 'ka'), pairs))  4.31 us
    pallas_call x1, Pallas kernels, body(): pl.pallas_call(functools.partial(update_kernel, 512), in_specs=[whole] *...  1.9 us
  transfers between devices with their start and end apart: 2, of which 0 were waited for; matrix products, arithmetic and copies ran while one was open for 0% of the time, Pallas kernels for 19%

profile of v1, /device:TPU:0, one launch (start us, length us, event | category | flops | bytes accessed | tf_op | source)
XLA Modules:
  0.0 45.7 jit_solution(12006856475898265626)
XLA Ops:
  0.0 0.0 copy-start.3
  0.0 3.0 %collective-permute-start.1 = (s32[3,512]{1,0:T(4,128)}, s32[3,512]{1,0:T(4,128)S(1)}, u32[]{:S(2)}, u32[]{:S(2)}) collective-permute-start(s32[3,512]{1,0:T(4,128)} %param.12), channel_id=1, source_target_pairs={{1,0},{0,1},{3,2},{2,3},{5,4},{4,5},{7,6},{6,7},{11,8},{10,9},{9,1... | collective-permute-start | bytes 18440 | tf_op jit(solution)/shard_map/ppermute | solution.py:342
  3.0 1.3 %collective-permute-start = (s32[3,512]{1,0:T(4,128)}, s32[3,512]{1,0:T(4,128)S(1)}, u32[]{:S(2)}, u32[]{:S(2)}) collective-permute-start(s32[3,512]{1,0:T(4,128)} %param.12), channel_id=1, source_target_pairs={{0,0},{1,1},{2,2},{3,3},{4,4},{5,5},{6,6},{7,7},{10,8},{11,9},{8,1... | collective-permute-start | bytes 18440 | tf_op jit(solution)/shard_map/ppermute | solution.py:342
  4.3 0.0 copy-start.4
  4.3 0.7 %copy-done.4 = f32[64,8]{0,1:T(8,128)S(1)} copy-done((f32[64,8]{0,1:T(8,128)S(1)}, f32[64,8]{0,1:T(8,128)}, u32[]{:S(2)}) %copy-start.4) | copy-done | bytes 2072
  5.0 8.7 %factors.1 = (bf16[304,16384]{1,0:T(8,128)(2,1)}, f32[16,16384]{1,0:T(8,128)S(1)}, f32[304,144]{1,0:T(8,128)S(1)}, bf16[64,2048]{1,0:T(8,128)(2,1)S(1)}) custom-call(f32[3,16384]{1,0:T(4,128)} %pos_hbm.1, bf16[64,16384]{1,0:T(8,128)(2,1)} %feat_hbm.1, s32[1,16384]{1,0:T(1,128)} %bitcast.11, f32[8,64]{1,0:T(8,128)S(1)} %bitcast.10), custom_call_target="tpu_custom_call" | custom-call | flops 5000000000 | bytes 14000000 | tf_op jit(solution)/shard_map/factors/pallas_call | solution.py:346
  13.7 0.0 collective-permute-done.1.refs_1_
  13.7 0.0 collective-permute-done.refs_0_
  13.7 0.0 copy-start
  13.7 0.0 copy-start.1
  13.7 0.0 copy-start.2
  13.7 0.3 pack.1
  14.1 9.5 %all-gather = bf16[1600,128]{1,0:T(8,128)(2,1)S(1)} all-gather(bf16[400,128]{1,0:T(8,128)(2,1)S(1)} %pack.1), channel_id=2, replica_groups=mesh['atom'=4,'ka'=8] {'atom'}, dimensions={0}, use_global_device_ids=true | all-gather | bytes 512000 | tf_op jit(solution)/shard_map/all_gather | solution.py:386
  23.5 0.0 copy-done.3
  23.5 6.2 %back.1 = bf16[8,8,2048]{2,1,0:T(8,128)(2,1)S(1)} custom-call(bf16[4,400,128]{2,1,0:T(8,128)(2,1)S(1)} %bitcast.6, f32[16,64]{1,0:T(8,128)S(1)} %bitcast.9, bf16[304,16384]{1,0:T(8,128)(2,1)} %get-tuple-element.10.basis_hbm, f32[16,16384]{1,0:T(8,128)S(1)} %get-tuple-element.11.z), custom_call_target="tpu_custom_call" | custom-call | flops 5000000000 | bytes 11000000 | tf_op jit(solution)/shard_map/back/pallas_call | solution.py:388
  29.7 14.1 %all_to_all.5.message = bf16[8,8,2048]{2,1,0:T(8,128)(2,1)S(1)} all-to-all(bf16[8,8,2048]{2,1,0:T(8,128)(2,1)S(1)} %back.1), channel_id=1, replica_groups=mesh['atom'=4,'ka'=8] {'ka'}, dimensions={0} | all-to-all | bytes 524288 | tf_op jit(solution)/shard_map/all_to_all | solution.py:408
  43.8 0.0 copy-done
  43.8 0.0 copy-done.1
  43.8 0.0 copy-done.2
  43.8 1.9 %update.1 = bf16[64,2048]{1,0:T(8,128)(2,1)} custom-call(bf16[8,8,2048]{2,1,0:T(8,128)(2,1)S(1)} %all_to_all.5.message, bf16[64,2048]{1,0:T(8,128)(2,1)S(1)} %get-tuple-element.12.feat, f32[1,64]{1,0:T(1,128)S(1)} %bitcast.8, bf16[64,256]{1,0:T(8,128)(2,1)S(1)} %bitcast.7, bf16[64,256]{1,0:T(8,128)(2,1)S(1)} %copy-done.1), custom_call_target="tpu_custom_call" | custom-call | tf_op jit(solution)/shard_map/update/pallas_call | solution.py:410
Async XLA Ops:
  0.0 23.5 %copy-start.3 = (f32[64,16]{0,1:T(8,128)S(1)}, f32[64,16]{0,1:T(8,128)}, u32[]{:S(2)}) copy-start(f32[64,16]{0,1:T(8,128)} %param.14) | copy-start | bytes 12292
  0.0 13.7 %collective-permute-start.1 = (s32[3,512]{1,0:T(4,128)}, s32[3,512]{1,0:T(4,128)S(1)}, u32[]{:S(2)}, u32[]{:S(2)}) collective-permute-start(s32[3,512]{1,0:T(4,128)} %param.12), channel_id=1, source_target_pairs={{1,0},{0,1},{3,2},{2,3},{5,4},{4,5},{7,6},{6,7},{11,8},{10,9},{9,1... | collective-permute-start | bytes 18440 | tf_op jit(solution)/shard_map/ppermute | solution.py:342
  3.0 10.7 %collective-permute-start = (s32[3,512]{1,0:T(4,128)}, s32[3,512]{1,0:T(4,128)S(1)}, u32[]{:S(2)}, u32[]{:S(2)}) collective-permute-start(s32[3,512]{1,0:T(4,128)} %param.12), channel_id=1, source_target_pairs={{0,0},{1,1},{2,2},{3,3},{4,4},{5,5},{6,6},{7,7},{10,8},{11,9},{8,1... | collective-permute-start | bytes 18440 | tf_op jit(solution)/shard_map/ppermute | solution.py:342
  4.3 0.7 %copy-start.4 = (f32[64,8]{0,1:T(8,128)S(1)}, f32[64,8]{0,1:T(8,128)}, u32[]{:S(2)}) copy-start(f32[64,8]{0,1:T(8,128)} %param.13) | copy-start | bytes 6148
  13.7 30.1 %copy-start = (bf16[256,64]{0,1:T(8,128)(2,1)S(1)}, bf16[256,64]{0,1:T(8,128)(2,1)}, u32[]{:S(2)}) copy-start(bf16[256,64]{0,1:T(8,128)(2,1)} %param.16) | copy-start | bytes 98308
  13.7 30.1 %copy-start.1 = (bf16[64,256]{1,0:T(8,128)(2,1)S(1)}, bf16[64,256]{1,0:T(8,128)(2,1)}, u32[]{:S(2)}) copy-start(bf16[64,256]{1,0:T(8,128)(2,1)} %down.1) | copy-start | bytes 98308
  13.7 30.1 %copy-start.2 = (f32[64]{0:T(128)S(1)}, f32[64]{0:T(128)}, u32[]{:S(2)}) copy-start(f32[64]{0:T(128)} %param.15) | copy-start | bytes 772

commit v2 on v1

--- a/solution.py
+++ b/solution.py
@@ -16,7 +16,8 @@
 GROUP = 8
 ROWS = 304
 CHUNK = 1024
-WIDE = 2048
+SPAN = 4
+PARTS = 4
 LANES = 128
 PAYLOAD = 400
 k_cutoff = 14.0
@@ -68,27 +69,31 @@
 
 
 def spread(scr, row):
-    return jnp.broadcast_to(scr[row : row + 1, :], (8, LANES))
-
-
-def factor_chunk(pos, feat, species, table, odd, start, full, terms, z_out, w0, w1, w2):
+    pieces = [jnp.broadcast_to(scr[row + k : row + k + 1, :], (8, LANES)) for k in range(SPAN)]
+    return jnp.concatenate(pieces, 1)
+
+
+def comb(scr, row):
+    return jnp.concatenate([scr[pl.ds(row + k, 8, stride=8), :] for k in range(SPAN)], 1)
+
+
+def factor_chunk(pos, feat, species, table, odd, start, here, full, terms, z_out, w0, w1, w2):
     for axis, scr in enumerate((w0, w1, w2)):
         rows = [pos[axis : axis + 1, pl.ds(start + LANES * k, LANES)] for k in range(8)]
         waves_to(scr, jnp.concatenate(rows, 0))
-    for k in range(8):
-        part = pl.ds(start + LANES * k, LANES)
-        c1 = w1[pl.ds(k, 8, stride=8), :]
-        s1 = w1[pl.ds(64 + k, 8, stride=8), :]
+    for k in range(0, 8, SPAN):
+        part = pl.ds(start + LANES * k, LANES * SPAN)
+        local = pl.ds(here + LANES * k, LANES * SPAN)
+        c1 = comb(w1, k)
+        s1 = comb(w1, 64 + k)
         for m in range(16):
             left = spread(w0, 8 * m + k)
-            full[16 * m : 16 * m + 16, part] = jnp.concatenate([left * c1, left * s1], 0).astype(bf16)
-        c0 = w0[pl.ds(k, 8, stride=8), :]
-        s0 = w0[pl.ds(64 + k, 8, stride=8), :]
-        full[256:272, part] = jnp.concatenate([c0, s0], 0).astype(bf16)
-        full[272:288, part] = jnp.concatenate([c1, s1], 0).astype(bf16)
-        z_out[0:8, part] = w2[pl.ds(k, 8, stride=8), :]
-        z_out[8:16, part] = w2[pl.ds(64 + k, 8, stride=8), :]
-        kinds = jnp.broadcast_to(species[0:1, part], (8, LANES))
+            full[16 * m : 16 * m + 16, local] = jnp.concatenate([left * c1, left * s1], 0).astype(bf16)
+        full[256:272, local] = jnp.concatenate([comb(w0, k), comb(w0, 64 + k)], 0).astype(bf16)
+        full[272:288, local] = jnp.concatenate([c1, s1], 0).astype(bf16)
+        z_out[0:8, part] = comb(w2, k)
+        z_out[8:16, part] = comb(w2, 64 + k)
+        kinds = jnp.broadcast_to(species[0:1, part], (8, LANES * SPAN))
         embedded = table[0]
         for s in range(1, NSPEC):
             embedded = jnp.where(kinds == s, table[s], embedded)
@@ -112,8 +117,9 @@
     )
 
 
-def factor_kernel(ka_split, pos_hbm, feat_hbm, species_hbm, table, basis, z_out, acc, local_out,
-                  pos, feat, species, full, terms, w0, w1, w2, sems, out_sems):
+def factor_kernel(ka_split, pos_hbm, feat_hbm, species_hbm, table, z_out, acc, local_out, *refs):
+    basis = refs[:PARTS]
+    pos, feat, species, terms, w0, w1, w2, sems = refs[PARTS:]
     me = lax.axis_index("ka")
     group = me // ka_split
     atoms, width = feat.shape[1], local_out.shape[1]
@@ -128,30 +134,33 @@
     ]
     for copy in copies:
         copy.start()
-    full[288:304, :] = (iota((16, atoms), 0) == 0).astype(f32).astype(bf16)
+    size = atoms // PARTS
+    for full in basis:
+        full[288:304, :] = (iota((16, size), 0) == 0).astype(f32).astype(bf16)
     odd = (group % 2) == 1
     own = exact_dot(choose(group, GROUP), table[...], 1, 1)
-    columns = [jnp.broadcast_to(own[:, s : s + 1], (8, LANES)) for s in range(NSPEC)]
+    columns = [jnp.broadcast_to(own[:, s : s + 1], (8, LANES * SPAN)) for s in range(NSPEC)]
     for copy in copies:
         copy.wait()
 
-    def store(j):
-        part = pl.ds(pl.multiple_of(j * CHUNK, CHUNK), CHUNK)
-        return pltpu.make_async_copy(full.at[:, part], basis.at[:, part], out_sems.at[j])
-
-    def step(j, carry):
-        start = pl.multiple_of(j * CHUNK, CHUNK)
-        factor_chunk(pos, feat, species, columns, odd, start, full, terms, z_out, w0, w1, w2)
-        store(j).start()
-        return carry
-
-    steps = atoms // CHUNK
-    lax.fori_loop(0, steps, step, 0)
-    acc[...] = lax.dot_general(
-        full[...], terms[...], (((1,), (1,)), ((), ())), preferred_element_type=f32
-    )
-    for j in range(steps):
-        store(j).wait()
+    total = None
+    for p, full in enumerate(basis):
+
+        def step(j, carry):
+            here = pl.multiple_of(j * CHUNK, CHUNK)
+            factor_chunk(
+                pos, feat, species, columns, odd, p * size + here, here, full, terms, z_out, w0, w1, w2
+            )
+            return carry
+
+        lax.fori_loop(0, size // CHUNK, step, 0)
+    for p, full in enumerate(basis):
+        piece = lax.dot_general(
+            full[...], terms[:, p * size : (p + 1) * size],
+            (((1,), (1,)), ((), ())), preferred_element_type=f32,
+        )
+        total = piece if total is None else total + piece
+    acc[...] = total
 
 
 def pack_kernel(acc, *refs):
@@ -271,23 +280,15 @@
     gt_scr[128:144, :] = jnp.concatenate([low, jnp.zeros_like(low)], 0).astype(bf16)
 
 
-def back_kernel(ka_split, scaling, sub, payload, weights, basis_hbm, z, out, gt_scr, basis, sems):
+def back_kernel(ka_split, scaling, sub, payload, weights, z, *refs):
+    basis, out, gt_scr = refs[:PARTS], refs[PARTS], refs[PARTS + 1]
     width = out.shape[2]
-    steps = basis.shape[1] // WIDE
-    fetches = []
-    for j in range(steps):
-        part = pl.ds(j * WIDE, WIDE)
-        fetches.append(pltpu.make_async_copy(basis_hbm.at[:, part], basis.at[:, part], sems.at[j]))
-    for fetch in fetches:
-        fetch.start()
     filter_rows(payload, weights, lax.axis_index("ka") // ka_split, scaling, gt_scr)
-    for j in range(steps):
-        fetches[j].wait()
-        product = jnp.dot(
-            gt_scr[:, 0:ROWS], basis[:, j * WIDE : (j + 1) * WIDE], preferred_element_type=f32
-        )
-        for start in range(0, WIDE, sub):
-            place = j * WIDE + start
+    for j, piece in enumerate(basis):
+        size = piece.shape[1]
+        product = jnp.dot(gt_scr[:, 0:ROWS], piece[...], preferred_element_type=f32)
+        for start in range(0, size, sub):
+            place = j * size + start
             message = product[128:136, start : start + sub]
             for m in range(16):
                 part = product[8 * m : 8 * m + 8, start : start + sub]
@@ -343,27 +344,26 @@
 
     whole = pl.BlockSpec(memory_space=pltpu.VMEM)
     hbm = pl.BlockSpec(memory_space=pltpu.HBM)
-    basis, z, acc, local_features = pl.pallas_call(
+    hbm = pl.BlockSpec(memory_space=pltpu.HBM)
+    z, acc, local_features, *basis = pl.pallas_call(
         functools.partial(factor_kernel, ka_split),
         in_specs=[hbm, hbm, hbm, whole],
-        out_specs=[hbm, whole, whole, whole],
+        out_specs=[whole] * (3 + PARTS),
         out_shape=[
-            pltpu.HBM((ROWS, atoms_here), bf16),
             jax.ShapeDtypeStruct((16, atoms_here), f32),
             jax.ShapeDtypeStruct((ROWS, 144), f32),
             jax.ShapeDtypeStruct((channels, local_count), bf16),
-        ],
+        ]
+        + [jax.ShapeDtypeStruct((ROWS, atoms_here // PARTS), bf16)] * PARTS,
         scratch_shapes=[
             pltpu.VMEM((3, atoms_here), f32),
             pltpu.VMEM((16, atoms_here), bf16),
             pltpu.VMEM((1, atoms_here), jnp.int32),
-            pltpu.VMEM((ROWS, atoms_here), bf16),
             pltpu.VMEM((144, atoms_here), bf16),
             pltpu.VMEM((LANES, LANES), f32),
             pltpu.VMEM((LANES, LANES), f32),
             pltpu.VMEM((LANES, LANES), f32),
             pltpu.SemaphoreType.DMA((4,)),
-            pltpu.SemaphoreType.DMA((atoms_here // CHUNK,)),
         ],
         compiler_params=params,
         cost_estimate=pl.CostEstimate(flops=5 * 10**9, bytes_accessed=14 * 10**6, transcendentals=0),
@@ -387,18 +387,14 @@
 
     message = pl.pallas_call(
         functools.partial(back_kernel, ka_split, scaling, min(512, local_count)),
-        in_specs=[whole, whole, hbm, whole],
+        in_specs=[whole] * (3 + PARTS),
         out_specs=whole,
         out_shape=jax.ShapeDtypeStruct((n_ka, GROUP, local_count), bf16),
-        scratch_shapes=[
-            pltpu.VMEM((144, 384), bf16),
-            pltpu.VMEM(basis.shape, bf16),
-            pltpu.SemaphoreType.DMA((atoms_here // WIDE,)),
-        ],
+        scratch_shapes=[pltpu.VMEM((144, 384), bf16)],
         compiler_params=params,
         cost_estimate=pl.CostEstimate(flops=5 * 10**9, bytes_accessed=11 * 10**6, transcendentals=0),
         name="back",
-    )(gathered, filter_weight.T, pltpu.with_memory_space_constraint(basis, pltpu.HBM), z)
+    )(gathered, filter_weight.T, z, *basis)
 
     groups = None
     if ka_split > 1:

time: 46 us -> 41.7 us (0.907)
  Pallas kernels: 17.1 us -> 12.7 us
    pallas_call x1, Pallas kernels: 6.2 us -> 3.78 us  [body(): pl.pallas_call(functools.partial(back_kernel, ka_split, scaling, min(512,...]
    pallas_call x1, Pallas kernels: 8.68 us -> 6.75 us  [body(): pl.pallas_call(functools.partial(factor_kernel, ka_split), in_specs=[hbm,...]
  transfers between devices with their start and end apart: 2 -> 2, of which waited for: 0 -> 0; matrix products, arithmetic and copies ran while one was open for 0% -> 0% of each run, Pallas kernels for 19% -> 16%
where the time goes in v2:
time: 41.7 us; the launch traced here: 41.4 us
  blocking collectives  23.6 us (57%)
  Pallas kernels  12.7 us (30%)
  starting transfers between devices  4.31 us (10%)
  local copies, waits for them, and re-layouts  0.7 us (2%)
    all_to_all x1, blocking collectives, body(): lax.all_to_all(message, 'ka', 0, 0, axis_index_groups=groups, tiled=True)  14.1 us
    all_gather x1, blocking collectives, body(): gathered = lax.all_gather(payload, 'atom')  9.47 us
    pallas_call x1, Pallas kernels, body(): pl.pallas_call(functools.partial(factor_kernel, ka_split), in_specs=[hbm,...  6.75 us
    ppermute x2, starting transfers between devices, body(): millers.append(lax.ppermute(miller, ('atom', 'ka'), pairs))  4.31 us
    pallas_call x1, Pallas kernels, body(): pl.pallas_call(functools.partial(back_kernel, ka_split, scaling, min(512,...  3.78 us
    pallas_call x1, Pallas kernels, body(): pl.pallas_call(functools.partial(update_kernel, 512), in_specs=[whole] *...  1.9 us
  transfers between devices with their start and end apart: 2, of which 0 were waited for; matrix products, arithmetic and copies ran while one was open for 0% of the time, Pallas kernels for 16%

profile of v2, /device:TPU:0, one launch (start us, length us, event | category | flops | bytes accessed | tf_op | source)
XLA Modules:
  0.0 41.4 jit_solution(8803681132096751861)
XLA Ops:
  0.0 3.0 %collective-permute-start.1 = (s32[3,512]{1,0:T(4,128)}, s32[3,512]{1,0:T(4,128)S(1)}, u32[]{:S(2)}, u32[]{:S(2)}) collective-permute-start(s32[3,512]{1,0:T(4,128)} %param.12), channel_id=1, source_target_pairs={{1,0},{0,1},{3,2},{2,3},{5,4},{4,5},{7,6},{6,7},{11,8},{10,9},{9,1... | collective-permute-start | bytes 18440 | tf_op jit(solution)/shard_map/ppermute | solution.py:343
  3.0 1.3 %collective-permute-start = (s32[3,512]{1,0:T(4,128)}, s32[3,512]{1,0:T(4,128)S(1)}, u32[]{:S(2)}, u32[]{:S(2)}) collective-permute-start(s32[3,512]{1,0:T(4,128)} %param.12), channel_id=1, source_target_pairs={{0,0},{1,1},{2,2},{3,3},{4,4},{5,5},{6,6},{7,7},{10,8},{11,9},{8,1... | collective-permute-start | bytes 18440 | tf_op jit(solution)/shard_map/ppermute | solution.py:343
  4.3 0.0 copy-start.4
  4.3 0.7 %copy-done.4 = f32[64,8]{0,1:T(8,128)S(1)} copy-done((f32[64,8]{0,1:T(8,128)S(1)}, f32[64,8]{0,1:T(8,128)}, u32[]{:S(2)}) %copy-start.4) | copy-done | bytes 2072
  5.0 0.0 copy-start.3
  5.0 6.7 %factors.1 = (f32[16,16384]{1,0:T(8,128)S(1)}, f32[304,144]{1,0:T(8,128)S(1)}, bf16[64,2048]{1,0:T(8,128)(2,1)S(1)}, bf16[304,4096]{1,0:T(8,128)(2,1)S(1)}, bf16...) custom-call(f32[3,16384]{1,0:T(4,128)} %pos_hbm.1, ...), custom_call_target="tpu_custom_call" | custom-call | flops 5000000000 | bytes 14000000 | tf_op jit(solution)/shard_map/factors/pallas_call | solution.py:348
  11.8 0.0 collective-permute-done.1.refs_1_
  11.8 0.0 collective-permute-done.refs_0_
  11.8 0.3 pack.1
  12.1 9.5 %all-gather = bf16[1600,128]{1,0:T(8,128)(2,1)S(1)} all-gather(bf16[400,128]{1,0:T(8,128)(2,1)S(1)} %pack.1), channel_id=2, replica_groups=mesh['atom'=4,'ka'=8] {'atom'}, dimensions={0}, use_global_device_ids=true | all-gather | bytes 512000 | tf_op jit(solution)/shard_map/all_gather | solution.py:386
  21.6 0.0 copy-done.3
  21.6 0.0 copy-start
  21.6 0.0 copy-start.1
  21.6 0.0 copy-start.2
  21.6 3.8 %back.1 = bf16[8,8,2048]{2,1,0:T(8,128)(2,1)S(1)} custom-call(bf16[4,400,128]{2,1,0:T(8,128)(2,1)S(1)} %bitcast.6, f32[16,64]{1,0:T(8,128)S(1)} %bitcast.9, f32[16,16384]{1,0:T(8,128)S(1)} %get-tuple-element.13.z, bf16[304,4096]{1,0:T(8,128)(2,1)S(1)} %get-tuple-element.14.refs_0_, bf16[304,4096]{1,0:T(8,128)(2,1)S(1)} %get-tuple-element.15.refs_1_, ...), custom_call_target="tpu_custom_call" | custom-call | flops 5000000000 | bytes 11000000 | tf_op jit(solution)/shard_map/back/pallas_call | solution.py:388
  25.4 14.1 %all_to_all.5.message = bf16[8,8,2048]{2,1,0:T(8,128)(2,1)S(1)} all-to-all(bf16[8,8,2048]{2,1,0:T(8,128)(2,1)S(1)} %back.1), channel_id=1, replica_groups=mesh['atom'=4,'ka'=8] {'ka'}, dimensions={0} | all-to-all | bytes 524288 | tf_op jit(solution)/shard_map/all_to_all | solution.py:404
  39.5 0.0 copy-done
  39.5 0.0 copy-done.1
  39.5 0.0 copy-done.2
  39.5 1.9 %update.1 = bf16[64,2048]{1,0:T(8,128)(2,1)} custom-call(bf16[8,8,2048]{2,1,0:T(8,128)(2,1)S(1)} %all_to_all.5.message, bf16[64,2048]{1,0:T(8,128)(2,1)S(1)} %get-tuple-element.18.feat, f32[1,64]{1,0:T(1,128)S(1)} %bitcast.8, bf16[64,256]{1,0:T(8,128)(2,1)S(1)} %bitcast.7, bf16[64,256]{1,0:T(8,128)(2,1)S(1)} %copy-done.1), custom_call_target="tpu_custom_call" | custom-call | tf_op jit(solution)/shard_map/update/pallas_call | solution.py:406
Async XLA Ops:
  0.0 11.8 %collective-permute-start.1 = (s32[3,512]{1,0:T(4,128)}, s32[3,512]{1,0:T(4,128)S(1)}, u32[]{:S(2)}, u32[]{:S(2)}) collective-permute-start(s32[3,512]{1,0:T(4,128)} %param.12), channel_id=1, source_target_pairs={{1,0},{0,1},{3,2},{2,3},{5,4},{4,5},{7,6},{6,7},{11,8},{10,9},{9,1... | collective-permute-start | bytes 18440 | tf_op jit(solution)/shard_map/ppermute | solution.py:343
  3.0 8.8 %collective-permute-start = (s32[3,512]{1,0:T(4,128)}, s32[3,512]{1,0:T(4,128)S(1)}, u32[]{:S(2)}, u32[]{:S(2)}) collective-permute-start(s32[3,512]{1,0:T(4,128)} %param.12), channel_id=1, source_target_pairs={{0,0},{1,1},{2,2},{3,3},{4,4},{5,5},{6,6},{7,7},{10,8},{11,9},{8,1... | collective-permute-start | bytes 18440 | tf_op jit(solution)/shard_map/ppermute | solution.py:343
  4.3 0.7 %copy-start.4 = (f32[64,8]{0,1:T(8,128)S(1)}, f32[64,8]{0,1:T(8,128)}, u32[]{:S(2)}) copy-start(f32[64,8]{0,1:T(8,128)} %param.13) | copy-start | bytes 6148
  5.0 16.6 %copy-start.3 = (f32[64,16]{0,1:T(8,128)S(1)}, f32[64,16]{0,1:T(8,128)}, u32[]{:S(2)}) copy-start(f32[64,16]{0,1:T(8,128)} %param.14) | copy-start | bytes 12292
  21.6 17.9 %copy-start = (bf16[256,64]{0,1:T(8,128)(2,1)S(1)}, bf16[256,64]{0,1:T(8,128)(2,1)}, u32[]{:S(2)}) copy-start(bf16[256,64]{0,1:T(8,128)(2,1)} %param.16) | copy-start | bytes 98308
  21.6 17.9 %copy-start.1 = (bf16[64,256]{1,0:T(8,128)(2,1)S(1)}, bf16[64,256]{1,0:T(8,128)(2,1)}, u32[]{:S(2)}) copy-start(bf16[64,256]{1,0:T(8,128)(2,1)} %down.1) | copy-start | bytes 98308
  21.6 17.9 %copy-start.2 = (f32[64]{0:T(128)S(1)}, f32[64]{0:T(128)}, u32[]{:S(2)}) copy-start(f32[64]{0:T(128)} %param.15) | copy-start | bytes 772

commit v3 on v2

--- a/solution.py
+++ b/solution.py
@@ -77,33 +77,35 @@
     return jnp.concatenate([scr[pl.ds(row + k, 8, stride=8), :] for k in range(SPAN)], 1)
 
 
-def factor_chunk(pos, feat, species, table, odd, start, here, full, terms, z_out, w0, w1, w2):
+def harmonics_chunk(pos, start, w0, w1, w2):
     for axis, scr in enumerate((w0, w1, w2)):
         rows = [pos[axis : axis + 1, pl.ds(start + LANES * k, LANES)] for k in range(8)]
         waves_to(scr, jnp.concatenate(rows, 0))
-    for k in range(0, 8, SPAN):
-        part = pl.ds(start + LANES * k, LANES * SPAN)
-        local = pl.ds(here + LANES * k, LANES * SPAN)
-        c1 = comb(w1, k)
-        s1 = comb(w1, 64 + k)
-        for m in range(16):
-            left = spread(w0, 8 * m + k)
-            full[16 * m : 16 * m + 16, local] = jnp.concatenate([left * c1, left * s1], 0).astype(bf16)
-        full[256:272, local] = jnp.concatenate([comb(w0, k), comb(w0, 64 + k)], 0).astype(bf16)
-        full[272:288, local] = jnp.concatenate([c1, s1], 0).astype(bf16)
-        z_out[0:8, part] = comb(w2, k)
-        z_out[8:16, part] = comb(w2, 64 + k)
-        kinds = jnp.broadcast_to(species[0:1, part], (8, LANES * SPAN))
-        embedded = table[0]
-        for s in range(1, NSPEC):
-            embedded = jnp.where(kinds == s, table[s], embedded)
-        wide = feat[:, part].astype(f32)
-        own = jnp.where(odd, wide[8:16], wide[0:8])
-        source = (own + embedded).astype(bf16).astype(f32)
-        for m in range(0, 16, 2):
-            pair = [source * spread(w2, 8 * m + k), source * spread(w2, 8 * m + 8 + k)]
-            terms[8 * m : 8 * m + 16, part] = jnp.concatenate(pair, 0).astype(bf16)
-        terms[128:144, part] = jnp.concatenate([source, jnp.zeros_like(source)], 0).astype(bf16)
+
+
+def factor_chunk(feat, species, table, odd, start, here, k, full, terms, z_out, w0, w1, w2):
+    part = pl.ds(start, LANES * SPAN)
+    local = pl.ds(here, LANES * SPAN)
+    c1 = comb(w1, k)
+    s1 = comb(w1, 64 + k)
+    for m in range(16):
+        left = spread(w0, 8 * m + k)
+        full[16 * m : 16 * m + 16, local] = jnp.concatenate([left * c1, left * s1], 0).astype(bf16)
+    full[256:272, local] = jnp.concatenate([comb(w0, k), comb(w0, 64 + k)], 0).astype(bf16)
+    full[272:288, local] = jnp.concatenate([c1, s1], 0).astype(bf16)
+    z_out[0:8, part] = comb(w2, k)
+    z_out[8:16, part] = comb(w2, 64 + k)
+    kinds = jnp.broadcast_to(species[0:1, part], (8, LANES * SPAN))
+    embedded = table[0]
+    for s in range(1, NSPEC):
+        embedded = jnp.where(kinds == s, table[s], embedded)
+    wide = feat[:, part].astype(f32)
+    own = jnp.where(odd, wide[8:16], wide[0:8])
+    source = (own + embedded).astype(bf16).astype(f32)
+    for m in range(0, 16, 2):
+        pair = [source * spread(w2, 8 * m + k), source * spread(w2, 8 * m + 8 + k)]
+        terms[8 * m : 8 * m + 16, part] = jnp.concatenate(pair, 0).astype(bf16)
+    terms[128:144, part] = jnp.concatenate([source, jnp.zeros_like(source)], 0).astype(bf16)
 
 
 def choose(group, count):
@@ -117,43 +119,54 @@
     )
 
 
-def factor_kernel(ka_split, pos_hbm, feat_hbm, species_hbm, table, z_out, acc, local_out, *refs):
+def factor_kernel(ka_split, pos_hbm, feat_hbm, species_hbm, table_hbm, z_out, acc, local_out, *refs):
     basis = refs[:PARTS]
-    pos, feat, species, terms, w0, w1, w2, sems = refs[PARTS:]
+    pos, feat, species, table, terms, w0, w1, w2, sems = refs[PARTS:]
     me = lax.axis_index("ka")
     group = me // ka_split
     atoms, width = feat.shape[1], local_out.shape[1]
     first = pl.multiple_of((group // 2) * 16, 16)
-    copies = [
-        pltpu.make_async_copy(pos_hbm, pos, sems.at[0]),
-        pltpu.make_async_copy(species_hbm, species, sems.at[1]),
-        pltpu.make_async_copy(feat_hbm.at[pl.ds(first, 16), :], feat, sems.at[2]),
-        pltpu.make_async_copy(
-            feat_hbm.at[:, pl.ds(pl.multiple_of(me * width, width), width)], local_out, sems.at[3]
-        ),
-    ]
-    for copy in copies:
+    size = atoms // PARTS
+    copies = [pltpu.make_async_copy(table_hbm, table, sems.at[0])]
+    waits = []
+    for p in range(PARTS):
+        cut = pl.ds(p * size, size)
+        waits.append(
+            [
+                pltpu.make_async_copy(pos_hbm.at[:, cut], pos.at[:, cut], sems.at[3 * p + 2]),
+                pltpu.make_async_copy(species_hbm.at[:, cut], species.at[:, cut], sems.at[3 * p + 3]),
+                pltpu.make_async_copy(
+                    feat_hbm.at[pl.ds(first, 16), cut], feat.at[:, cut], sems.at[3 * p + 4]
+                ),
+            ]
+        )
+        copies += waits[p]
+    keep = pltpu.make_async_copy(
+        feat_hbm.at[:, pl.ds(pl.multiple_of(me * width, width), width)], local_out, sems.at[1]
+    )
+    for copy in copies + [keep]:
         copy.start()
-    size = atoms // PARTS
     for full in basis:
         full[288:304, :] = (iota((16, size), 0) == 0).astype(f32).astype(bf16)
     odd = (group % 2) == 1
+    copies[0].wait()
     own = exact_dot(choose(group, GROUP), table[...], 1, 1)
     columns = [jnp.broadcast_to(own[:, s : s + 1], (8, LANES * SPAN)) for s in range(NSPEC)]
-    for copy in copies:
-        copy.wait()
-
+
+    def step(p, j):
+        here = pl.multiple_of(j * CHUNK, CHUNK)
+        harmonics_chunk(pos, p * size + here, w0, w1, w2)
+        for k in range(0, 8, SPAN):
+            factor_chunk(
+                feat, species, columns, odd, p * size + here + k * LANES, here + k * LANES, k,
+                basis[p], terms, z_out, w0, w1, w2,
+            )
+
+    for p in range(PARTS):
+        for copy in waits[p]:
+            copy.wait()
+        lax.fori_loop(0, size // CHUNK, lambda j, carry: step(p, j), None, unroll=4)
     total = None
-    for p, full in enumerate(basis):
-
-        def step(j, carry):
-            here = pl.multiple_of(j * CHUNK, CHUNK)
-            factor_chunk(
-                pos, feat, species, columns, odd, p * size + here, here, full, terms, z_out, w0, w1, w2
-            )
-            return carry
-
-        lax.fori_loop(0, size // CHUNK, step, 0)
     for p, full in enumerate(basis):
         piece = lax.dot_general(
             full[...], terms[:, p * size : (p + 1) * size],
@@ -161,6 +174,7 @@
         )
         total = piece if total is None else total + piece
     acc[...] = total
+    keep.wait()
 
 
 def pack_kernel(acc, *refs):
@@ -192,6 +206,10 @@
     out[368:400, :] = counts[:, 128:256].astype(bf16)
 
 
+def fold_kernel(left, right, out):
+    out[...] = (left[...].astype(f32) + right[...].astype(f32)).astype(bf16)
+
+
 def radial_sum(square, weight_of):
     magnitude = jnp.sqrt(square)
     total = None
@@ -203,9 +221,9 @@
 
 
 def filter_rows(payload, weights, group, scaling, gt_scr):
-    total = payload[0].astype(f32)
-    for a in range(1, payload.shape[0]):
-        total = total + payload[a].astype(f32)
+    total = payload[0][...].astype(f32)
+    for part in payload[1:]:
+        total = total + part[...].astype(f32)
     counts = jnp.concatenate([total[336:368], total[368:400]], 1)
     lane = iota((32, LANES), 1)
     index = iota((32, LANES), 0) - MAXM
@@ -280,8 +298,8 @@
     gt_scr[128:144, :] = jnp.concatenate([low, jnp.zeros_like(low)], 0).astype(bf16)
 
 
-def back_kernel(ka_split, scaling, sub, payload, weights, z, *refs):
-    basis, out, gt_scr = refs[:PARTS], refs[PARTS], refs[PARTS + 1]
+def back_kernel(ka_split, scaling, sub, weights, z, *refs):
+    basis, payload, out, gt_scr = refs[:PARTS], refs[PARTS:-2], refs[-2], refs[-1]
     width = out.shape[2]
     filter_rows(payload, weights, lax.axis_index("ka") // ka_split, scaling, gt_scr)
     for j, piece in enumerate(basis):
@@ -334,12 +352,17 @@
     params = pltpu.CompilerParams(vmem_limit_bytes=24 * 1024 * 1024)
 
     blocks = n_ka // n_atom
+    near = blocks // 2
+    flips = [
+        [near * a + j for j in range(near)] + [n_ka - 1 - near * a - j for j in range(blocks - near)]
+        for a in range(n_atom)
+    ]
     millers = []
     for j in range(blocks):
         pairs = []
         for a in range(n_atom):
             for b in range(n_ka):
-                pairs.append((a * n_ka + (b ^ (blocks * a + j)), a * n_ka + b))
+                pairs.append((a * n_ka + (b ^ flips[a][j]), a * n_ka + b))
         millers.append(lax.ppermute(miller, ("atom", "ka"), pairs))
 
     whole = pl.BlockSpec(memory_space=pltpu.VMEM)
@@ -347,7 +370,7 @@
     hbm = pl.BlockSpec(memory_space=pltpu.HBM)
     z, acc, local_features, *basis = pl.pallas_call(
         functools.partial(factor_kernel, ka_split),
-        in_specs=[hbm, hbm, hbm, whole],
+        in_specs=[hbm] * 4,
         out_specs=[whole] * (3 + PARTS),
         out_shape=[
             jax.ShapeDtypeStruct((16, atoms_here), f32),
@@ -359,11 +382,12 @@
             pltpu.VMEM((3, atoms_here), f32),
             pltpu.VMEM((16, atoms_here), bf16),
             pltpu.VMEM((1, atoms_here), jnp.int32),
+            pltpu.VMEM((NSPEC, channels), f32),
             pltpu.VMEM((144, atoms_here), bf16),
             pltpu.VMEM((LANES, LANES), f32),
             pltpu.VMEM((LANES, LANES), f32),
             pltpu.VMEM((LANES, LANES), f32),
-            pltpu.SemaphoreType.DMA((4,)),
+            pltpu.SemaphoreType.DMA((2 + 3 * PARTS,)),
         ],
         compiler_params=params,
         cost_estimate=pl.CostEstimate(flops=5 * 10**9, bytes_accessed=14 * 10**6, transcendentals=0),
@@ -372,7 +396,7 @@
         pltpu.with_memory_space_constraint(positions, pltpu.HBM),
         pltpu.with_memory_space_constraint(features, pltpu.HBM),
         pltpu.with_memory_space_constraint(species.reshape(1, atoms_here), pltpu.HBM),
-        species_table.T,
+        pltpu.with_memory_space_constraint(species_table.T, pltpu.HBM),
     )
 
     payload = pl.pallas_call(
@@ -383,18 +407,30 @@
         compiler_params=params,
         name="pack",
     )(acc, *millers)
-    gathered = lax.all_gather(payload, "atom")
+    if n_atom == 4:
+        across = lax.ppermute(payload, "atom", [(a, a ^ 2) for a in range(4)])
+        payload = pl.pallas_call(
+            fold_kernel,
+            in_specs=[whole] * 2,
+            out_specs=whole,
+            out_shape=jax.ShapeDtypeStruct((PAYLOAD, LANES), bf16),
+            compiler_params=params,
+            name="fold",
+        )(payload, across)
+        gathered = [payload, lax.ppermute(payload, "atom", [(a, a ^ 1) for a in range(4)])]
+    else:
+        gathered = list(lax.all_gather(payload, "atom"))
 
     message = pl.pallas_call(
         functools.partial(back_kernel, ka_split, scaling, min(512, local_count)),
-        in_specs=[whole] * (3 + PARTS),
+        in_specs=[whole] * (2 + PARTS + len(gathered)),
         out_specs=whole,
         out_shape=jax.ShapeDtypeStruct((n_ka, GROUP, local_count), bf16),
         scratch_shapes=[pltpu.VMEM((144, 384), bf16)],
         compiler_params=params,
         cost_estimate=pl.CostEstimate(flops=5 * 10**9, bytes_accessed=11 * 10**6, transcendentals=0),
         name="back",
-    )(gathered, filter_weight.T, z, *basis)
+    )(filter_weight.T, z, *basis, *gathered)
 
     groups = None
     if ka_split > 1:
@@ -404,7 +440,7 @@
     message = lax.all_to_all(message, "ka", 0, 0, axis_index_groups=groups, tiled=True)
 
     return pl.pallas_call(
-        functools.partial(update_kernel, 512),
+        functools.partial(update_kernel, local_count),
         in_specs=[whole] * 5,
         out_specs=whole,
         out_shape=jax.ShapeDtypeStruct((channels, local_count), bf16),

time: 41.7 us -> 37.7 us (0.904)
  blocking collectives: 23.6 us -> 11.9 us
  starting transfers between devices: 4.31 us -> 10.1 us
  waiting for transfers between devices: 0.01 us -> 3.94 us
  Pallas kernels: 12.7 us -> 11.5 us
  local copies, waits for them, and re-layouts: 0.7 us -> 0.01 us
    all_gather x1 -> x0, blocking collectives: 9.47 us -> none  [body(): gathered = lax.all_gather(payload, 'atom')]
    ppermute x0 -> x2, waiting for transfers between devices: none -> 3.93 us  [the longest x1 2.64 us: body(): across = lax.ppermute(payload, 'atom', [(a, a ^ 2) for a in range(4)])]
    ppermute x2, starting transfers between devices: 4.31 us -> 7.35 us  [body(): millers.append(lax.ppermute(miller, ('atom', 'ka'), pairs))]
    ppermute x0 -> x2, starting transfers between devices: none -> 2.75 us  [the longest x1 2.68 us: body(): across = lax.ppermute(payload, 'atom', [(a, a ^ 2) for a in range(4)])]
    all_to_all x1, blocking collectives: 14.1 us -> 11.9 us  [body(): lax.all_to_all(message, 'ka', 0, 0, axis_index_groups=groups, tiled=True)]
    pallas_call x2 -> x3, Pallas kernels: 8.64 us -> 7.72 us  [the longest x1 6.14 us: body(): pl.pallas_call(functools.partial(factor_kernel, ka_split), in_specs=[hbm]...]
    unnamed x10 -> x8, local copies, waits for them, and re-layouts: 0.7 us -> 0.01 us
  transfers between devices with their start and end apart: 2 -> 4, of which waited for: 0 -> 2; matrix products, arithmetic and copies ran while one was open for 0% -> 0% of each run, Pallas kernels for 16% -> 16%
where the time goes in v3:
time: 37.7 us; the launch traced here: 37.5 us
  blocking collectives  11.9 us (32%)
  Pallas kernels  11.5 us (31%)
  starting transfers between devices  10.1 us (27%)
  waiting for transfers between devices  3.94 us (10%)
    all_to_all x1, blocking collectives, body(): lax.all_to_all(message, 'ka', 0, 0, axis_index_groups=groups, tiled=True)  11.9 us
    ppermute x2, starting transfers between devices, body(): millers.append(lax.ppermute(miller, ('atom', 'ka'), pairs))  7.35 us
    pallas_call x1, Pallas kernels, body(): pl.pallas_call(functools.partial(factor_kernel, ka_split), in_specs=[hbm]...  6.14 us
    pallas_call x1, Pallas kernels, body(): pl.pallas_call(functools.partial(back_kernel, ka_split, scaling, min(512,...  3.45 us
    ppermute x1, starting transfers between devices, body(): across = lax.ppermute(payload, 'atom', [(a, a ^ 2) for a in range(4)])  2.68 us
    ppermute x1, waiting for transfers between devices, body(): across = lax.ppermute(payload, 'atom', [(a, a ^ 2) for a in range(4)])  2.64 us
    pallas_call x1, Pallas kernels, body(): pl.pallas_call(functools.partial(update_kernel, local_count), in_specs=[w...  1.55 us
    ppermute x1, waiting for transfers between devices, body(): lax.ppermute(payload, 'atom', [(a, a ^ 1) for a in range(4)])  1.29 us
  transfers between devices with their start and end apart: 4, of which 2 were waited for; matrix products, arithmetic and copies ran while one was open for 0% of the time, Pallas kernels for 16%

profile of v3, /device:TPU:0, one launch (start us, length us, event | category | flops | bytes accessed | tf_op | source)
XLA Modules:
  0.0 37.5 jit_solution(13223564981607344135)
XLA Ops:
  0.0 6.0 %collective-permute-start.1 = (s32[3,512]{1,0:T(4,128)}, s32[3,512]{1,0:T(4,128)S(1)}, u32[]{:S(2)}, u32[]{:S(2)}) collective-permute-start(s32[3,512]{1,0:T(4,128)} %param.12), channel_id=1, source_target_pairs={{7,0},{6,1},{5,2},{4,3},{3,4},{2,5},{1,6},{0,7},{14,8},{15,9},{12,... | collective-permute-start | bytes 18440 | tf_op jit(solution)/shard_map/ppermute | solution.py:366
  6.0 1.3 %collective-permute-start = (s32[3,512]{1,0:T(4,128)}, s32[3,512]{1,0:T(4,128)S(1)}, u32[]{:S(2)}, u32[]{:S(2)}) collective-permute-start(s32[3,512]{1,0:T(4,128)} %param.12), channel_id=1, source_target_pairs={{0,0},{1,1},{2,2},{3,3},{4,4},{5,5},{6,6},{7,7},{9,8},{8,9},{11,10... | collective-permute-start | bytes 18440 | tf_op jit(solution)/shard_map/ppermute | solution.py:366
  7.3 0.0 copy-start.3
  7.4 6.1 %factors.1 = (f32[16,16384]{1,0:T(8,128)S(1)}, f32[304,144]{1,0:T(8,128)S(1)}, bf16[64,2048]{1,0:T(8,128)(2,1)S(1)}, bf16[304,4096]{1,0:T(8,128)(2,1)S(1)}, bf16...) custom-call(f32[3,16384]{1,0:T(4,128)} %pos_hbm.1, ...), custom_call_target="tpu_custom_call" | custom-call | flops 5000000000 | bytes 14000000 | tf_op jit(solution)/shard_map/factors/pallas_call | solution.py:371
  13.5 0.0 collective-permute-done.1.refs_1_
  13.5 0.0 collective-permute-done.refs_0_
  13.5 0.3 pack.1.left
  13.8 2.7 %collective-permute-start.2 = (bf16[400,128]{1,0:T(8,128)(2,1)S(1)}, bf16[400,128]{1,0:T(8,128)(2,1)S(1)}, u32[]{:S(2)}, u32[]{:S(2)}) collective-permute-start(bf16[400,128]{1,0:T(8,128)(2,1)S(1)} %pack.1.left), channel_id=1, source_target_pairs={{0,16},{8,24},{16,0},{24,8},{1,17},{9,25},{17,1},{25,9},{2,18},{10... | collective-permute-start | bytes 307208 | tf_op jit(solution)/shard_map/ppermute | solution.py:411
  16.5 2.6 %collective-permute-done.2.right = bf16[400,128]{1,0:T(8,128)(2,1)S(1)} collective-permute-done((bf16[400,128]{1,0:T(8,128)(2,1)S(1)}, bf16[400,128]{1,0:T(8,128)(2,1)S(1)}, u32[]{:S(2)}, u32[]{:S(2)}) %collective-permute-start.2) | collective-permute-done | bytes 102432 | tf_op jit(solution)/shard_map/ppermute | solution.py:411
  19.2 0.1 collective-permute-start.3
  19.3 1.3 %collective-permute-done.3.refs_5_ = bf16[400,128]{1,0:T(8,128)(2,1)S(1)} collective-permute-done((bf16[400,128]{1,0:T(8,128)(2,1)S(1)}, bf16[400,128]{1,0:T(8,128)(2,1)S(1)}, u32[]{:S(2)}, u32[]{:S(2)}) %collective-permute-start.3) | collective-permute-done | bytes 102432 | tf_op jit(solution)/shard_map/ppermute | solution.py:420
  20.5 0.0 copy-done.3
  20.5 0.0 copy-start
  20.6 0.0 copy-start.1
  20.6 0.0 copy-start.2
  20.6 3.5 %back.1 = bf16[8,8,2048]{2,1,0:T(8,128)(2,1)S(1)} custom-call(f32[16,64]{1,0:T(8,128)S(1)} %bitcast.7, f32[16,16384]{1,0:T(8,128)S(1)} %get-tuple-element.12.z, bf16[304,4096]{1,0:T(8,128)(2,1)S(1)} %get-tuple-element.13.refs_0_, bf16[304,4096]{1,0:T(8,128)(2,1)S(1)} %get-tuple-element.14.refs_1_, bf16[304,4096]{1,0:T(8,128)(2,1)S(1)} %get-tuple-element.15.refs_2_, ...), custom_call_target="tpu_custom_call" | custom-call | flops 5000000000 | bytes 11000000 | tf_op jit(solution)/shard_map/back/pallas_call | solution.py:424
  24.0 11.9 %all_to_all.5.message = bf16[8,8,2048]{2,1,0:T(8,128)(2,1)S(1)} all-to-all(bf16[8,8,2048]{2,1,0:T(8,128)(2,1)S(1)} %back.1), channel_id=1, replica_groups=mesh['atom'=4,'ka'=8] {'ka'}, dimensions={0} | all-to-all | bytes 524288 | tf_op jit(solution)/shard_map/all_to_all | solution.py:440
  35.9 0.0 copy-done
  36.0 0.0 copy-done.1
  36.0 0.0 copy-done.2
  36.0 1.6 %update.1 = bf16[64,2048]{1,0:T(8,128)(2,1)} custom-call(bf16[8,8,2048]{2,1,0:T(8,128)(2,1)S(1)} %all_to_all.5.message, bf16[64,2048]{1,0:T(8,128)(2,1)S(1)} %get-tuple-element.18.feat, f32[1,64]{1,0:T(1,128)S(1)} %bitcast.6, bf16[64,256]{1,0:T(8,128)(2,1)S(1)} %bitcast.5, bf16[64,256]{1,0:T(8,128)(2,1)S(1)} %copy-done.1), custom_call_target="tpu_custom_call" | custom-call | tf_op jit(solution)/shard_map/update/pallas_call | solution.py:442
  (1 shorter events, 0.0 us)
Async XLA Ops:
  0.0 13.5 %collective-permute-start.1 = (s32[3,512]{1,0:T(4,128)}, s32[3,512]{1,0:T(4,128)S(1)}, u32[]{:S(2)}, u32[]{:S(2)}) collective-permute-start(s32[3,512]{1,0:T(4,128)} %param.12), channel_id=1, source_target_pairs={{7,0},{6,1},{5,2},{4,3},{3,4},{2,5},{1,6},{0,7},{14,8},{15,9},{12,... | collective-permute-start | bytes 18440 | tf_op jit(solution)/shard_map/ppermute | solution.py:366
  6.0 7.5 %collective-permute-start = (s32[3,512]{1,0:T(4,128)}, s32[3,512]{1,0:T(4,128)S(1)}, u32[]{:S(2)}, u32[]{:S(2)}) collective-permute-start(s32[3,512]{1,0:T(4,128)} %param.12), channel_id=1, source_target_pairs={{0,0},{1,1},{2,2},{3,3},{4,4},{5,5},{6,6},{7,7},{9,8},{8,9},{11,10... | collective-permute-start | bytes 18440 | tf_op jit(solution)/shard_map/ppermute | solution.py:366
  7.3 13.2 %copy-start.3 = (f32[64,16]{0,1:T(8,128)S(1)}, f32[64,16]{0,1:T(8,128)}, u32[]{:S(2)}) copy-start(f32[64,16]{0,1:T(8,128)} %param.14) | copy-start | bytes 12292
  13.8 5.3 %collective-permute-start.2 = (bf16[400,128]{1,0:T(8,128)(2,1)S(1)}, bf16[400,128]{1,0:T(8,128)(2,1)S(1)}, u32[]{:S(2)}, u32[]{:S(2)}) collective-permute-start(bf16[400,128]{1,0:T(8,128)(2,1)S(1)} %pack.1.left), channel_id=1, source_target_pairs={{0,16},{8,24},{16,0},{24,8},{1,17},{9,25},{17,1},{25,9},{2,18},{10... | collective-permute-start | bytes 307208 | tf_op jit(solution)/shard_map/ppermute | solution.py:411
  19.2 1.4 %collective-permute-start.3 = (bf16[400,128]{1,0:T(8,128)(2,1)S(1)}, bf16[400,128]{1,0:T(8,128)(2,1)S(1)}, u32[]{:S(2)}, u32[]{:S(2)}) collective-permute-start(bf16[400,128]{1,0:T(8,128)(2,1)S(1)} %fold.1.refs_4_), channel_id=1, source_target_pairs={{0,8},{8,0},{16,24},{24,16},{1,9},{9,1},{17,25},{25,17},{2,10},{10... | collective-permute-start | bytes 307208 | tf_op jit(solution)/shard_map/ppermute | solution.py:420
  20.5 15.4 %copy-start = (bf16[256,64]{0,1:T(8,128)(2,1)S(1)}, bf16[256,64]{0,1:T(8,128)(2,1)}, u32[]{:S(2)}) copy-start(bf16[256,64]{0,1:T(8,128)(2,1)} %param.16) | copy-start | bytes 98308
  20.6 15.4 %copy-start.1 = (bf16[64,256]{1,0:T(8,128)(2,1)S(1)}, bf16[64,256]{1,0:T(8,128)(2,1)}, u32[]{:S(2)}) copy-start(bf16[64,256]{1,0:T(8,128)(2,1)} %down.1) | copy-start | bytes 98308
  20.6 15.4 %copy-start.2 = (f32[64]{0:T(128)S(1)}, f32[64]{0:T(128)}, u32[]{:S(2)}) copy-start(f32[64]{0:T(128)} %param.15) | copy-start | bytes 772

commit v4 on v3

--- a/solution.py
+++ b/solution.py
@@ -177,7 +177,7 @@
     keep.wait()
 
 
-def pack_kernel(acc, *refs):
+def pack_kernel(acc, own, *refs):
     millers, out = refs[:-1], refs[-1]
     out[0:ROWS, :] = acc[:, 0:LANES].astype(bf16)
     tail = jnp.concatenate([acc[:, 128:144], jnp.zeros((ROWS, 112), f32)], 1)
@@ -187,8 +187,10 @@
     pieces = [flat[0:8, 0:128], flat[0:8, 128:256], flat[0:8, 256:384], zero]
     out[304:336, :] = jnp.concatenate(pieces, 0).astype(bf16)
     counts = jnp.zeros((32, 256), f32)
-    for ref in millers:
-        m0, m1, m2 = ref[0:1, :], ref[1:2, :], ref[2:3, :]
+    at_first = lax.axis_index("atom") == 0
+    for j, ref in enumerate(millers[::-1]):
+        value = jnp.where(at_first, own[...], ref[...]) if j == 0 else ref[...]
+        m0, m1, m2 = value[0:1, :], value[1:2, :], value[2:3, :]
         sign = jnp.where(17 * m0 + m1 < 0, -1, 1)
         m0, m1, m2 = m0 * sign, m1 * sign, m2 * sign
         inner = jnp.where(
@@ -220,19 +222,9 @@
     return total
 
 
-def filter_rows(payload, weights, group, scaling, gt_scr):
-    total = payload[0][...].astype(f32)
-    for part in payload[1:]:
-        total = total + part[...].astype(f32)
-    counts = jnp.concatenate([total[336:368], total[368:400]], 1)
-    lane = iota((32, LANES), 1)
-    index = iota((32, LANES), 0) - MAXM
-    height = (lane % 64) // 8 + 1
-    plus = jnp.where(jnp.abs(index) == height, 1.0, 0.0)
-    minus = jnp.where(index == height, 1.0, jnp.where(index == -height, -1.0, 0.0))
-    minus = jnp.where(lane < 64, -minus, minus)
-    spread = jnp.concatenate([plus, minus], 1).astype(f32)
-    wide = exact_dot(counts.T, spread, 1, 0)
+def tables_kernel(ka_split, scaling, weights, token, radial_out, flat_out):
+    del token
+    group = lax.axis_index("ka") // ka_split
     across = exact_dot(weights[...], choose(group, LANES), 1, 1)
     lane = iota((88, LANES), 1)
     row = iota((88, LANES), 0)
@@ -247,13 +239,40 @@
     radial = radial_sum((planar + third * third).astype(f32), lambda b: across[b : b + 1, :]) * scaling
     radial = jnp.concatenate([radial[0:64], radial], 0)
 
+    radial_out[...] = radial
+
+    lane = iota((8, LANES), 1)
+    cell = (lane // 16 + 1) * (lane // 16 + 1) + (lane % 8 + 1) * (lane % 8 + 1)
+    edge = jnp.where(lane < 32, (lane % 8 + 1) * (lane % 8 + 1), 0)
+    own = exact_dot(choose(group, GROUP), weights[...], 1, 1)
+    flat_out[...] = radial_sum(
+        jnp.concatenate([cell, edge], 1).astype(f32), lambda b: own[:, b : b + 1]
+    ) * scaling
+
+
+def filter_rows(payload, radial, flat, gt_scr):
+    total = payload[0][...].astype(f32)
+    for part in payload[1:]:
+        total = total + part[...].astype(f32)
+    counts = jnp.concatenate([total[336:368], total[368:400]], 1)
+    lane = iota((32, LANES), 1)
+    index = iota((32, LANES), 0) - MAXM
+    height = (lane % 64) // 8 + 1
+    plus = jnp.where(jnp.abs(index) == height, 1.0, 0.0)
+    minus = jnp.where(index == height, 1.0, jnp.where(index == -height, -1.0, 0.0))
+    minus = jnp.where(lane < 64, -minus, minus)
+    spread = jnp.concatenate([plus, minus], 1).astype(f32)
+    high = jnp.floor(counts * (1.0 / 64.0))
+    split = jnp.concatenate([high, counts - 64.0 * high], 0).astype(bf16)
+    scale = jnp.concatenate([64.0 * spread, spread], 0).astype(bf16)
+    wide = lax.dot_general(split, scale, (((0,), (0,)), ((), ())), preferred_element_type=f32)
     def by_rows(value):
         both = value[0:128].reshape(8, 2, 8, LANES)
         edges = [value[128:136], value[144:152], value[160:168]]
         return jnp.concatenate([both[:, 0].reshape(64, LANES), both[:, 1].reshape(64, LANES)] + edges, 0)
 
-    w_sum = by_rows(wide[:, 0:128]) * radial
-    w_dif = by_rows(wide[:, 128:256]) * radial
+    w_sum = by_rows(wide[:, 0:128]) * radial[...]
+    w_dif = by_rows(wide[:, 128:256]) * radial[...]
     upper = total[0:128].reshape(8, 2, 8, LANES)
     lower = total[128:256].reshape(8, 2, 8, LANES)
     cc, cs = upper[:, 0].reshape(64, LANES), upper[:, 1].reshape(64, LANES)
@@ -275,12 +294,6 @@
     gt_scr[0:128, :] = full.T.astype(bf16)
 
     lane = iota((8, LANES), 1)
-    cell = (lane // 16 + 1) * (lane // 16 + 1) + (lane % 8 + 1) * (lane % 8 + 1)
-    edge = jnp.where(lane < 32, (lane % 8 + 1) * (lane % 8 + 1), 0)
-    own = exact_dot(choose(group, GROUP), weights[...], 1, 1)
-    flat = radial_sum(
-        jnp.concatenate([cell, edge], 1).astype(f32), lambda b: own[:, b : b + 1]
-    ) * scaling
     count0 = jnp.broadcast_to(counts[8:9, 0:128], (8, LANES))
     count1 = jnp.broadcast_to(counts[8:9, 128:256], (8, LANES))
     left = (lane // 8) % 2 == 0
@@ -298,10 +311,10 @@
     gt_scr[128:144, :] = jnp.concatenate([low, jnp.zeros_like(low)], 0).astype(bf16)
 
 
-def back_kernel(ka_split, scaling, sub, weights, z, *refs):
+def back_kernel(sub, radial, flat, z, *refs):
     basis, payload, out, gt_scr = refs[:PARTS], refs[PARTS:-2], refs[-2], refs[-1]
     width = out.shape[2]
-    filter_rows(payload, weights, lax.axis_index("ka") // ka_split, scaling, gt_scr)
+    filter_rows(payload, radial, flat, gt_scr)
     for j, piece in enumerate(basis):
         size = piece.shape[1]
         product = jnp.dot(gt_scr[:, 0:ROWS], piece[...], preferred_element_type=f32)
@@ -362,7 +375,8 @@
         pairs = []
         for a in range(n_atom):
             for b in range(n_ka):
-                pairs.append((a * n_ka + (b ^ flips[a][j]), a * n_ka + b))
+                if flips[a][j]:
+                    pairs.append((a * n_ka + (b ^ flips[a][j]), a * n_ka + b))
         millers.append(lax.ppermute(miller, ("atom", "ka"), pairs))
 
     whole = pl.BlockSpec(memory_space=pltpu.VMEM)
@@ -401,12 +415,24 @@
 
     payload = pl.pallas_call(
         pack_kernel,
-        in_specs=[whole] * (1 + blocks),
+        in_specs=[whole] * (2 + blocks),
         out_specs=whole,
         out_shape=jax.ShapeDtypeStruct((PAYLOAD, LANES), bf16),
         compiler_params=params,
         name="pack",
-    )(acc, *millers)
+    )(acc, miller, *millers[::-1])
+    radial, flat = pl.pallas_call(
+        functools.partial(tables_kernel, ka_split, scaling),
+        in_specs=[whole, pl.BlockSpec(memory_space=pl.ANY)],
+        out_specs=[whole, whole],
+        out_shape=[
+            jax.ShapeDtypeStruct((152, LANES), f32),
+            jax.ShapeDtypeStruct((GROUP, 2 * LANES), f32),
+        ],
+        compiler_params=params,
+        cost_estimate=pl.CostEstimate(flops=10**9, bytes_accessed=10**6, transcendentals=10**6),
+        name="tables",
+    )(filter_weight.T, payload)
     if n_atom == 4:
         across = lax.ppermute(payload, "atom", [(a, a ^ 2) for a in range(4)])
         payload = pl.pallas_call(
@@ -422,15 +448,15 @@
         gathered = list(lax.all_gather(payload, "atom"))
 
     message = pl.pallas_call(
-        functools.partial(back_kernel, ka_split, scaling, min(512, local_count)),
-        in_specs=[whole] * (2 + PARTS + len(gathered)),
+        functools.partial(back_kernel, min(512, local_count)),
+        in_specs=[whole] * (3 + PARTS + len(gathered)),
         out_specs=whole,
         out_shape=jax.ShapeDtypeStruct((n_ka, GROUP, local_count), bf16),
         scratch_shapes=[pltpu.VMEM((144, 384), bf16)],
         compiler_params=params,
         cost_estimate=pl.CostEstimate(flops=5 * 10**9, bytes_accessed=11 * 10**6, transcendentals=0),
         name="back",
-    )(filter_weight.T, z, *basis, *gathered)
+    )(radial, flat, z, *basis, *gathered)
 
     groups = None
     if ka_split > 1:

time: 37.7 us -> 37.2 us (0.987)
  waiting for transfers between devices: 3.94 us -> 3.5 us
    ppermute x2, starting transfers between devices: 7.35 us -> 6.65 us  [body(): millers.append(lax.ppermute(miller, ('atom', 'ka'), pairs))]
    ppermute x1, starting transfers between devices: 2.68 us -> 3.37 us  [body(): across = lax.ppermute(payload, 'atom', [(a, a ^ 2) for a in range(4)])]
    ppermute x1, waiting for transfers between devices: 1.29 us -> 0.86 us  [body(): lax.ppermute(payload, 'atom', [(a, a ^ 1) for a in range(4)])]
    pallas_call x2 -> x3, Pallas kernels: 3.75 us -> 3.63 us  [the longest x1 2.93 us: body(): pl.pallas_call(functools.partial(back_kernel, min(512, local_count)), in_...]
  transfers between devices with their start and end apart: 4 -> 4, of which waited for: 2 -> 2; matrix products, arithmetic and copies ran while one was open for 0% -> 0% of each run, Pallas kernels for 16% -> 18%
where the time goes in v4:
time: 37.2 us; the launch traced here: 37 us
  blocking collectives  11.9 us (32%)
  Pallas kernels  11.3 us (30%)
  starting transfers between devices  10.1 us (27%)
  waiting for transfers between devices  3.5 us (9%)
    all_to_all x1, blocking collectives, body(): lax.all_to_all(message, 'ka', 0, 0, axis_index_groups=groups, tiled=True)  11.9 us
    ppermute x2, starting transfers between devices, body(): millers.append(lax.ppermute(miller, ('atom', 'ka'), pairs))  6.65 us
    pallas_call x1, Pallas kernels, body(): pl.pallas_call(functools.partial(factor_kernel, ka_split), in_specs=[hbm]...  6.14 us
    ppermute x1, starting transfers between devices, body(): across = lax.ppermute(payload, 'atom', [(a, a ^ 2) for a in range(4)])  3.37 us
    pallas_call x1, Pallas kernels, body(): pl.pallas_call(functools.partial(back_kernel, min(512, local_count)), in_...  2.93 us
    ppermute x1, waiting for transfers between devices, body(): across = lax.ppermute(payload, 'atom', [(a, a ^ 2) for a in range(4)])  2.64 us
    pallas_call x1, Pallas kernels, body(): pl.pallas_call(functools.partial(update_kernel, local_count), in_specs=[w...  1.55 us
    ppermute x1, waiting for transfers between devices, body(): lax.ppermute(payload, 'atom', [(a, a ^ 1) for a in range(4)])  0.86 us
  transfers between devices with their start and end apart: 4, of which 2 were waited for; matrix products, arithmetic and copies ran while one was open for 0% of the time, Pallas kernels for 18%

profile of v4, /device:TPU:0, one launch (start us, length us, event | category | flops | bytes accessed | tf_op | source)
XLA Modules:
  0.0 37.0 jit_solution(13506650895133361554)
XLA Ops:
  0.0 6.0 %collective-permute-start = (s32[3,512]{1,0:T(4,128)}, s32[3,512]{1,0:T(4,128)S(1)}, u32[]{:S(2)}, u32[]{:S(2)}) collective-permute-start(s32[3,512]{1,0:T(4,128)} %own.1), channel_id=1, source_target_pairs={{7,0},{6,1},{5,2},{4,3},{3,4},{2,5},{1,6},{0,7},{14,8},{15,9},{12,... | collective-permute-start | bytes 18440 | tf_op jit(solution)/shard_map/ppermute | solution.py:380
  6.0 0.6 %collective-permute-start.1 = (s32[3,512]{1,0:T(4,128)}, s32[3,512]{1,0:T(4,128)S(1)}, u32[]{:S(2)}, u32[]{:S(2)}) collective-permute-start(s32[3,512]{1,0:T(4,128)} %own.1), channel_id=1, source_target_pairs={{9,8},{8,9},{11,10},{10,11},{13,12},{12,13},{15,14},{14,15},{18,16... | collective-permute-start | bytes 18440 | tf_op jit(solution)/shard_map/ppermute | solution.py:380
  6.7 0.0 copy-start.2
  6.7 0.0 copy-start.4
  6.7 6.1 %factors.1 = (f32[16,16384]{1,0:T(8,128)S(1)}, f32[304,144]{1,0:T(8,128)S(1)}, bf16[64,2048]{1,0:T(8,128)(2,1)S(1)}, bf16[304,4096]{1,0:T(8,128)(2,1)S(1)}, bf16...) custom-call(f32[3,16384]{1,0:T(4,128)} %pos_hbm.1, ...), custom_call_target="tpu_custom_call" | custom-call | flops 5000000000 | bytes 14000000 | tf_op jit(solution)/shard_map/factors/pallas_call | solution.py:385
  12.8 0.0 collective-permute-done.refs_0_
  12.8 0.0 collective-permute-done.1.refs_1_
  12.8 0.0 copy-done.2
  12.9 0.3 pack.1.token.left
  13.1 3.4 %collective-permute-start.2 = (bf16[400,128]{1,0:T(8,128)(2,1)S(1)}, bf16[400,128]{1,0:T(8,128)(2,1)S(1)}, u32[]{:S(2)}, u32[]{:S(2)}) collective-permute-start(bf16[400,128]{1,0:T(8,128)(2,1)S(1)} %pack.1.token.left), channel_id=1, source_target_pairs={{0,16},{8,24},{16,0},{24,8},{1,17},{9,25},{17,1},{25,9},{2,18},{10... | collective-permute-start | bytes 307208 | tf_op jit(solution)/shard_map/ppermute | solution.py:437
  16.5 2.6 %collective-permute-done.2.right = bf16[400,128]{1,0:T(8,128)(2,1)S(1)} collective-permute-done((bf16[400,128]{1,0:T(8,128)(2,1)S(1)}, bf16[400,128]{1,0:T(8,128)(2,1)S(1)}, u32[]{:S(2)}, u32[]{:S(2)}) %collective-permute-start.2) | collective-permute-done | bytes 102432 | tf_op jit(solution)/shard_map/ppermute | solution.py:437
  19.2 0.1 collective-permute-start.3
  19.3 0.0 copy-done.4
  19.3 0.4 %tables.1 = (f32[152,128]{1,0:T(8,128)S(1)}, f32[8,256]{1,0:T(8,128)S(1)}) custom-call(f32[16,64]{1,0:T(8,128)S(1)} %bitcast.7, bf16[400,128]{1,0:T(8,128)(2,1)S(1)} %pack.1.token.left), custom_call_target="tpu_custom_call" | custom-call | flops 1000000000 | bytes 1000000 | tf_op jit(solution)/shard_map/tables/pallas_call | solution.py:424
  19.7 0.9 %collective-permute-done.3.refs_5_ = bf16[400,128]{1,0:T(8,128)(2,1)S(1)} collective-permute-done((bf16[400,128]{1,0:T(8,128)(2,1)S(1)}, bf16[400,128]{1,0:T(8,128)(2,1)S(1)}, u32[]{:S(2)}, u32[]{:S(2)}) %collective-permute-start.3) | collective-permute-done | bytes 102432 | tf_op jit(solution)/shard_map/ppermute | solution.py:446
  20.6 0.0 copy-start
  20.6 0.0 copy-start.1
  20.6 0.0 copy-start.3
  20.6 2.9 %back.1 = bf16[8,8,2048]{2,1,0:T(8,128)(2,1)S(1)} custom-call(f32[152,128]{1,0:T(8,128)S(1)} %get-tuple-element.15.radial, f32[8,256]{1,0:T(8,128)S(1)} %get-tuple-element.16.flat, f32[16,16384]{1,0:T(8,128)S(1)} %get-tuple-element.17.z, bf16[304,4096]{1,0:T(8,128)(2,1)S(1)} %get-tuple-element.18.refs_0_, bf16[304,4096]{1,0:T(8,128)(2,1)S(1)} %get-tuple-element.19.refs_1_, ...), custom_call_target="tpu_custom_call" | custom-call | flops 5000000000 | bytes 11000000 | tf_op jit(solution)/shard_map/back/pallas_call | solution.py:450
  23.5 11.9 %all_to_all.5.message = bf16[8,8,2048]{2,1,0:T(8,128)(2,1)S(1)} all-to-all(bf16[8,8,2048]{2,1,0:T(8,128)(2,1)S(1)} %back.1), channel_id=1, replica_groups=mesh['atom'=4,'ka'=8] {'ka'}, dimensions={0} | all-to-all | bytes 524288 | tf_op jit(solution)/shard_map/all_to_all | solution.py:466
  35.4 0.0 copy-done
  35.4 0.0 copy-done.1
  35.4 0.0 copy-done.3
  35.4 1.6 %update.1 = bf16[64,2048]{1,0:T(8,128)(2,1)} custom-call(bf16[8,8,2048]{2,1,0:T(8,128)(2,1)S(1)} %all_to_all.5.message, bf16[64,2048]{1,0:T(8,128)(2,1)S(1)} %get-tuple-element.22.feat, f32[1,64]{1,0:T(1,128)S(1)} %bitcast.6, bf16[64,256]{1,0:T(8,128)(2,1)S(1)} %bitcast.5, bf16[64,256]{1,0:T(8,128)(2,1)S(1)} %copy-done.1), custom_call_target="tpu_custom_call" | custom-call | tf_op jit(solution)/shard_map/update/pallas_call | solution.py:468
  (1 shorter events, 0.0 us)
Async XLA Ops:
  0.0 12.8 %collective-permute-start = (s32[3,512]{1,0:T(4,128)}, s32[3,512]{1,0:T(4,128)S(1)}, u32[]{:S(2)}, u32[]{:S(2)}) collective-permute-start(s32[3,512]{1,0:T(4,128)} %own.1), channel_id=1, source_target_pairs={{7,0},{6,1},{5,2},{4,3},{3,4},{2,5},{1,6},{0,7},{14,8},{15,9},{12,... | collective-permute-start | bytes 18440 | tf_op jit(solution)/shard_map/ppermute | solution.py:380
  6.0 6.8 %collective-permute-start.1 = (s32[3,512]{1,0:T(4,128)}, s32[3,512]{1,0:T(4,128)S(1)}, u32[]{:S(2)}, u32[]{:S(2)}) collective-permute-start(s32[3,512]{1,0:T(4,128)} %own.1), channel_id=1, source_target_pairs={{9,8},{8,9},{11,10},{10,11},{13,12},{12,13},{15,14},{14,15},{18,16... | collective-permute-start | bytes 18440 | tf_op jit(solution)/shard_map/ppermute | solution.py:380
  6.7 6.2 %copy-start.2 = (s32[3,512]{1,0:T(4,128)S(1)}, s32[3,512]{1,0:T(4,128)}, u32[]{:S(2)}) copy-start(s32[3,512]{1,0:T(4,128)} %own.1) | copy-start | bytes 18436
  6.7 12.6 %copy-start.4 = (f32[64,16]{0,1:T(8,128)S(1)}, f32[64,16]{0,1:T(8,128)}, u32[]{:S(2)}) copy-start(f32[64,16]{0,1:T(8,128)} %param.14) | copy-start | bytes 12292
  13.1 6.0 %collective-permute-start.2 = (bf16[400,128]{1,0:T(8,128)(2,1)S(1)}, bf16[400,128]{1,0:T(8,128)(2,1)S(1)}, u32[]{:S(2)}, u32[]{:S(2)}) collective-permute-start(bf16[400,128]{1,0:T(8,128)(2,1)S(1)} %pack.1.token.left), channel_id=1, source_target_pairs={{0,16},{8,24},{16,0},{24,8},{1,17},{9,25},{17,1},{25,9},{2,18},{10... | collective-permute-start | bytes 307208 | tf_op jit(solution)/shard_map/ppermute | solution.py:437
  19.2 1.4 %collective-permute-start.3 = (bf16[400,128]{1,0:T(8,128)(2,1)S(1)}, bf16[400,128]{1,0:T(8,128)(2,1)S(1)}, u32[]{:S(2)}, u32[]{:S(2)}) collective-permute-start(bf16[400,128]{1,0:T(8,128)(2,1)S(1)} %fold.1.refs_4_), channel_id=1, source_target_pairs={{0,8},{8,0},{16,24},{24,16},{1,9},{9,1},{17,25},{25,17},{2,10},{10... | collective-permute-start | bytes 307208 | tf_op jit(solution)/shard_map/ppermute | solution.py:446
  20.6 14.9 %copy-start = (bf16[256,64]{0,1:T(8,128)(2,1)S(1)}, bf16[256,64]{0,1:T(8,128)(2,1)}, u32[]{:S(2)}) copy-start(bf16[256,64]{0,1:T(8,128)(2,1)} %param.16) | copy-start | bytes 98308
  20.6 14.9 %copy-start.1 = (bf16[64,256]{1,0:T(8,128)(2,1)S(1)}, bf16[64,256]{1,0:T(8,128)(2,1)}, u32[]{:S(2)}) copy-start(bf16[64,256]{1,0:T(8,128)(2,1)} %down.1) | copy-start | bytes 98308
  20.6 14.9 %copy-start.3 = (f32[64]{0:T(128)S(1)}, f32[64]{0:T(128)}, u32[]{:S(2)}) copy-start(f32[64]{0:T(128)} %param.15) | copy-start | bytes 772

commit v5 on v4

--- a/solution.py
+++ b/solution.py
@@ -21,6 +21,8 @@
 LANES = 128
 PAYLOAD = 400
 k_cutoff = 14.0
+FAR = (6, 3, 4, 5)
+NEAR = (1, 2, 1, 2)
 f32 = jnp.float32
 bf16 = jnp.bfloat16
 
@@ -177,8 +179,37 @@
     keep.wait()
 
 
-def pack_kernel(acc, own, *refs):
-    millers, out = refs[:-1], refs[-1]
+def histogram(value):
+    m0, m1, m2 = value[0:1, :], value[1:2, :], value[2:3, :]
+    sign = jnp.where(17 * m0 + m1 < 0, -1, 1)
+    m0, m1, m2 = m0 * sign, m1 * sign, m2 * sign
+    inner = jnp.where(
+        m1 > 0, 16 * m0 + m1 - 17, jnp.where(m1 < 0, 16 * m0 - m1 - 9, 127 + m0)
+    )
+    row = jnp.where(m0 > 0, inner, jnp.where(m1 > 0, 143 + m1, 160))
+    column = jnp.where(row == 160, jnp.abs(m2), m2) + MAXM
+    size = row.shape[1]
+    row_hot = (iota((256, size), 0) == row).astype(f32).astype(bf16)
+    column_hot = (iota((32, size), 0) == column).astype(f32).astype(bf16)
+    return lax.dot_general(
+        column_hot, row_hot, (((1,), (1,)), ((), ())), preferred_element_type=f32
+    )
+
+
+def pack_kernel(chained, acc, own, *refs):
+    if chained:
+        (first,), (out, pair_out) = refs[:1], refs[1:]
+        pair_out[0:3, :] = own[...]
+        pair_out[3:6, :] = first[...]
+        at_start = jnp.where(lax.axis_index("atom") == 0, 1.0, 0.0)
+        counts = histogram(first[...]) + at_start * histogram(own[...])
+    else:
+        millers, out = refs[:-1], refs[-1]
+        at_start = lax.axis_index("atom") == 0
+        counts = jnp.zeros((32, 256), f32)
+        for j, ref in enumerate(millers[::-1]):
+            value = jnp.where(at_start, own[...], ref[...]) if j == 0 else ref[...]
+            counts = counts + histogram(value)
     out[0:ROWS, :] = acc[:, 0:LANES].astype(bf16)
     tail = jnp.concatenate([acc[:, 128:144], jnp.zeros((ROWS, 112), f32)], 1)
     tail = jnp.concatenate([tail, jnp.zeros((384 - ROWS, LANES), f32)], 0)
@@ -186,30 +217,17 @@
     zero = jnp.zeros((GROUP, LANES), f32)
     pieces = [flat[0:8, 0:128], flat[0:8, 128:256], flat[0:8, 256:384], zero]
     out[304:336, :] = jnp.concatenate(pieces, 0).astype(bf16)
-    counts = jnp.zeros((32, 256), f32)
-    at_first = lax.axis_index("atom") == 0
-    for j, ref in enumerate(millers[::-1]):
-        value = jnp.where(at_first, own[...], ref[...]) if j == 0 else ref[...]
-        m0, m1, m2 = value[0:1, :], value[1:2, :], value[2:3, :]
-        sign = jnp.where(17 * m0 + m1 < 0, -1, 1)
-        m0, m1, m2 = m0 * sign, m1 * sign, m2 * sign
-        inner = jnp.where(
-            m1 > 0, 16 * m0 + m1 - 17, jnp.where(m1 < 0, 16 * m0 - m1 - 9, 127 + m0)
-        )
-        row = jnp.where(m0 > 0, inner, jnp.where(m1 > 0, 143 + m1, 160))
-        column = jnp.where(row == 160, jnp.abs(m2), m2) + MAXM
-        size = row.shape[1]
-        row_hot = (iota((256, size), 0) == row).astype(f32).astype(bf16)
-        column_hot = (iota((32, size), 0) == column).astype(f32).astype(bf16)
-        counts = counts + lax.dot_general(
-            column_hot, row_hot, (((1,), (1,)), ((), ())), preferred_element_type=f32
-        )
     out[336:368, :] = counts[:, 0:128].astype(bf16)
     out[368:400, :] = counts[:, 128:256].astype(bf16)
 
 
-def fold_kernel(left, right, out):
-    out[...] = (left[...].astype(f32) + right[...].astype(f32)).astype(bf16)
+def fold_kernel(left, right, pair, out):
+    out[0:336, :] = (left[0:336, :].astype(f32) + right[0:336, :].astype(f32)).astype(bf16)
+    atom = lax.axis_index("atom")
+    last = jnp.where(atom // 2 == atom % 2, 1.0, 0.0)
+    extra = histogram(pair[0:3, :]) + last * histogram(pair[3:6, :])
+    counts = left[336:400, :].astype(f32) + right[336:400, :].astype(f32)
+    out[336:400, :] = (counts + jnp.concatenate([extra[:, 0:128], extra[:, 128:256]], 0)).astype(bf16)
 
 
 def radial_sum(square, weight_of):
@@ -364,20 +382,25 @@
     scaling = 1.0 / math.sqrt(atoms_here * n_atom * K)
     params = pltpu.CompilerParams(vmem_limit_bytes=24 * 1024 * 1024)
 
-    blocks = n_ka // n_atom
-    near = blocks // 2
-    flips = [
-        [near * a + j for j in range(near)] + [n_ka - 1 - near * a - j for j in range(blocks - near)]
-        for a in range(n_atom)
-    ]
-    millers = []
-    for j in range(blocks):
+    def exchange(value, flips):
         pairs = []
         for a in range(n_atom):
             for b in range(n_ka):
-                if flips[a][j]:
-                    pairs.append((a * n_ka + (b ^ flips[a][j]), a * n_ka + b))
-        millers.append(lax.ppermute(miller, ("atom", "ka"), pairs))
+                if flips[a]:
+                    pairs.append((a * n_ka + (b ^ flips[a]), a * n_ka + b))
+        return lax.ppermute(value, ("atom", "ka"), pairs)
+
+    chained = (n_atom, n_ka) == (4, 8)
+    if chained:
+        millers = [exchange(miller, FAR)]
+    else:
+        blocks = n_ka // n_atom
+        near = blocks // 2
+        flips = [
+            [near * a + j for j in range(near)] + [n_ka - 1 - near * a - j for j in range(blocks - near)]
+            for a in range(n_atom)
+        ]
+        millers = [exchange(miller, [row[j] for row in flips]) for j in range(blocks)]
 
     whole = pl.BlockSpec(memory_space=pltpu.VMEM)
     hbm = pl.BlockSpec(memory_space=pltpu.HBM)
@@ -413,11 +436,14 @@
         pltpu.with_memory_space_constraint(species_table.T, pltpu.HBM),
     )
 
-    payload = pl.pallas_call(
-        pack_kernel,
-        in_specs=[whole] * (2 + blocks),
-        out_specs=whole,
-        out_shape=jax.ShapeDtypeStruct((PAYLOAD, LANES), bf16),
+    packed = [jax.ShapeDtypeStruct((PAYLOAD, LANES), bf16)]
+    if chained:
+        packed.append(jax.ShapeDtypeStruct((6, miller.shape[1]), jnp.int32))
+    payload, *pair = pl.pallas_call(
+        functools.partial(pack_kernel, chained),
+        in_specs=[whole] * (2 + len(millers)),
+        out_specs=[whole] * len(packed),
+        out_shape=packed,
         compiler_params=params,
         name="pack",
     )(acc, miller, *millers[::-1])
@@ -433,16 +459,16 @@
         cost_estimate=pl.CostEstimate(flops=10**9, bytes_accessed=10**6, transcendentals=10**6),
         name="tables",
     )(filter_weight.T, payload)
-    if n_atom == 4:
+    if chained:
         across = lax.ppermute(payload, "atom", [(a, a ^ 2) for a in range(4)])
         payload = pl.pallas_call(
             fold_kernel,
-            in_specs=[whole] * 2,
+            in_specs=[whole] * 3,
             out_specs=whole,
             out_shape=jax.ShapeDtypeStruct((PAYLOAD, LANES), bf16),
             compiler_params=params,
             name="fold",
-        )(payload, across)
+        )(payload, across, exchange(pair[0], NEAR))
         gathered = [payload, lax.ppermute(payload, "atom", [(a, a ^ 1) for a in range(4)])]
     else:
         gathered = list(lax.all_gather(payload, "atom"))

time: 37.2 us -> 35.4 us (0.952)
  starting transfers between devices: 10.1 us -> 7.18 us
  Pallas kernels: 11.3 us -> 12 us
  blocking collectives: 11.9 us -> 12.4 us
    ppermute x1, starting transfers between devices: 3.37 us -> 0.54 us  [body(): across = lax.ppermute(payload, 'atom', [(a, a ^ 2) for a in range(4)])]
    ppermute x2, waiting for transfers between devices: 0.01 us -> 2.22 us  [exchange(): return lax.ppermute(value, ('atom', 'ka'), pairs)]
    ppermute x1, waiting for transfers between devices: 2.64 us -> 0.44 us  [body(): across = lax.ppermute(payload, 'atom', [(a, a ^ 2) for a in range(4)])]
    all_to_all x1, blocking collectives: 11.9 us -> 12.4 us  [body(): lax.all_to_all(message, 'ka', 0, 0, axis_index_groups=groups, tiled=True)]
  transfers between devices with their start and end apart: 4 -> 4, of which waited for: 2 -> 3; matrix products, arithmetic and copies ran while one was open for 0% -> 0% of each run, Pallas kernels for 18% -> 19%
where the time goes in v5:
time: 35.4 us; the launch traced here: 35.2 us
  blocking collectives  12.4 us (35%)
  Pallas kernels  12 us (34%)
  starting transfers between devices  7.18 us (20%)
  waiting for transfers between devices  3.52 us (10%)
    all_to_all x1, blocking collectives, body(): lax.all_to_all(message, 'ka', 0, 0, axis_index_groups=groups, tiled=True)  12.4 us
    ppermute x2, starting transfers between devices, exchange(): return lax.ppermute(value, ('atom', 'ka'), pairs)  6.57 us
    pallas_call x1, Pallas kernels, body(): pl.pallas_call(functools.partial(factor_kernel, ka_split), in_specs=[hbm]...  6.18 us
    pallas_call x1, Pallas kernels, body(): pl.pallas_call(functools.partial(back_kernel, min(512, local_count)), in_...  3.25 us
    ppermute x2, waiting for transfers between devices, exchange(): return lax.ppermute(value, ('atom', 'ka'), pairs)  2.22 us
    pallas_call x1, Pallas kernels, body(): pl.pallas_call(functools.partial(update_kernel, local_count), in_specs=[w...  1.56 us
    ppermute x1, waiting for transfers between devices, body(): lax.ppermute(payload, 'atom', [(a, a ^ 1) for a in range(4)])  0.86 us
  transfers between devices with their start and end apart: 4, of which 3 were waited for; matrix products, arithmetic and copies ran while one was open for 0% of the time, Pallas kernels for 19%

profile of v5, /device:TPU:0, one launch (start us, length us, event | category | flops | bytes accessed | tf_op | source)
XLA Modules:
  0.0 35.2 jit_solution(463854598787640480)
XLA Ops:
  0.0 5.0 %collective-permute-start = (s32[3,512]{1,0:T(4,128)}, s32[3,512]{1,0:T(4,128)S(1)}, u32[]{:S(2)}, u32[]{:S(2)}) collective-permute-start(s32[3,512]{1,0:T(4,128)} %own.1), channel_id=1, source_target_pairs={{6,0},{7,1},{4,2},{5,3},{2,4},{3,5},{0,6},{1,7},{11,8},{10,9},{9,1... | collective-permute-start | bytes 18440 | tf_op jit(solution)/shard_map/ppermute | solution.py:391
  5.0 0.0 copy-start.2
  5.1 0.0 copy-start.4
  5.1 6.2 %factors.1 = (f32[16,16384]{1,0:T(8,128)S(1)}, f32[304,144]{1,0:T(8,128)S(1)}, bf16[64,2048]{1,0:T(8,128)(2,1)S(1)}, bf16[304,4096]{1,0:T(8,128)(2,1)S(1)}, bf16...) custom-call(f32[3,16384]{1,0:T(4,128)} %pos_hbm.1, ...), custom_call_target="tpu_custom_call" | custom-call | flops 5000000000 | bytes 14000000 | tf_op jit(solution)/shard_map/factors/pallas_call | solution.py:408
  11.2 0.0 collective-permute-done.refs_0_
  11.3 0.0 copy-done.2
  11.3 0.3 pack.1
  11.6 0.5 %collective-permute-start.1 = (bf16[400,128]{1,0:T(8,128)(2,1)S(1)}, bf16[400,128]{1,0:T(8,128)(2,1)S(1)}, u32[]{:S(2)}, u32[]{:S(2)}) collective-permute-start(bf16[400,128]{1,0:T(8,128)(2,1)S(1)} %get-tuple-element.17.token.left), channel_id=1, source_target_pairs={{0,16},{8,24},{16,0},{24,8},{1,17},{9,25},{17,1},{25,9},{2,18},{10... | collective-permute-start | bytes 307208 | tf_op jit(solution)/shard_map/ppermute | solution.py:463
  12.1 1.5 %collective-permute-start.2 = (s32[6,512]{1,0:T(8,128)S(1)}, s32[6,512]{1,0:T(8,128)S(1)}, u32[]{:S(2)}, u32[]{:S(2)}) collective-permute-start(s32[6,512]{1,0:T(8,128)S(1)} %get-tuple-element.25), channel_id=1, source_target_pairs={{1,0},{0,1},{3,2},{2,3},{5,4},{4,5},{7,6},{6,7},{10,8},{11,9},{8,1... | collective-permute-start | bytes 36872 | tf_op jit(solution)/shard_map/ppermute | solution.py:391
  13.7 2.2 %collective-permute-done.2.pair = s32[6,512]{1,0:T(8,128)S(1)} collective-permute-done((s32[6,512]{1,0:T(8,128)S(1)}, s32[6,512]{1,0:T(8,128)S(1)}, u32[]{:S(2)}, u32[]{:S(2)}) %collective-permute-start.2) | collective-permute-done | bytes 12320 | tf_op jit(solution)/shard_map/ppermute | solution.py:391
  15.9 0.4 %collective-permute-done.1.right = bf16[400,128]{1,0:T(8,128)(2,1)S(1)} collective-permute-done((bf16[400,128]{1,0:T(8,128)(2,1)S(1)}, bf16[400,128]{1,0:T(8,128)(2,1)S(1)}, u32[]{:S(2)}, u32[]{:S(2)}) %collective-permute-start.1) | collective-permute-done | bytes 102432 | tf_op jit(solution)/shard_map/ppermute | solution.py:463
  16.3 0.3 fold.1.refs_4_
  16.6 0.1 collective-permute-start.3
  16.7 0.0 copy-done.4
  16.7 0.4 %tables.1 = (f32[152,128]{1,0:T(8,128)S(1)}, f32[8,256]{1,0:T(8,128)S(1)}) custom-call(f32[16,64]{1,0:T(8,128)S(1)} %bitcast.7, bf16[400,128]{1,0:T(8,128)(2,1)S(1)} %get-tuple-element.17.token.left), custom_call_target="tpu_custom_call" | custom-call | flops 1000000000 | bytes 1000000 | tf_op jit(solution)/shard_map/tables/pallas_call | solution.py:450
  17.1 0.9 %collective-permute-done.3.refs_5_ = bf16[400,128]{1,0:T(8,128)(2,1)S(1)} collective-permute-done((bf16[400,128]{1,0:T(8,128)(2,1)S(1)}, bf16[400,128]{1,0:T(8,128)(2,1)S(1)}, u32[]{:S(2)}, u32[]{:S(2)}) %collective-permute-start.3) | collective-permute-done | bytes 102432 | tf_op jit(solution)/shard_map/ppermute | solution.py:472
  18.0 0.0 copy-start
  18.0 0.0 copy-start.1
  18.0 3.3 %back.1 = bf16[8,8,2048]{2,1,0:T(8,128)(2,1)S(1)} custom-call(f32[152,128]{1,0:T(8,128)S(1)} %get-tuple-element.18.radial, f32[8,256]{1,0:T(8,128)S(1)} %get-tuple-element.19.flat, f32[16,16384]{1,0:T(8,128)S(1)} %get-tuple-element.20.z, bf16[304,4096]{1,0:T(8,128)(2,1)S(1)} %get-tuple-element.21.refs_0_, bf16[304,4096]{1,0:T(8,128)(2,1)S(1)} %get-tuple-element.22.refs_1_, ...), custom_call_target="tpu_custom_call" | custom-call | flops 5000000000 | bytes 11000000 | tf_op jit(solution)/shard_map/back/pallas_call | solution.py:476
  21.2 12.4 %all_to_all.5.message = bf16[8,8,2048]{2,1,0:T(8,128)(2,1)S(1)} all-to-all(bf16[8,8,2048]{2,1,0:T(8,128)(2,1)S(1)} %back.1), channel_id=1, replica_groups=mesh['atom'=4,'ka'=8] {'ka'}, dimensions={0} | all-to-all | bytes 524288 | tf_op jit(solution)/shard_map/all_to_all | solution.py:492
  33.6 0.0 copy-done
  33.6 0.0 copy-done.1
  33.7 0.0 copy-done.3
  33.7 1.6 %update.1 = bf16[64,2048]{1,0:T(8,128)(2,1)} custom-call(bf16[8,8,2048]{2,1,0:T(8,128)(2,1)S(1)} %all_to_all.5.message, bf16[64,2048]{1,0:T(8,128)(2,1)S(1)} %get-tuple-element.26.feat, f32[1,64]{1,0:T(1,128)S(1)} %bitcast.6, bf16[64,256]{1,0:T(8,128)(2,1)S(1)} %bitcast.5, bf16[64,256]{1,0:T(8,128)(2,1)S(1)} %copy-done.1), custom_call_target="tpu_custom_call" | custom-call | tf_op jit(solution)/shard_map/update/pallas_call | solution.py:494
  (1 shorter events, 0.0 us)
Async XLA Ops:
  0.0 11.2 %collective-permute-start = (s32[3,512]{1,0:T(4,128)}, s32[3,512]{1,0:T(4,128)S(1)}, u32[]{:S(2)}, u32[]{:S(2)}) collective-permute-start(s32[3,512]{1,0:T(4,128)} %own.1), channel_id=1, source_target_pairs={{6,0},{7,1},{4,2},{5,3},{2,4},{3,5},{0,6},{1,7},{11,8},{10,9},{9,1... | collective-permute-start | bytes 18440 | tf_op jit(solution)/shard_map/ppermute | solution.py:391
  5.0 6.2 %copy-start.2 = (s32[3,512]{1,0:T(4,128)S(1)}, s32[3,512]{1,0:T(4,128)}, u32[]{:S(2)}) copy-start(s32[3,512]{1,0:T(4,128)} %own.1) | copy-start | bytes 18436
  5.1 11.6 %copy-start.4 = (f32[64,16]{0,1:T(8,128)S(1)}, f32[64,16]{0,1:T(8,128)}, u32[]{:S(2)}) copy-start(f32[64,16]{0,1:T(8,128)} %param.14) | copy-start | bytes 12292
  11.6 4.7 %collective-permute-start.1 = (bf16[400,128]{1,0:T(8,128)(2,1)S(1)}, bf16[400,128]{1,0:T(8,128)(2,1)S(1)}, u32[]{:S(2)}, u32[]{:S(2)}) collective-permute-start(bf16[400,128]{1,0:T(8,128)(2,1)S(1)} %get-tuple-element.17.token.left), channel_id=1, source_target_pairs={{0,16},{8,24},{16,0},{24,8},{1,17},{9,25},{17,1},{25,9},{2,18},{10... | collective-permute-start | bytes 307208 | tf_op jit(solution)/shard_map/ppermute | solution.py:463
  12.1 3.7 %collective-permute-start.2 = (s32[6,512]{1,0:T(8,128)S(1)}, s32[6,512]{1,0:T(8,128)S(1)}, u32[]{:S(2)}, u32[]{:S(2)}) collective-permute-start(s32[6,512]{1,0:T(8,128)S(1)} %get-tuple-element.25), channel_id=1, source_target_pairs={{1,0},{0,1},{3,2},{2,3},{5,4},{4,5},{7,6},{6,7},{10,8},{11,9},{8,1... | collective-permute-start | bytes 36872 | tf_op jit(solution)/shard_map/ppermute | solution.py:391
  16.6 1.4 %collective-permute-start.3 = (bf16[400,128]{1,0:T(8,128)(2,1)S(1)}, bf16[400,128]{1,0:T(8,128)(2,1)S(1)}, u32[]{:S(2)}, u32[]{:S(2)}) collective-permute-start(bf16[400,128]{1,0:T(8,128)(2,1)S(1)} %fold.1.refs_4_), channel_id=1, source_target_pairs={{0,8},{8,0},{16,24},{24,16},{1,9},{9,1},{17,25},{25,17},{2,10},{10... | collective-permute-start | bytes 307208 | tf_op jit(solution)/shard_map/ppermute | solution.py:472
  18.0 15.7 %copy-start = (bf16[256,64]{0,1:T(8,128)(2,1)S(1)}, bf16[256,64]{0,1:T(8,128)(2,1)}, u32[]{:S(2)}) copy-start(bf16[256,64]{0,1:T(8,128)(2,1)} %param.16) | copy-start | bytes 98308
  18.0 15.7 %copy-start.1 = (bf16[64,256]{1,0:T(8,128)(2,1)S(1)}, bf16[64,256]{1,0:T(8,128)(2,1)}, u32[]{:S(2)}) copy-start(bf16[64,256]{1,0:T(8,128)(2,1)} %down.1) | copy-start | bytes 98308
  18.0 15.7 %copy-start.3 = (f32[64]{0:T(128)S(1)}, f32[64]{0:T(128)}, u32[]{:S(2)}) copy-start(f32[64]{0:T(128)} %param.15) | copy-start | bytes 772

commit v6 on v5

--- a/solution.py
+++ b/solution.py
@@ -71,7 +71,7 @@
 
 
 def spread(scr, row):
-    pieces = [jnp.broadcast_to(scr[row + k : row + k + 1, :], (8, LANES)) for k in range(SPAN)]
+    pieces = [scr[pl.ds(row + k, 8, stride=0), :] for k in range(SPAN)]
     return jnp.concatenate(pieces, 1)
 
 
@@ -152,8 +152,11 @@
         full[288:304, :] = (iota((16, size), 0) == 0).astype(f32).astype(bf16)
     odd = (group % 2) == 1
     copies[0].wait()
-    own = exact_dot(choose(group, GROUP), table[...], 1, 1)
-    columns = [jnp.broadcast_to(own[:, s : s + 1], (8, LANES * SPAN)) for s in range(NSPEC)]
+    mask = iota((8, 64), 1) == group * GROUP + iota((8, 64), 0)
+    columns = []
+    for s in range(NSPEC):
+        own = jnp.sum(jnp.where(mask, table[s : s + 1, :], 0.0), axis=1, keepdims=True)
+        columns.append(jnp.broadcast_to(own, (8, LANES * SPAN)))
 
     def step(p, j):
         here = pl.multiple_of(j * CHUNK, CHUNK)

time: 35.4 us -> 35.3 us (level)
  no operation moved by 1% of the time
where the time goes in v6:
time: 35.3 us; the launch traced here: 35.1 us
  blocking collectives  12.4 us (35%)
  Pallas kernels  11.9 us (34%)
  starting transfers between devices  7.18 us (20%)
  waiting for transfers between devices  3.52 us (10%)
    all_to_all x1, blocking collectives, body(): lax.all_to_all(message, 'ka', 0, 0, axis_index_groups=groups, tiled=True)  12.4 us
    ppermute x2, starting transfers between devices, exchange(): return lax.ppermute(value, ('atom', 'ka'), pairs)  6.57 us
    pallas_call x1, Pallas kernels, body(): pl.pallas_call(functools.partial(factor_kernel, ka_split), in_specs=[hbm]...  6.09 us
    pallas_call x1, Pallas kernels, body(): pl.pallas_call(functools.partial(back_kernel, min(512, local_count)), in_...  3.25 us
    ppermute x2, waiting for transfers between devices, exchange(): return lax.ppermute(value, ('atom', 'ka'), pairs)  2.22 us
    pallas_call x1, Pallas kernels, body(): pl.pallas_call(functools.partial(update_kernel, local_count), in_specs=[w...  1.55 us
    ppermute x1, waiting for transfers between devices, body(): lax.ppermute(payload, 'atom', [(a, a ^ 1) for a in range(4)])  0.86 us
  transfers between devices with their start and end apart: 4, of which 3 were waited for; matrix products, arithmetic and copies ran while one was open for 0% of the time, Pallas kernels for 19%

profile of v6, /device:TPU:0, one launch (start us, length us, event | category | flops | bytes accessed | tf_op | source)
XLA Modules:
  0.0 35.1 jit_solution(10824471745022517524)
XLA Ops:
  0.0 5.0 %collective-permute-start = (s32[3,512]{1,0:T(4,128)}, s32[3,512]{1,0:T(4,128)S(1)}, u32[]{:S(2)}, u32[]{:S(2)}) collective-permute-start(s32[3,512]{1,0:T(4,128)} %own.1), channel_id=1, source_target_pairs={{6,0},{7,1},{4,2},{5,3},{2,4},{3,5},{0,6},{1,7},{11,8},{10,9},{9,1... | collective-permute-start | bytes 18440 | tf_op jit(solution)/shard_map/ppermute | solution.py:394
  5.0 0.0 copy-start.2
  5.1 0.0 copy-start.4
  5.1 6.1 %factors.1 = (f32[16,16384]{1,0:T(8,128)S(1)}, f32[304,144]{1,0:T(8,128)S(1)}, bf16[64,2048]{1,0:T(8,128)(2,1)S(1)}, bf16[304,4096]{1,0:T(8,128)(2,1)S(1)}, bf16...) custom-call(f32[3,16384]{1,0:T(4,128)} %pos_hbm.1, ...), custom_call_target="tpu_custom_call" | custom-call | flops 5000000000 | bytes 14000000 | tf_op jit(solution)/shard_map/factors/pallas_call | solution.py:411
  11.1 0.0 collective-permute-done.refs_0_
  11.2 0.0 copy-done.2
  11.2 0.3 pack.1
  11.5 0.5 %collective-permute-start.1 = (bf16[400,128]{1,0:T(8,128)(2,1)S(1)}, bf16[400,128]{1,0:T(8,128)(2,1)S(1)}, u32[]{:S(2)}, u32[]{:S(2)}) collective-permute-start(bf16[400,128]{1,0:T(8,128)(2,1)S(1)} %get-tuple-element.17.token.left), channel_id=1, source_target_pairs={{0,16},{8,24},{16,0},{24,8},{1,17},{9,25},{17,1},{25,9},{2,18},{10... | collective-permute-start | bytes 307208 | tf_op jit(solution)/shard_map/ppermute | solution.py:466
  12.0 1.5 %collective-permute-start.2 = (s32[6,512]{1,0:T(8,128)S(1)}, s32[6,512]{1,0:T(8,128)S(1)}, u32[]{:S(2)}, u32[]{:S(2)}) collective-permute-start(s32[6,512]{1,0:T(8,128)S(1)} %get-tuple-element.25), channel_id=1, source_target_pairs={{1,0},{0,1},{3,2},{2,3},{5,4},{4,5},{7,6},{6,7},{10,8},{11,9},{8,1... | collective-permute-start | bytes 36872 | tf_op jit(solution)/shard_map/ppermute | solution.py:394
  13.6 2.2 %collective-permute-done.2.pair = s32[6,512]{1,0:T(8,128)S(1)} collective-permute-done((s32[6,512]{1,0:T(8,128)S(1)}, s32[6,512]{1,0:T(8,128)S(1)}, u32[]{:S(2)}, u32[]{:S(2)}) %collective-permute-start.2) | collective-permute-done | bytes 12320 | tf_op jit(solution)/shard_map/ppermute | solution.py:394
  15.8 0.4 %collective-permute-done.1.right = bf16[400,128]{1,0:T(8,128)(2,1)S(1)} collective-permute-done((bf16[400,128]{1,0:T(8,128)(2,1)S(1)}, bf16[400,128]{1,0:T(8,128)(2,1)S(1)}, u32[]{:S(2)}, u32[]{:S(2)}) %collective-permute-start.1) | collective-permute-done | bytes 102432 | tf_op jit(solution)/shard_map/ppermute | solution.py:466
  16.2 0.3 fold.1.refs_4_
  16.5 0.1 collective-permute-start.3
  16.6 0.0 copy-done.4
  16.6 0.4 %tables.1 = (f32[152,128]{1,0:T(8,128)S(1)}, f32[8,256]{1,0:T(8,128)S(1)}) custom-call(f32[16,64]{1,0:T(8,128)S(1)} %bitcast.7, bf16[400,128]{1,0:T(8,128)(2,1)S(1)} %get-tuple-element.17.token.left), custom_call_target="tpu_custom_call" | custom-call | flops 1000000000 | bytes 1000000 | tf_op jit(solution)/shard_map/tables/pallas_call | solution.py:453
  17.0 0.9 %collective-permute-done.3.refs_5_ = bf16[400,128]{1,0:T(8,128)(2,1)S(1)} collective-permute-done((bf16[400,128]{1,0:T(8,128)(2,1)S(1)}, bf16[400,128]{1,0:T(8,128)(2,1)S(1)}, u32[]{:S(2)}, u32[]{:S(2)}) %collective-permute-start.3) | collective-permute-done | bytes 102432 | tf_op jit(solution)/shard_map/ppermute | solution.py:475
  17.9 0.0 copy-start
  17.9 0.0 copy-start.1
  17.9 3.3 %back.1 = bf16[8,8,2048]{2,1,0:T(8,128)(2,1)S(1)} custom-call(f32[152,128]{1,0:T(8,128)S(1)} %get-tuple-element.18.radial, f32[8,256]{1,0:T(8,128)S(1)} %get-tuple-element.19.flat, f32[16,16384]{1,0:T(8,128)S(1)} %get-tuple-element.20.z, bf16[304,4096]{1,0:T(8,128)(2,1)S(1)} %get-tuple-element.21.refs_0_, bf16[304,4096]{1,0:T(8,128)(2,1)S(1)} %get-tuple-element.22.refs_1_, ...), custom_call_target="tpu_custom_call" | custom-call | flops 5000000000 | bytes 11000000 | tf_op jit(solution)/shard_map/back/pallas_call | solution.py:479
  21.2 12.4 %all_to_all.5.message = bf16[8,8,2048]{2,1,0:T(8,128)(2,1)S(1)} all-to-all(bf16[8,8,2048]{2,1,0:T(8,128)(2,1)S(1)} %back.1), channel_id=1, replica_groups=mesh['atom'=4,'ka'=8] {'ka'}, dimensions={0} | all-to-all | bytes 524288 | tf_op jit(solution)/shard_map/all_to_all | solution.py:495
  33.6 0.0 copy-done
  33.6 0.0 copy-done.1
  33.6 0.0 copy-done.3
  33.6 1.6 %update.1 = bf16[64,2048]{1,0:T(8,128)(2,1)} custom-call(bf16[8,8,2048]{2,1,0:T(8,128)(2,1)S(1)} %all_to_all.5.message, bf16[64,2048]{1,0:T(8,128)(2,1)S(1)} %get-tuple-element.26.feat, f32[1,64]{1,0:T(1,128)S(1)} %bitcast.6, bf16[64,256]{1,0:T(8,128)(2,1)S(1)} %bitcast.5, bf16[64,256]{1,0:T(8,128)(2,1)S(1)} %copy-done.1), custom_call_target="tpu_custom_call" | custom-call | tf_op jit(solution)/shard_map/update/pallas_call | solution.py:497
  (1 shorter events, 0.0 us)
Async XLA Ops:
  0.0 11.2 %collective-permute-start = (s32[3,512]{1,0:T(4,128)}, s32[3,512]{1,0:T(4,128)S(1)}, u32[]{:S(2)}, u32[]{:S(2)}) collective-permute-start(s32[3,512]{1,0:T(4,128)} %own.1), channel_id=1, source_target_pairs={{6,0},{7,1},{4,2},{5,3},{2,4},{3,5},{0,6},{1,7},{11,8},{10,9},{9,1... | collective-permute-start | bytes 18440 | tf_op jit(solution)/shard_map/ppermute | solution.py:394
  5.0 6.1 %copy-start.2 = (s32[3,512]{1,0:T(4,128)S(1)}, s32[3,512]{1,0:T(4,128)}, u32[]{:S(2)}) copy-start(s32[3,512]{1,0:T(4,128)} %own.1) | copy-start | bytes 18436
  5.1 11.5 %copy-start.4 = (f32[64,16]{0,1:T(8,128)S(1)}, f32[64,16]{0,1:T(8,128)}, u32[]{:S(2)}) copy-start(f32[64,16]{0,1:T(8,128)} %param.14) | copy-start | bytes 12292
  11.5 4.7 %collective-permute-start.1 = (bf16[400,128]{1,0:T(8,128)(2,1)S(1)}, bf16[400,128]{1,0:T(8,128)(2,1)S(1)}, u32[]{:S(2)}, u32[]{:S(2)}) collective-permute-start(bf16[400,128]{1,0:T(8,128)(2,1)S(1)} %get-tuple-element.17.token.left), channel_id=1, source_target_pairs={{0,16},{8,24},{16,0},{24,8},{1,17},{9,25},{17,1},{25,9},{2,18},{10... | collective-permute-start | bytes 307208 | tf_op jit(solution)/shard_map/ppermute | solution.py:466
  12.0 3.7 %collective-permute-start.2 = (s32[6,512]{1,0:T(8,128)S(1)}, s32[6,512]{1,0:T(8,128)S(1)}, u32[]{:S(2)}, u32[]{:S(2)}) collective-permute-start(s32[6,512]{1,0:T(8,128)S(1)} %get-tuple-element.25), channel_id=1, source_target_pairs={{1,0},{0,1},{3,2},{2,3},{5,4},{4,5},{7,6},{6,7},{10,8},{11,9},{8,1... | collective-permute-start | bytes 36872 | tf_op jit(solution)/shard_map/ppermute | solution.py:394
  16.5 1.4 %collective-permute-start.3 = (bf16[400,128]{1,0:T(8,128)(2,1)S(1)}, bf16[400,128]{1,0:T(8,128)(2,1)S(1)}, u32[]{:S(2)}, u32[]{:S(2)}) collective-permute-start(bf16[400,128]{1,0:T(8,128)(2,1)S(1)} %fold.1.refs_4_), channel_id=1, source_target_pairs={{0,8},{8,0},{16,24},{24,16},{1,9},{9,1},{17,25},{25,17},{2,10},{10... | collective-permute-start | bytes 307208 | tf_op jit(solution)/shard_map/ppermute | solution.py:475
  17.9 15.7 %copy-start = (bf16[256,64]{0,1:T(8,128)(2,1)S(1)}, bf16[256,64]{0,1:T(8,128)(2,1)}, u32[]{:S(2)}) copy-start(bf16[256,64]{0,1:T(8,128)(2,1)} %param.16) | copy-start | bytes 98308
  17.9 15.7 %copy-start.1 = (bf16[64,256]{1,0:T(8,128)(2,1)S(1)}, bf16[64,256]{1,0:T(8,128)(2,1)}, u32[]{:S(2)}) copy-start(bf16[64,256]{1,0:T(8,128)(2,1)} %down.1) | copy-start | bytes 98308
  17.9 15.7 %copy-start.3 = (f32[64]{0:T(128)S(1)}, f32[64]{0:T(128)}, u32[]{:S(2)}) copy-start(f32[64]{0:T(128)} %param.15) | copy-start | bytes 772

commit v7 on v6

--- a/solution.py
+++ b/solution.py
@@ -424,9 +424,9 @@
             pltpu.VMEM((1, atoms_here), jnp.int32),
             pltpu.VMEM((NSPEC, channels), f32),
             pltpu.VMEM((144, atoms_here), bf16),
-            pltpu.VMEM((LANES, LANES), f32),
-            pltpu.VMEM((LANES, LANES), f32),
-            pltpu.VMEM((LANES, LANES), f32),
+            pltpu.VMEM((LANES + 8, LANES), f32),
+            pltpu.VMEM((LANES + 8, LANES), f32),
+            pltpu.VMEM((LANES + 8, LANES), f32),
             pltpu.SemaphoreType.DMA((2 + 3 * PARTS,)),
         ],
         compiler_params=params,

time: 35.3 us -> 35.3 us (level)
  no operation moved by 1% of the time
where the time goes in v7:
time: 35.3 us; the launch traced here: 35.1 us
  blocking collectives  12.4 us (35%)
  Pallas kernels  11.9 us (34%)
  starting transfers between devices  7.18 us (20%)
  waiting for transfers between devices  3.52 us (10%)
    all_to_all x1, blocking collectives, body(): lax.all_to_all(message, 'ka', 0, 0, axis_index_groups=groups, tiled=True)  12.4 us
    ppermute x2, starting transfers between devices, exchange(): return lax.ppermute(value, ('atom', 'ka'), pairs)  6.57 us
    pallas_call x1, Pallas kernels, body(): pl.pallas_call(functools.partial(factor_kernel, ka_split), in_specs=[hbm]...  6.07 us
    pallas_call x1, Pallas kernels, body(): pl.pallas_call(functools.partial(back_kernel, min(512, local_count)), in_...  3.25 us
    ppermute x2, waiting for transfers between devices, exchange(): return lax.ppermute(value, ('atom', 'ka'), pairs)  2.22 us
    pallas_call x1, Pallas kernels, body(): pl.pallas_call(functools.partial(update_kernel, local_count), in_specs=[w...  1.55 us
    ppermute x1, waiting for transfers between devices, body(): lax.ppermute(payload, 'atom', [(a, a ^ 1) for a in range(4)])  0.86 us
  transfers between devices with their start and end apart: 4, of which 3 were waited for; matrix products, arithmetic and copies ran while one was open for 0% of the time, Pallas kernels for 19%

profile of v7, /device:TPU:0, one launch (start us, length us, event | category | flops | bytes accessed | tf_op | source)
XLA Modules:
  0.0 35.1 jit_solution(2559324183936913806)
XLA Ops:
  0.0 5.0 %collective-permute-start = (s32[3,512]{1,0:T(4,128)}, s32[3,512]{1,0:T(4,128)S(1)}, u32[]{:S(2)}, u32[]{:S(2)}) collective-permute-start(s32[3,512]{1,0:T(4,128)} %own.1), channel_id=1, source_target_pairs={{6,0},{7,1},{4,2},{5,3},{2,4},{3,5},{0,6},{1,7},{11,8},{10,9},{9,1... | collective-permute-start | bytes 18440 | tf_op jit(solution)/shard_map/ppermute | solution.py:394
  5.0 0.0 copy-start.2
  5.1 0.0 copy-start.4
  5.1 6.1 %factors.1 = (f32[16,16384]{1,0:T(8,128)S(1)}, f32[304,144]{1,0:T(8,128)S(1)}, bf16[64,2048]{1,0:T(8,128)(2,1)S(1)}, bf16[304,4096]{1,0:T(8,128)(2,1)S(1)}, bf16...) custom-call(f32[3,16384]{1,0:T(4,128)} %pos_hbm.1, ...), custom_call_target="tpu_custom_call" | custom-call | flops 5000000000 | bytes 14000000 | tf_op jit(solution)/shard_map/factors/pallas_call | solution.py:411
  11.1 0.0 collective-permute-done.refs_0_
  11.1 0.0 copy-done.2
  11.2 0.3 pack.1
  11.5 0.5 %collective-permute-start.1 = (bf16[400,128]{1,0:T(8,128)(2,1)S(1)}, bf16[400,128]{1,0:T(8,128)(2,1)S(1)}, u32[]{:S(2)}, u32[]{:S(2)}) collective-permute-start(bf16[400,128]{1,0:T(8,128)(2,1)S(1)} %get-tuple-element.17.token.left), channel_id=1, source_target_pairs={{0,16},{8,24},{16,0},{24,8},{1,17},{9,25},{17,1},{25,9},{2,18},{10... | collective-permute-start | bytes 307208 | tf_op jit(solution)/shard_map/ppermute | solution.py:466
  12.0 1.5 %collective-permute-start.2 = (s32[6,512]{1,0:T(8,128)S(1)}, s32[6,512]{1,0:T(8,128)S(1)}, u32[]{:S(2)}, u32[]{:S(2)}) collective-permute-start(s32[6,512]{1,0:T(8,128)S(1)} %get-tuple-element.25), channel_id=1, source_target_pairs={{1,0},{0,1},{3,2},{2,3},{5,4},{4,5},{7,6},{6,7},{10,8},{11,9},{8,1... | collective-permute-start | bytes 36872 | tf_op jit(solution)/shard_map/ppermute | solution.py:394
  13.5 2.2 %collective-permute-done.2.pair = s32[6,512]{1,0:T(8,128)S(1)} collective-permute-done((s32[6,512]{1,0:T(8,128)S(1)}, s32[6,512]{1,0:T(8,128)S(1)}, u32[]{:S(2)}, u32[]{:S(2)}) %collective-permute-start.2) | collective-permute-done | bytes 12320 | tf_op jit(solution)/shard_map/ppermute | solution.py:394
  15.8 0.4 %collective-permute-done.1.right = bf16[400,128]{1,0:T(8,128)(2,1)S(1)} collective-permute-done((bf16[400,128]{1,0:T(8,128)(2,1)S(1)}, bf16[400,128]{1,0:T(8,128)(2,1)S(1)}, u32[]{:S(2)}, u32[]{:S(2)}) %collective-permute-start.1) | collective-permute-done | bytes 102432 | tf_op jit(solution)/shard_map/ppermute | solution.py:466
  16.2 0.3 fold.1.refs_4_
  16.5 0.1 collective-permute-start.3
  16.6 0.0 copy-done.4
  16.6 0.4 %tables.1 = (f32[152,128]{1,0:T(8,128)S(1)}, f32[8,256]{1,0:T(8,128)S(1)}) custom-call(f32[16,64]{1,0:T(8,128)S(1)} %bitcast.7, bf16[400,128]{1,0:T(8,128)(2,1)S(1)} %get-tuple-element.17.token.left), custom_call_target="tpu_custom_call" | custom-call | flops 1000000000 | bytes 1000000 | tf_op jit(solution)/shard_map/tables/pallas_call | solution.py:453
  17.0 0.9 %collective-permute-done.3.refs_5_ = bf16[400,128]{1,0:T(8,128)(2,1)S(1)} collective-permute-done((bf16[400,128]{1,0:T(8,128)(2,1)S(1)}, bf16[400,128]{1,0:T(8,128)(2,1)S(1)}, u32[]{:S(2)}, u32[]{:S(2)}) %collective-permute-start.3) | collective-permute-done | bytes 102432 | tf_op jit(solution)/shard_map/ppermute | solution.py:475
  17.9 0.0 copy-start
  17.9 0.0 copy-start.1
  17.9 3.3 %back.1 = bf16[8,8,2048]{2,1,0:T(8,128)(2,1)S(1)} custom-call(f32[152,128]{1,0:T(8,128)S(1)} %get-tuple-element.18.radial, f32[8,256]{1,0:T(8,128)S(1)} %get-tuple-element.19.flat, f32[16,16384]{1,0:T(8,128)S(1)} %get-tuple-element.20.z, bf16[304,4096]{1,0:T(8,128)(2,1)S(1)} %get-tuple-element.21.refs_0_, bf16[304,4096]{1,0:T(8,128)(2,1)S(1)} %get-tuple-element.22.refs_1_, ...), custom_call_target="tpu_custom_call" | custom-call | flops 5000000000 | bytes 11000000 | tf_op jit(solution)/shard_map/back/pallas_call | solution.py:479
  21.1 12.4 %all_to_all.5.message = bf16[8,8,2048]{2,1,0:T(8,128)(2,1)S(1)} all-to-all(bf16[8,8,2048]{2,1,0:T(8,128)(2,1)S(1)} %back.1), channel_id=1, replica_groups=mesh['atom'=4,'ka'=8] {'ka'}, dimensions={0} | all-to-all | bytes 524288 | tf_op jit(solution)/shard_map/all_to_all | solution.py:495
  33.5 0.0 copy-done
  33.5 0.0 copy-done.1
  33.5 0.0 copy-done.3
  33.6 1.6 %update.1 = bf16[64,2048]{1,0:T(8,128)(2,1)} custom-call(bf16[8,8,2048]{2,1,0:T(8,128)(2,1)S(1)} %all_to_all.5.message, bf16[64,2048]{1,0:T(8,128)(2,1)S(1)} %get-tuple-element.26.feat, f32[1,64]{1,0:T(1,128)S(1)} %bitcast.6, bf16[64,256]{1,0:T(8,128)(2,1)S(1)} %bitcast.5, bf16[64,256]{1,0:T(8,128)(2,1)S(1)} %copy-done.1), custom_call_target="tpu_custom_call" | custom-call | tf_op jit(solution)/shard_map/update/pallas_call | solution.py:497
  (1 shorter events, 0.0 us)
Async XLA Ops:
  0.0 11.1 %collective-permute-start = (s32[3,512]{1,0:T(4,128)}, s32[3,512]{1,0:T(4,128)S(1)}, u32[]{:S(2)}, u32[]{:S(2)}) collective-permute-start(s32[3,512]{1,0:T(4,128)} %own.1), channel_id=1, source_target_pairs={{6,0},{7,1},{4,2},{5,3},{2,4},{3,5},{0,6},{1,7},{11,8},{10,9},{9,1... | collective-permute-start | bytes 18440 | tf_op jit(solution)/shard_map/ppermute | solution.py:394
  5.0 6.1 %copy-start.2 = (s32[3,512]{1,0:T(4,128)S(1)}, s32[3,512]{1,0:T(4,128)}, u32[]{:S(2)}) copy-start(s32[3,512]{1,0:T(4,128)} %own.1) | copy-start | bytes 18436
  5.1 11.5 %copy-start.4 = (f32[64,16]{0,1:T(8,128)S(1)}, f32[64,16]{0,1:T(8,128)}, u32[]{:S(2)}) copy-start(f32[64,16]{0,1:T(8,128)} %param.14) | copy-start | bytes 12292
  11.5 4.7 %collective-permute-start.1 = (bf16[400,128]{1,0:T(8,128)(2,1)S(1)}, bf16[400,128]{1,0:T(8,128)(2,1)S(1)}, u32[]{:S(2)}, u32[]{:S(2)}) collective-permute-start(bf16[400,128]{1,0:T(8,128)(2,1)S(1)} %get-tuple-element.17.token.left), channel_id=1, source_target_pairs={{0,16},{8,24},{16,0},{24,8},{1,17},{9,25},{17,1},{25,9},{2,18},{10... | collective-permute-start | bytes 307208 | tf_op jit(solution)/shard_map/ppermute | solution.py:466
  12.0 3.7 %collective-permute-start.2 = (s32[6,512]{1,0:T(8,128)S(1)}, s32[6,512]{1,0:T(8,128)S(1)}, u32[]{:S(2)}, u32[]{:S(2)}) collective-permute-start(s32[6,512]{1,0:T(8,128)S(1)} %get-tuple-element.25), channel_id=1, source_target_pairs={{1,0},{0,1},{3,2},{2,3},{5,4},{4,5},{7,6},{6,7},{10,8},{11,9},{8,1... | collective-permute-start | bytes 36872 | tf_op jit(solution)/shard_map/ppermute | solution.py:394
  16.5 1.4 %collective-permute-start.3 = (bf16[400,128]{1,0:T(8,128)(2,1)S(1)}, bf16[400,128]{1,0:T(8,128)(2,1)S(1)}, u32[]{:S(2)}, u32[]{:S(2)}) collective-permute-start(bf16[400,128]{1,0:T(8,128)(2,1)S(1)} %fold.1.refs_4_), channel_id=1, source_target_pairs={{0,8},{8,0},{16,24},{24,16},{1,9},{9,1},{17,25},{25,17},{2,10},{10... | collective-permute-start | bytes 307208 | tf_op jit(solution)/shard_map/ppermute | solution.py:475
  17.9 15.7 %copy-start = (bf16[256,64]{0,1:T(8,128)(2,1)S(1)}, bf16[256,64]{0,1:T(8,128)(2,1)}, u32[]{:S(2)}) copy-start(bf16[256,64]{0,1:T(8,128)(2,1)} %param.16) | copy-start | bytes 98308
  17.9 15.7 %copy-start.1 = (bf16[64,256]{1,0:T(8,128)(2,1)S(1)}, bf16[64,256]{1,0:T(8,128)(2,1)}, u32[]{:S(2)}) copy-start(bf16[64,256]{1,0:T(8,128)(2,1)} %down.1) | copy-start | bytes 98308
  17.9 15.7 %copy-start.3 = (f32[64]{0:T(128)S(1)}, f32[64]{0:T(128)}, u32[]{:S(2)}) copy-start(f32[64]{0:T(128)} %param.15) | copy-start | bytes 772

commit v8 on v7

--- a/solution.py
+++ b/solution.py
@@ -204,8 +204,7 @@
         (first,), (out, pair_out) = refs[:1], refs[1:]
         pair_out[0:3, :] = own[...]
         pair_out[3:6, :] = first[...]
-        at_start = jnp.where(lax.axis_index("atom") == 0, 1.0, 0.0)
-        counts = histogram(first[...]) + at_start * histogram(own[...])
+        counts = histogram(first[...])
     else:
         millers, out = refs[:-1], refs[-1]
         at_start = lax.axis_index("atom") == 0
@@ -224,12 +223,13 @@
     out[368:400, :] = counts[:, 128:256].astype(bf16)
 
 
-def fold_kernel(left, right, pair, out):
+def fold_kernel(left, right, pair, own_counts, out):
     out[0:336, :] = (left[0:336, :].astype(f32) + right[0:336, :].astype(f32)).astype(bf16)
     atom = lax.axis_index("atom")
     last = jnp.where(atom // 2 == atom % 2, 1.0, 0.0)
     extra = histogram(pair[0:3, :]) + last * histogram(pair[3:6, :])
     counts = left[336:400, :].astype(f32) + right[336:400, :].astype(f32)
+    counts = counts + jnp.where(atom % 2 == 0, 1.0, 0.0) * own_counts[...]
     out[336:400, :] = (counts + jnp.concatenate([extra[:, 0:128], extra[:, 128:256]], 0)).astype(bf16)
 
 
@@ -243,8 +243,10 @@
     return total
 
 
-def tables_kernel(ka_split, scaling, weights, token, radial_out, flat_out):
+def tables_kernel(ka_split, scaling, weights, own, token, radial_out, flat_out, counts_out):
     del token
+    counts = histogram(own[...])
+    counts_out[...] = jnp.concatenate([counts[:, 0:128], counts[:, 128:256]], 0)
     group = lax.axis_index("ka") // ka_split
     across = exact_dot(weights[...], choose(group, LANES), 1, 1)
     lane = iota((88, LANES), 1)
@@ -450,28 +452,29 @@
         compiler_params=params,
         name="pack",
     )(acc, miller, *millers[::-1])
-    radial, flat = pl.pallas_call(
+    radial, flat, own_counts = pl.pallas_call(
         functools.partial(tables_kernel, ka_split, scaling),
-        in_specs=[whole, pl.BlockSpec(memory_space=pl.ANY)],
-        out_specs=[whole, whole],
+        in_specs=[whole, whole, pl.BlockSpec(memory_space=pl.ANY)],
+        out_specs=[whole] * 3,
         out_shape=[
             jax.ShapeDtypeStruct((152, LANES), f32),
             jax.ShapeDtypeStruct((GROUP, 2 * LANES), f32),
+            jax.ShapeDtypeStruct((64, LANES), f32),
         ],
         compiler_params=params,
         cost_estimate=pl.CostEstimate(flops=10**9, bytes_accessed=10**6, transcendentals=10**6),
         name="tables",
-    )(filter_weight.T, payload)
+    )(filter_weight.T, miller, payload)
     if chained:
         across = lax.ppermute(payload, "atom", [(a, a ^ 2) for a in range(4)])
         payload = pl.pallas_call(
             fold_kernel,
-            in_specs=[whole] * 3,
+            in_specs=[whole] * 4,
             out_specs=whole,
             out_shape=jax.ShapeDtypeStruct((PAYLOAD, LANES), bf16),
             compiler_params=params,
             name="fold",
-        )(payload, across, exchange(pair[0], NEAR))
+        )(payload, across, exchange(pair[0], NEAR), own_counts)
         gathered = [payload, lax.ppermute(payload, "atom", [(a, a ^ 1) for a in range(4)])]
     else:
         gathered = list(lax.all_gather(payload, "atom"))

time: 35.3 us -> 35.2 us (level)
    ppermute x2, waiting for transfers between devices: 2.22 us -> 1.71 us  [exchange(): return lax.ppermute(value, ('atom', 'ka'), pairs)]
    ppermute x1, waiting for transfers between devices: 0.86 us -> 1.29 us  [body(): lax.ppermute(payload, 'atom', [(a, a ^ 1) for a in range(4)])]
where the time goes in v8:
time: 35.2 us; the launch traced here: 35 us
  blocking collectives  12.4 us (35%)
  Pallas kernels  11.9 us (34%)
  starting transfers between devices  7.18 us (20%)
  waiting for transfers between devices  3.45 us (10%)
    all_to_all x1, blocking collectives, body(): lax.all_to_all(message, 'ka', 0, 0, axis_index_groups=groups, tiled=True)  12.4 us
    ppermute x2, starting transfers between devices, exchange(): return lax.ppermute(value, ('atom', 'ka'), pairs)  6.57 us
    pallas_call x1, Pallas kernels, body(): pl.pallas_call(functools.partial(factor_kernel, ka_split), in_specs=[hbm]...  6.07 us
    pallas_call x1, Pallas kernels, body(): pl.pallas_call(functools.partial(back_kernel, min(512, local_count)), in_...  3.25 us
    ppermute x2, waiting for transfers between devices, exchange(): return lax.ppermute(value, ('atom', 'ka'), pairs)  1.71 us
    pallas_call x1, Pallas kernels, body(): pl.pallas_call(functools.partial(update_kernel, local_count), in_specs=[w...  1.55 us
    ppermute x1, waiting for transfers between devices, body(): lax.ppermute(payload, 'atom', [(a, a ^ 1) for a in range(4)])  1.29 us
  transfers between devices with their start and end apart: 4, of which 3 were waited for; matrix products, arithmetic and copies ran while one was open for 0% of the time, Pallas kernels for 19%

profile of v8, /device:TPU:0, one launch (start us, length us, event | category | flops | bytes accessed | tf_op | source)
XLA Modules:
  0.0 35.0 jit_solution(405647573073579934)
XLA Ops:
  0.0 5.0 %collective-permute-start = (s32[3,512]{1,0:T(4,128)}, s32[3,512]{1,0:T(4,128)S(1)}, u32[]{:S(2)}, u32[]{:S(2)}) collective-permute-start(s32[3,512]{1,0:T(4,128)} %own.3), channel_id=1, source_target_pairs={{6,0},{7,1},{4,2},{5,3},{2,4},{3,5},{0,6},{1,7},{11,8},{10,9},{9,1... | collective-permute-start | bytes 18440 | tf_op jit(solution)/shard_map/ppermute | solution.py:396
  5.0 0.0 copy-start.2
  5.1 0.0 copy-start.4
  5.1 6.1 %factors.1 = (f32[16,16384]{1,0:T(8,128)S(1)}, f32[304,144]{1,0:T(8,128)S(1)}, bf16[64,2048]{1,0:T(8,128)(2,1)S(1)}, bf16[304,4096]{1,0:T(8,128)(2,1)S(1)}, bf16...) custom-call(f32[3,16384]{1,0:T(4,128)} %pos_hbm.1, ...), custom_call_target="tpu_custom_call" | custom-call | flops 5000000000 | bytes 14000000 | tf_op jit(solution)/shard_map/factors/pallas_call | solution.py:413
  11.1 0.0 collective-permute-done.refs_0_
  11.1 0.0 copy-done.2
  11.2 0.2 pack.1
  11.4 0.5 %collective-permute-start.1 = (bf16[400,128]{1,0:T(8,128)(2,1)S(1)}, bf16[400,128]{1,0:T(8,128)(2,1)S(1)}, u32[]{:S(2)}, u32[]{:S(2)}) collective-permute-start(bf16[400,128]{1,0:T(8,128)(2,1)S(1)} %get-tuple-element.18.token.left), channel_id=1, source_target_pairs={{0,16},{8,24},{16,0},{24,8},{1,17},{9,25},{17,1},{25,9},{2,18},{10... | collective-permute-start | bytes 307208 | tf_op jit(solution)/shard_map/ppermute | solution.py:469
  11.9 1.5 %collective-permute-start.2 = (s32[6,512]{1,0:T(8,128)S(1)}, s32[6,512]{1,0:T(8,128)S(1)}, u32[]{:S(2)}, u32[]{:S(2)}) collective-permute-start(s32[6,512]{1,0:T(8,128)S(1)} %get-tuple-element.26), channel_id=1, source_target_pairs={{1,0},{0,1},{3,2},{2,3},{5,4},{4,5},{7,6},{6,7},{10,8},{11,9},{8,1... | collective-permute-start | bytes 36872 | tf_op jit(solution)/shard_map/ppermute | solution.py:396
  13.4 0.0 copy-done.4
  13.4 0.5 %tables.1 = (f32[152,128]{1,0:T(8,128)S(1)}, f32[8,256]{1,0:T(8,128)S(1)}, f32[64,128]{1,0:T(8,128)S(1)}) custom-call(f32[16,64]{1,0:T(8,128)S(1)} %bitcast.7, s32[3,512]{1,0:T(4,128)S(1)} %copy-done.2, bf16[400,128]{1,0:T(8,128)(2,1)S(1)} %get-tuple-element.18.token.left), custom_call_target="tpu_custom_call" | custom-call | flops 1000000000 | bytes 1000000 | tf_op jit(solution)/shard_map/tables/pallas_call | solution.py:455
  13.9 1.7 %collective-permute-done.2.pair = s32[6,512]{1,0:T(8,128)S(1)} collective-permute-done((s32[6,512]{1,0:T(8,128)S(1)}, s32[6,512]{1,0:T(8,128)S(1)}, u32[]{:S(2)}, u32[]{:S(2)}) %collective-permute-start.2) | collective-permute-done | bytes 12320 | tf_op jit(solution)/shard_map/ppermute | solution.py:396
  15.6 0.4 %collective-permute-done.1.right = bf16[400,128]{1,0:T(8,128)(2,1)S(1)} collective-permute-done((bf16[400,128]{1,0:T(8,128)(2,1)S(1)}, bf16[400,128]{1,0:T(8,128)(2,1)S(1)}, u32[]{:S(2)}, u32[]{:S(2)}) %collective-permute-start.1) | collective-permute-done | bytes 102432 | tf_op jit(solution)/shard_map/ppermute | solution.py:469
  16.1 0.3 fold.1.refs_4_
  16.4 0.1 collective-permute-start.3
  16.5 1.3 %collective-permute-done.3.refs_5_ = bf16[400,128]{1,0:T(8,128)(2,1)S(1)} collective-permute-done((bf16[400,128]{1,0:T(8,128)(2,1)S(1)}, bf16[400,128]{1,0:T(8,128)(2,1)S(1)}, u32[]{:S(2)}, u32[]{:S(2)}) %collective-permute-start.3) | collective-permute-done | bytes 102432 | tf_op jit(solution)/shard_map/ppermute | solution.py:478
  17.8 0.0 copy-start
  17.8 0.0 copy-start.1
  17.8 3.3 %back.1 = bf16[8,8,2048]{2,1,0:T(8,128)(2,1)S(1)} custom-call(f32[152,128]{1,0:T(8,128)S(1)} %get-tuple-element.19.radial, f32[8,256]{1,0:T(8,128)S(1)} %get-tuple-element.20.flat, f32[16,16384]{1,0:T(8,128)S(1)} %get-tuple-element.21.z, bf16[304,4096]{1,0:T(8,128)(2,1)S(1)} %get-tuple-element.22.refs_0_, bf16[304,4096]{1,0:T(8,128)(2,1)S(1)} %get-tuple-element.23.refs_1_, ...), custom_call_target="tpu_custom_call" | custom-call | flops 5000000000 | bytes 11000000 | tf_op jit(solution)/shard_map/back/pallas_call | solution.py:482
  21.0 12.4 %all_to_all.5.message = bf16[8,8,2048]{2,1,0:T(8,128)(2,1)S(1)} all-to-all(bf16[8,8,2048]{2,1,0:T(8,128)(2,1)S(1)} %back.1), channel_id=1, replica_groups=mesh['atom'=4,'ka'=8] {'ka'}, dimensions={0} | all-to-all | bytes 524288 | tf_op jit(solution)/shard_map/all_to_all | solution.py:498
  33.4 0.0 copy-done
  33.4 0.0 copy-done.1
  33.4 0.0 copy-done.3
  33.4 1.6 %update.1 = bf16[64,2048]{1,0:T(8,128)(2,1)} custom-call(bf16[8,8,2048]{2,1,0:T(8,128)(2,1)S(1)} %all_to_all.5.message, bf16[64,2048]{1,0:T(8,128)(2,1)S(1)} %get-tuple-element.28.feat, f32[1,64]{1,0:T(1,128)S(1)} %bitcast.6, bf16[64,256]{1,0:T(8,128)(2,1)S(1)} %bitcast.5, bf16[64,256]{1,0:T(8,128)(2,1)S(1)} %copy-done.1), custom_call_target="tpu_custom_call" | custom-call | tf_op jit(solution)/shard_map/update/pallas_call | solution.py:500
  (1 shorter events, 0.0 us)
Async XLA Ops:
  0.0 11.1 %collective-permute-start = (s32[3,512]{1,0:T(4,128)}, s32[3,512]{1,0:T(4,128)S(1)}, u32[]{:S(2)}, u32[]{:S(2)}) collective-permute-start(s32[3,512]{1,0:T(4,128)} %own.3), channel_id=1, source_target_pairs={{6,0},{7,1},{4,2},{5,3},{2,4},{3,5},{0,6},{1,7},{11,8},{10,9},{9,1... | collective-permute-start | bytes 18440 | tf_op jit(solution)/shard_map/ppermute | solution.py:396
  5.0 6.1 %copy-start.2 = (s32[3,512]{1,0:T(4,128)S(1)}, s32[3,512]{1,0:T(4,128)}, u32[]{:S(2)}) copy-start(s32[3,512]{1,0:T(4,128)} %own.3) | copy-start | bytes 18436
  5.1 8.4 %copy-start.4 = (f32[64,16]{0,1:T(8,128)S(1)}, f32[64,16]{0,1:T(8,128)}, u32[]{:S(2)}) copy-start(f32[64,16]{0,1:T(8,128)} %param.14) | copy-start | bytes 12292
  11.4 4.7 %collective-permute-start.1 = (bf16[400,128]{1,0:T(8,128)(2,1)S(1)}, bf16[400,128]{1,0:T(8,128)(2,1)S(1)}, u32[]{:S(2)}, u32[]{:S(2)}) collective-permute-start(bf16[400,128]{1,0:T(8,128)(2,1)S(1)} %get-tuple-element.18.token.left), channel_id=1, source_target_pairs={{0,16},{8,24},{16,0},{24,8},{1,17},{9,25},{17,1},{25,9},{2,18},{10... | collective-permute-start | bytes 307208 | tf_op jit(solution)/shard_map/ppermute | solution.py:469
  11.9 3.7 %collective-permute-start.2 = (s32[6,512]{1,0:T(8,128)S(1)}, s32[6,512]{1,0:T(8,128)S(1)}, u32[]{:S(2)}, u32[]{:S(2)}) collective-permute-start(s32[6,512]{1,0:T(8,128)S(1)} %get-tuple-element.26), channel_id=1, source_target_pairs={{1,0},{0,1},{3,2},{2,3},{5,4},{4,5},{7,6},{6,7},{10,8},{11,9},{8,1... | collective-permute-start | bytes 36872 | tf_op jit(solution)/shard_map/ppermute | solution.py:396
  16.4 1.4 %collective-permute-start.3 = (bf16[400,128]{1,0:T(8,128)(2,1)S(1)}, bf16[400,128]{1,0:T(8,128)(2,1)S(1)}, u32[]{:S(2)}, u32[]{:S(2)}) collective-permute-start(bf16[400,128]{1,0:T(8,128)(2,1)S(1)} %fold.1.refs_4_), channel_id=1, source_target_pairs={{0,8},{8,0},{16,24},{24,16},{1,9},{9,1},{17,25},{25,17},{2,10},{10... | collective-permute-start | bytes 307208 | tf_op jit(solution)/shard_map/ppermute | solution.py:478
  17.8 15.7 %copy-start = (bf16[256,64]{0,1:T(8,128)(2,1)S(1)}, bf16[256,64]{0,1:T(8,128)(2,1)}, u32[]{:S(2)}) copy-start(bf16[256,64]{0,1:T(8,128)(2,1)} %param.16) | copy-start | bytes 98308
  17.8 15.7 %copy-start.1 = (bf16[64,256]{1,0:T(8,128)(2,1)S(1)}, bf16[64,256]{1,0:T(8,128)(2,1)}, u32[]{:S(2)}) copy-start(bf16[64,256]{1,0:T(8,128)(2,1)} %down.1) | copy-start | bytes 98308
  17.8 15.7 %copy-start.3 = (f32[64]{0:T(128)S(1)}, f32[64]{0:T(128)}, u32[]{:S(2)}) copy-start(f32[64]{0:T(128)} %param.15) | copy-start | bytes 772

commit v9 on v8

--- a/solution.py
+++ b/solution.py
@@ -37,7 +37,7 @@
     return [float(v) for v in series.convert(kind=np.polynomial.Polynomial).coef]
 
 
-SIN = fit(np.sin, 7, True)
+SIN = fit(np.sin, 6, True)
 COS = fit(np.cos, 7, False)
 
 

time: 35.2 us -> 35.2 us (level)
  no operation moved by 1% of the time
where the time goes in v9:
time: 35.2 us; the launch traced here: 35 us
  blocking collectives  12.4 us (35%)
  Pallas kernels  11.9 us (34%)
  starting transfers between devices  7.18 us (20%)
  waiting for transfers between devices  3.45 us (10%)
    all_to_all x1, blocking collectives, body(): lax.all_to_all(message, 'ka', 0, 0, axis_index_groups=groups, tiled=True)  12.4 us
    ppermute x2, starting transfers between devices, exchange(): return lax.ppermute(value, ('atom', 'ka'), pairs)  6.57 us
    pallas_call x1, Pallas kernels, body(): pl.pallas_call(functools.partial(factor_kernel, ka_split), in_specs=[hbm]...  6.1 us
    pallas_call x1, Pallas kernels, body(): pl.pallas_call(functools.partial(back_kernel, min(512, local_count)), in_...  3.25 us
    ppermute x2, waiting for transfers between devices, exchange(): return lax.ppermute(value, ('atom', 'ka'), pairs)  1.71 us
    pallas_call x1, Pallas kernels, body(): pl.pallas_call(functools.partial(update_kernel, local_count), in_specs=[w...  1.55 us
    ppermute x1, waiting for transfers between devices, body(): lax.ppermute(payload, 'atom', [(a, a ^ 1) for a in range(4)])  1.29 us
  transfers between devices with their start and end apart: 4, of which 3 were waited for; matrix products, arithmetic and copies ran while one was open for 0% of the time, Pallas kernels for 19%

profile of v9, /device:TPU:0, one launch (start us, length us, event | category | flops | bytes accessed | tf_op | source)
XLA Modules:
  0.0 35.0 jit_solution(15845524623072381420)
XLA Ops:
  0.0 5.0 %collective-permute-start = (s32[3,512]{1,0:T(4,128)}, s32[3,512]{1,0:T(4,128)S(1)}, u32[]{:S(2)}, u32[]{:S(2)}) collective-permute-start(s32[3,512]{1,0:T(4,128)} %own.3), channel_id=1, source_target_pairs={{6,0},{7,1},{4,2},{5,3},{2,4},{3,5},{0,6},{1,7},{11,8},{10,9},{9,1... | collective-permute-start | bytes 18440 | tf_op jit(solution)/shard_map/ppermute | solution.py:396
  5.0 0.0 copy-start.2
  5.1 0.0 copy-start.4
  5.1 6.1 %factors.1 = (f32[16,16384]{1,0:T(8,128)S(1)}, f32[304,144]{1,0:T(8,128)S(1)}, bf16[64,2048]{1,0:T(8,128)(2,1)S(1)}, bf16[304,4096]{1,0:T(8,128)(2,1)S(1)}, bf16...) custom-call(f32[3,16384]{1,0:T(4,128)} %pos_hbm.1, ...), custom_call_target="tpu_custom_call" | custom-call | flops 5000000000 | bytes 14000000 | tf_op jit(solution)/shard_map/factors/pallas_call | solution.py:413
  11.2 0.0 collective-permute-done.refs_0_
  11.2 0.0 copy-done.2
  11.2 0.2 pack.1
  11.4 0.5 %collective-permute-start.1 = (bf16[400,128]{1,0:T(8,128)(2,1)S(1)}, bf16[400,128]{1,0:T(8,128)(2,1)S(1)}, u32[]{:S(2)}, u32[]{:S(2)}) collective-permute-start(bf16[400,128]{1,0:T(8,128)(2,1)S(1)} %get-tuple-element.18.token.left), channel_id=1, source_target_pairs={{0,16},{8,24},{16,0},{24,8},{1,17},{9,25},{17,1},{25,9},{2,18},{10... | collective-permute-start | bytes 307208 | tf_op jit(solution)/shard_map/ppermute | solution.py:469
  11.9 1.5 %collective-permute-start.2 = (s32[6,512]{1,0:T(8,128)S(1)}, s32[6,512]{1,0:T(8,128)S(1)}, u32[]{:S(2)}, u32[]{:S(2)}) collective-permute-start(s32[6,512]{1,0:T(8,128)S(1)} %get-tuple-element.26), channel_id=1, source_target_pairs={{1,0},{0,1},{3,2},{2,3},{5,4},{4,5},{7,6},{6,7},{10,8},{11,9},{8,1... | collective-permute-start | bytes 36872 | tf_op jit(solution)/shard_map/ppermute | solution.py:396
  13.5 0.0 copy-done.4
  13.5 0.5 %tables.1 = (f32[152,128]{1,0:T(8,128)S(1)}, f32[8,256]{1,0:T(8,128)S(1)}, f32[64,128]{1,0:T(8,128)S(1)}) custom-call(f32[16,64]{1,0:T(8,128)S(1)} %bitcast.7, s32[3,512]{1,0:T(4,128)S(1)} %copy-done.2, bf16[400,128]{1,0:T(8,128)(2,1)S(1)} %get-tuple-element.18.token.left), custom_call_target="tpu_custom_call" | custom-call | flops 1000000000 | bytes 1000000 | tf_op jit(solution)/shard_map/tables/pallas_call | solution.py:455
  14.0 1.7 %collective-permute-done.2.pair = s32[6,512]{1,0:T(8,128)S(1)} collective-permute-done((s32[6,512]{1,0:T(8,128)S(1)}, s32[6,512]{1,0:T(8,128)S(1)}, u32[]{:S(2)}, u32[]{:S(2)}) %collective-permute-start.2) | collective-permute-done | bytes 12320 | tf_op jit(solution)/shard_map/ppermute | solution.py:396
  15.7 0.4 %collective-permute-done.1.right = bf16[400,128]{1,0:T(8,128)(2,1)S(1)} collective-permute-done((bf16[400,128]{1,0:T(8,128)(2,1)S(1)}, bf16[400,128]{1,0:T(8,128)(2,1)S(1)}, u32[]{:S(2)}, u32[]{:S(2)}) %collective-permute-start.1) | collective-permute-done | bytes 102432 | tf_op jit(solution)/shard_map/ppermute | solution.py:469
  16.1 0.3 fold.1.refs_4_
  16.4 0.1 collective-permute-start.3
  16.5 1.3 %collective-permute-done.3.refs_5_ = bf16[400,128]{1,0:T(8,128)(2,1)S(1)} collective-permute-done((bf16[400,128]{1,0:T(8,128)(2,1)S(1)}, bf16[400,128]{1,0:T(8,128)(2,1)S(1)}, u32[]{:S(2)}, u32[]{:S(2)}) %collective-permute-start.3) | collective-permute-done | bytes 102432 | tf_op jit(solution)/shard_map/ppermute | solution.py:478
  17.8 0.0 copy-start
  17.8 0.0 copy-start.1
  17.8 3.3 %back.1 = bf16[8,8,2048]{2,1,0:T(8,128)(2,1)S(1)} custom-call(f32[152,128]{1,0:T(8,128)S(1)} %get-tuple-element.19.radial, f32[8,256]{1,0:T(8,128)S(1)} %get-tuple-element.20.flat, f32[16,16384]{1,0:T(8,128)S(1)} %get-tuple-element.21.z, bf16[304,4096]{1,0:T(8,128)(2,1)S(1)} %get-tuple-element.22.refs_0_, bf16[304,4096]{1,0:T(8,128)(2,1)S(1)} %get-tuple-element.23.refs_1_, ...), custom_call_target="tpu_custom_call" | custom-call | flops 5000000000 | bytes 11000000 | tf_op jit(solution)/shard_map/back/pallas_call | solution.py:482
  21.1 12.4 %all_to_all.5.message = bf16[8,8,2048]{2,1,0:T(8,128)(2,1)S(1)} all-to-all(bf16[8,8,2048]{2,1,0:T(8,128)(2,1)S(1)} %back.1), channel_id=1, replica_groups=mesh['atom'=4,'ka'=8] {'ka'}, dimensions={0} | all-to-all | bytes 524288 | tf_op jit(solution)/shard_map/all_to_all | solution.py:498
  33.4 0.0 copy-done
  33.5 0.0 copy-done.1
  33.5 0.0 copy-done.3
  33.5 1.6 %update.1 = bf16[64,2048]{1,0:T(8,128)(2,1)} custom-call(bf16[8,8,2048]{2,1,0:T(8,128)(2,1)S(1)} %all_to_all.5.message, bf16[64,2048]{1,0:T(8,128)(2,1)S(1)} %get-tuple-element.28.feat, f32[1,64]{1,0:T(1,128)S(1)} %bitcast.6, bf16[64,256]{1,0:T(8,128)(2,1)S(1)} %bitcast.5, bf16[64,256]{1,0:T(8,128)(2,1)S(1)} %copy-done.1), custom_call_target="tpu_custom_call" | custom-call | tf_op jit(solution)/shard_map/update/pallas_call | solution.py:500
  (1 shorter events, 0.0 us)
Async XLA Ops:
  0.0 11.2 %collective-permute-start = (s32[3,512]{1,0:T(4,128)}, s32[3,512]{1,0:T(4,128)S(1)}, u32[]{:S(2)}, u32[]{:S(2)}) collective-permute-start(s32[3,512]{1,0:T(4,128)} %own.3), channel_id=1, source_target_pairs={{6,0},{7,1},{4,2},{5,3},{2,4},{3,5},{0,6},{1,7},{11,8},{10,9},{9,1... | collective-permute-start | bytes 18440 | tf_op jit(solution)/shard_map/ppermute | solution.py:396
  5.0 6.1 %copy-start.2 = (s32[3,512]{1,0:T(4,128)S(1)}, s32[3,512]{1,0:T(4,128)}, u32[]{:S(2)}) copy-start(s32[3,512]{1,0:T(4,128)} %own.3) | copy-start | bytes 18436
  5.1 8.4 %copy-start.4 = (f32[64,16]{0,1:T(8,128)S(1)}, f32[64,16]{0,1:T(8,128)}, u32[]{:S(2)}) copy-start(f32[64,16]{0,1:T(8,128)} %param.14) | copy-start | bytes 12292
  11.4 4.7 %collective-permute-start.1 = (bf16[400,128]{1,0:T(8,128)(2,1)S(1)}, bf16[400,128]{1,0:T(8,128)(2,1)S(1)}, u32[]{:S(2)}, u32[]{:S(2)}) collective-permute-start(bf16[400,128]{1,0:T(8,128)(2,1)S(1)} %get-tuple-element.18.token.left), channel_id=1, source_target_pairs={{0,16},{8,24},{16,0},{24,8},{1,17},{9,25},{17,1},{25,9},{2,18},{10... | collective-permute-start | bytes 307208 | tf_op jit(solution)/shard_map/ppermute | solution.py:469
  11.9 3.7 %collective-permute-start.2 = (s32[6,512]{1,0:T(8,128)S(1)}, s32[6,512]{1,0:T(8,128)S(1)}, u32[]{:S(2)}, u32[]{:S(2)}) collective-permute-start(s32[6,512]{1,0:T(8,128)S(1)} %get-tuple-element.26), channel_id=1, source_target_pairs={{1,0},{0,1},{3,2},{2,3},{5,4},{4,5},{7,6},{6,7},{10,8},{11,9},{8,1... | collective-permute-start | bytes 36872 | tf_op jit(solution)/shard_map/ppermute | solution.py:396
  16.4 1.4 %collective-permute-start.3 = (bf16[400,128]{1,0:T(8,128)(2,1)S(1)}, bf16[400,128]{1,0:T(8,128)(2,1)S(1)}, u32[]{:S(2)}, u32[]{:S(2)}) collective-permute-start(bf16[400,128]{1,0:T(8,128)(2,1)S(1)} %fold.1.refs_4_), channel_id=1, source_target_pairs={{0,8},{8,0},{16,24},{24,16},{1,9},{9,1},{17,25},{25,17},{2,10},{10... | collective-permute-start | bytes 307208 | tf_op jit(solution)/shard_map/ppermute | solution.py:478
  17.8 15.7 %copy-start = (bf16[256,64]{0,1:T(8,128)(2,1)S(1)}, bf16[256,64]{0,1:T(8,128)(2,1)}, u32[]{:S(2)}) copy-start(bf16[256,64]{0,1:T(8,128)(2,1)} %param.16) | copy-start | bytes 98308
  17.8 15.7 %copy-start.1 = (bf16[64,256]{1,0:T(8,128)(2,1)S(1)}, bf16[64,256]{1,0:T(8,128)(2,1)}, u32[]{:S(2)}) copy-start(bf16[64,256]{1,0:T(8,128)(2,1)} %down.1) | copy-start | bytes 98308
  17.8 15.7 %copy-start.3 = (f32[64]{0:T(128)S(1)}, f32[64]{0:T(128)}, u32[]{:S(2)}) copy-start(f32[64]{0:T(128)} %param.15) | copy-start | bytes 772
